TPU v7x, 128 devices: a whole 4x4x4 slice. The times are simulated.
128 devices in a mesh: row: 16 (over y, x), col: 2 (over core), depth: 4 (over z).
Axes of the slice: x: 4, y: 4, z: 4, core: 2. Of those that a mesh axis runs over, the one named last changes fastest.
Arguments:
- tokens: bfloat16 [2048, 4096], P('depth', ('col', 'row')), may hold values from -6 to 6
- w_gate: bfloat16 [4096, 14336], P('col', 'row'), may hold values from -0.09375 to 0.09375
- w_up: bfloat16 [4096, 14336], P('col', 'row'), may hold values from -0.09375 to 0.09375
- w_down: bfloat16 [14336, 4096], P('row', 'col'), may hold values from -0.046875 to 0.046875
- d_out: bfloat16 [2048, 4096], P('depth', ('col', 'row')), may hold values from -1.5 to 1.5
Outputs:
- output: bfloat16 [2048, 4096], P('depth', ('col', 'row'))
- d_tokens: bfloat16 [2048, 4096], P('depth', ('col', 'row'))
- grad_gate: bfloat16 [4096, 14336], P(('col', 'depth'), 'row')
- grad_up: bfloat16 [4096, 14336], P(('col', 'depth'), 'row')
- grad_down: bfloat16 [14336, 4096], P(('row', 'depth'), 'col')
All inputs are finite; a program needn't handle non-finite values.
Results may differ from a plain program's by a relative error of at most 0.025.
Values may be sent and summed in bfloat16 or wider, within the bound.
No kernel may reach another device: no remote copies, remote signals or barrier semaphores. Data moves between devices by JAX's collectives and lax.ppermute only.
A program may use at most 128 MiB of HBM per device.

v0:
```python
import jax
import jax.numpy as jnp
from jax import lax
from jax.sharding import PartitionSpec as P


def contract_rows(left, right):
    return lax.dot_general(
        left, right, (((0,), (0,)), ((), ())), preferred_element_type=jnp.float32
    )


def contract_cols(left, right):
    return lax.dot_general(
        left, right, (((1,), (1,)), ((), ())), preferred_element_type=jnp.float32
    )


def local(tokens, w_gate, w_up, w_down, d_out):
    token_rows, cotangent_rows = (
        lax.all_gather(tokens, "row", axis=1, tiled=True),
        lax.all_gather(d_out, "row", axis=1, tiled=True),
    )
    gate_part = jnp.dot(token_rows, w_gate, preferred_element_type=jnp.float32)
    up_part = jnp.dot(token_rows, w_up, preferred_element_type=jnp.float32)
    gate, up = (
        lax.psum_scatter(
            gate_part.astype(jnp.bfloat16), "col", scatter_dimension=1, tiled=True
        ).astype(jnp.float32),
        lax.psum_scatter(
            up_part.astype(jnp.bfloat16), "col", scatter_dimension=1, tiled=True
        ).astype(jnp.float32),
    )
    sigmoid_gate = jax.nn.sigmoid(gate)
    act_share = (gate * sigmoid_gate * up).astype(jnp.bfloat16)
    act_full = lax.all_gather(act_share, "col", axis=1, tiled=True)
    out_part = jnp.dot(act_full, w_down, preferred_element_type=jnp.float32)
    output = lax.psum_scatter(out_part.astype(jnp.bfloat16), "row", scatter_dimension=1, tiled=True)
    d_act_part = contract_cols(cotangent_rows, w_down)
    d_act = lax.psum_scatter(
        d_act_part.astype(jnp.bfloat16), "col", scatter_dimension=1, tiled=True
    ).astype(jnp.float32)
    d_gate_share = (d_act * up * sigmoid_gate * (1.0 + gate * (1.0 - sigmoid_gate))).astype(
        jnp.bfloat16
    )
    d_up_share = (d_act * gate * sigmoid_gate).astype(jnp.bfloat16)
    d_gate_full, d_up_full = (
        lax.all_gather(d_gate_share, "col", axis=1, tiled=True),
        lax.all_gather(d_up_share, "col", axis=1, tiled=True),
    )
    d_tok_part = contract_cols(d_gate_full, w_gate) + contract_cols(d_up_full, w_up)
    d_tokens = lax.psum_scatter(
        d_tok_part.astype(jnp.bfloat16), "row", scatter_dimension=1, tiled=True
    )
    local_gate = contract_rows(token_rows, d_gate_full)
    local_up = contract_rows(token_rows, d_up_full)
    local_down = contract_rows(act_full, cotangent_rows)
    summed_gate, summed_up, summed_down = (
        lax.psum_scatter(
            local_gate.astype(jnp.bfloat16), "depth", scatter_dimension=0, tiled=True
        ).astype(jnp.float32),
        lax.psum_scatter(
            local_up.astype(jnp.bfloat16), "depth", scatter_dimension=0, tiled=True
        ).astype(jnp.float32),
        lax.psum_scatter(
            local_down.astype(jnp.bfloat16), "depth", scatter_dimension=0, tiled=True
        ).astype(jnp.float32),
    )
    return (
        output,
        d_tokens,
        summed_gate.astype(jnp.bfloat16),
        summed_up.astype(jnp.bfloat16),
        summed_down.astype(jnp.bfloat16),
    )


def solution(mesh):
    placed = (
        P("depth", ("col", "row")),
        P("col", "row"),
        P("col", "row"),
        P("row", "col"),
        P("depth", ("col", "row")),
    )
    return jax.shard_map(
        local,
        mesh=mesh,
        in_specs=placed,
        out_specs=(
            P("depth", ("col", "row")),
            P("depth", ("col", "row")),
            P(("col", "depth"), "row"),
            P(("col", "depth"), "row"),
            P(("row", "depth"), "col"),
        ),
        check_vma=False,
    )
```

profile of v0, /device:TPU:0, one launch (start us, length us, event | category | flops | bytes accessed | tf_op | source)
XLA Modules:
  0.0 458.2 jit_solution(14057994677380302006)
XLA Ops:
  7.2 0.0 all-gather.5.cloned.1.call-start
  7.2 0.7 all-gather.5.cloned.1.call-update
  7.9 0.0 all-gather.3.cloned.1.call-start
  7.9 0.7 all-gather.3.cloned.1.call-update
  8.6 0.0 reduce-scatter.17.cloned.1.call-start
  8.7 51.4 %all-gather.5.cloned.1.call-done = bf16[512,2048]{1,0:T(8,128)(2,1)} async-done(((bf16[512,128]{1,0:T(8,128)(2,1)}), bf16[512,2048]{1,0:T(8,128)(2,1)}) %all-gather.5.cloned.1.call-update) | async-done | bytes 2097168 | tf_op jit(solution)/shard_map/all_gather | solution.py:22
  60.1 5.7 %convolution_convert_fusion.2 = bf16[512,896]{0,1:T(8,128)(2,1)} fusion(bf16[512,2048]{1,0:T(8,128)(2,1)} %all-gather.5.cloned.1.call-done, bf16[896,2048]{1,0:T(8,128)(2,1)} %param.8), kind=kOutput, calls=%fused_computation.9 | convolution fusion | flops 1879506944 | bytes 6684672 | tf_op jit(solution)/shard_map/dot_general | solution.py:14
  65.8 0.0 reduce-scatter.17.cloned.1.call-update
  65.8 0.0 reduce-scatter.15.cloned.1.call-start
  65.9 43.3 %all-gather.3.cloned.1.call-done = bf16[512,2048]{1,0:T(8,128)(2,1)} async-done(((bf16[512,128]{1,0:T(8,128)(2,1)}), bf16[512,2048]{1,0:T(8,128)(2,1)}) %all-gather.3.cloned.1.call-update) | async-done | bytes 2097168 | tf_op jit(solution)/shard_map/all_gather | solution.py:21
  109.2 5.8 %convolution_convert_fusion.3 = bf16[512,896]{0,1:T(8,128)(2,1)} fusion(bf16[512,2048]{1,0:T(8,128)(2,1)} %all-gather.3.cloned.1.call-done, bf16[2048,896]{1,0:T(8,128)(2,1)} %param.7), kind=kOutput, calls=%fused_computation.10 | convolution fusion | flops 1879506944 | bytes 6684672 | tf_op jit(solution)/shard_map/dot_general | solution.py:25
  115.1 0.0 reduce-scatter.15.cloned.1.call-update
  115.1 0.0 reduce-scatter.13.cloned.1.call-start
  115.1 5.1 %convolution_convert_fusion.4 = bf16[512,896]{0,1:T(8,128)(2,1)} fusion(bf16[512,2048]{1,0:T(8,128)(2,1)S(1)} %copy-done.5, bf16[2048,896]{1,0:T(8,128)(2,1)} %param.6), kind=kOutput, calls=%fused_computation.11 | convolution fusion | flops 1879506944 | bytes 6684672 | tf_op jit(solution)/shard_map/dot_general | solution.py:24
  120.2 0.0 reduce-scatter.25.cloned.1.call-start
  120.3 2.2 reduce-scatter.17.cloned.1.call-done
  122.5 15.4 %reduce-scatter.15.cloned.1.call-done = bf16[512,448]{0,1:T(8,128)(2,1)} async-done(((bf16[512,896]{0,1:T(8,128)(2,1)}), bf16[512,448]{0,1:T(8,128)(2,1)}) %reduce-scatter.15.cloned.1.call-update) | async-done | bytes 458768 | tf_op jit(solution)/shard_map/reduce_scatter | solution.py:30
  137.9 15.2 %reduce-scatter.13.cloned.1.call-done = bf16[512,448]{0,1:T(8,128)(2,1)} async-done(((bf16[512,896]{0,1:T(8,128)(2,1)}), bf16[512,448]{0,1:T(8,128)(2,1)}) %reduce-scatter.13.cloned.1.call-update) | async-done | bytes 458768 | tf_op jit(solution)/shard_map/reduce_scatter | solution.py:27
  153.2 2.0 fusion.9
  155.2 2.5 all_gather.16
  157.7 0.9 copy-done
  158.6 2.4 convolution_convert_fusion.1
  161.0 2.5 copy.14
  163.6 0.0 reduce-scatter.27.cloned.1.call-start
  163.6 2.5 all_gather.19
  166.1 2.8 all_gather.18
  168.9 4.8 %fusion.10 = f32[512,2048]{1,0:T(8,128)S(1)} fusion(bf16[512,896]{0,1:T(8,128)(2,1)} %all_gather.18, bf16[2048,896]{1,0:T(8,128)(2,1)} %param.6), kind=kOutput, calls=%fused_computation.24 | convolution fusion | flops 1879048192 | bytes 8781824 | tf_op jit(solution)/shard_map/dot_general | solution.py:14
  173.7 2.4 add_convert_fusion
  176.1 2.5 copy.16
  178.7 0.0 reduce-scatter.19.cloned.1.call-start
  178.7 5.8 %convert_bitcast_fusion.1 = bf16[2048,896]{0,1:T(8,128)(2,1)} fusion(bf16[512,896]{0,1:T(8,128)(2,1)} %all_gather.18, bf16[512,2048]{1,0:T(8,128)(2,1)} %all-gather.3.cloned.1.call-done), kind=kOutput, calls=%fused_computation.2 | convolution fusion | flops 1880883200 | bytes 6684672 | tf_op jit(solution)/shard_map/dot_general | solution.py:8
  184.6 0.0 reduce-scatter.21.cloned.1.call-start
  184.6 1.5 copy-done.6
  186.1 3.9 convert_bitcast_fusion
  190.0 0.0 reduce-scatter.21.cloned.1.call-update
  190.1 0.0 reduce-scatter.23.cloned.1.call-start
  190.1 1.1 copy-done.1
  191.2 0.7 copy-done.4
  191.9 4.0 convolution_convert_fusion
  195.9 43.6 %reduce-scatter.25.cloned.1.call-done = bf16[128,512]{1,0:T(8,128)(2,1)} async-done(((bf16[2048,512]{1,0:T(8,128)(2,1)}), bf16[128,512]{1,0:T(8,128)(2,1)}) %reduce-scatter.25.cloned.1.call-update) | async-done | bytes 131088
  239.6 1.7 copy.15
  241.2 75.3 %reduce-scatter.27.cloned.1.call-done = bf16[128,512]{1,0:T(8,128)(2,1)} async-done(((bf16[2048,512]{1,0:T(8,128)(2,1)}), bf16[128,512]{1,0:T(8,128)(2,1)}) %reduce-scatter.27.cloned.1.call-update) | async-done | bytes 131088
  316.5 1.7 copy.17
  318.2 43.0 %reduce-scatter.19.cloned.1.call-done = bf16[512,896]{0,1:T(8,128)(2,1)} async-done(((bf16[2048,896]{0,1:T(8,128)(2,1)}), bf16[512,896]{0,1:T(8,128)(2,1)}) %reduce-scatter.19.cloned.1.call-update) | async-done | bytes 917520 | tf_op jit(solution)/shard_map/reduce_scatter | solution.py:59
  361.2 2.2 copy.12
  363.4 42.7 %reduce-scatter.21.cloned.1.call-done = bf16[512,896]{0,1:T(8,128)(2,1)} async-done(((bf16[2048,896]{0,1:T(8,128)(2,1)}), bf16[512,896]{0,1:T(8,128)(2,1)}) %reduce-scatter.21.cloned.1.call-update) | async-done | bytes 917520 | tf_op jit(solution)/shard_map/reduce_scatter | solution.py:62
  406.1 2.2 copy.13
  408.3 43.1 %reduce-scatter.23.cloned.1.call-done = bf16[224,2048]{1,0:T(8,128)(2,1)} async-done(((bf16[896,2048]{1,0:T(8,128)(2,1)}), bf16[224,2048]{1,0:T(8,128)(2,1)}) %reduce-scatter.23.cloned.1.call-update) | async-done | bytes 917520 | tf_op jit(solution)/shard_map/reduce_scatter | solution.py:65
  (15 shorter events, 0.1 us)
Async XLA Ops:
  7.2 53.0 %all-gather.5.cloned.1.call-start = ((), (), s32[]{:S(2)}) async-start(), calls=%async_computation.11 | async-start | bytes 2228224 | tf_op jit(solution)/shard_map/all_gather | solution.py:22
  7.9 101.3 %all-gather.3.cloned.1.call-start = ((), (), s32[]{:S(2)}) async-start(), calls=%async_computation.8 | async-start | bytes 2228224 | tf_op jit(solution)/shard_map/all_gather | solution.py:21
  8.6 113.9 %reduce-scatter.17.cloned.1.call-start = ((), (), s32[]{:S(2)}) async-start(), calls=%async_computation.12 | async-start | bytes 1376256 | tf_op jit(solution)/shard_map/reduce_scatter | solution.py:40
  65.8 72.1 %reduce-scatter.15.cloned.1.call-start = ((), (), s32[]{:S(2)}) async-start(), calls=%async_computation.10 | async-start | bytes 1376256 | tf_op jit(solution)/shard_map/reduce_scatter | solution.py:30
  109.2 5.9 %copy-start.5 = (bf16[512,2048]{1,0:T(8,128)(2,1)S(1)}, bf16[512,2048]{1,0:T(8,128)(2,1)}, u32[]{:S(2)}) copy-start(bf16[512,2048]{1,0:T(8,128)(2,1)} %all-gather.3.cloned.1.call-done) | copy-start | bytes 6291460
  115.1 38.1 %reduce-scatter.13.cloned.1.call-start = ((), (), s32[]{:S(2)}) async-start(), calls=%async_computation.9 | async-start | bytes 1376256 | tf_op jit(solution)/shard_map/reduce_scatter | solution.py:27
  120.2 119.3 %reduce-scatter.25.cloned.1.call-start = ((), (), s32[]{:S(2)}) async-start(), calls=%async_computation.16 | async-start | bytes 2228224
  153.2 5.5 %copy-start.2 = (bf16[896,2048]{1,0:T(8,128)(2,1)S(1)}, bf16[896,2048]{1,0:T(8,128)(2,1)}, u32[]{:S(2)}) copy-start(bf16[896,2048]{1,0:T(8,128)(2,1)} %param.8) | copy-start | bytes 11010052
  157.7 0.9 copy-start
  163.6 152.9 %reduce-scatter.27.cloned.1.call-start = ((), (), s32[]{:S(2)}) async-start(), calls=%async_computation.17 | async-start | bytes 2228224
  168.9 4.9 %copy-start.3 = (bf16[2048,896]{1,0:T(8,128)(2,1)S(1)}, bf16[2048,896]{1,0:T(8,128)(2,1)}, u32[]{:S(2)}) copy-start(bf16[2048,896]{1,0:T(8,128)(2,1)} %param.7) | copy-start | bytes 11010052
  178.7 182.5 %reduce-scatter.19.cloned.1.call-start = ((), (), s32[]{:S(2)}) async-start(), calls=%async_computation.13 | async-start | bytes 4587520 | tf_op jit(solution)/shard_map/reduce_scatter | solution.py:59
  184.5 1.6 copy-start.6
  184.6 221.5 %reduce-scatter.21.cloned.1.call-start = ((), (), s32[]{:S(2)}) async-start(), calls=%async_computation.14 | async-start | bytes 4587520 | tf_op jit(solution)/shard_map/reduce_scatter | solution.py:62
  190.0 1.2 copy-start.1
  190.0 1.9 copy-start.4
  190.1 261.3 %reduce-scatter.23.cloned.1.call-start = ((), (), s32[]{:S(2)}) async-start(), calls=%async_computation.15 | async-start | bytes 4587520 | tf_op jit(solution)/shard_map/reduce_scatter | solution.py:65
Sparse Core Ops, SparseCore 0:
  10.1 49.9 all-gather.4
  62.2 46.9 all-gather.2
  112.1 10.3 reduce-scatter.16
  125.4 12.4 reduce-scatter.14
  140.7 12.4 reduce-scatter.12
  163.7 75.8 reduce-scatter.24
  242.8 73.6 reduce-scatter.26
  319.1 42.0 reduce-scatter.18
  363.7 42.3 reduce-scatter.20
  409.0 42.3 reduce-scatter.22
where the time goes:
time: 459 us; the launch traced here: 458 us
  waiting for transfers between devices  377 us (82%)
  matrix products  40 us (9%)
  local copies, waits for them, and re-layouts  17.1 us (4%)
  between operations  14.2 us (3%)
  blocking collectives  7.74 us (2%)
    unnamed x12, waiting for transfers between devices  120 us
    all_gather x1, waiting for transfers between devices, local(): lax.all_gather(d_out, 'row', axis=1, tiled=True)  51.4 us
    all_gather x1, waiting for transfers between devices, local(): lax.all_gather(tokens, 'row', axis=1, tiled=True)  43.3 us
    reduce_scatter x1, waiting for transfers between devices, local(): lax.psum_scatter(local_down.astype(jnp.bfloat16), 'depth', scatter_dimens...  43.1 us
    reduce_scatter x1, waiting for transfers between devices, local(): lax.psum_scatter(local_gate.astype(jnp.bfloat16), 'depth', scatter_dimens...  43 us
    reduce_scatter x1, waiting for transfers between devices, local(): lax.psum_scatter(local_up.astype(jnp.bfloat16), 'depth', scatter_dimensio...  42.7 us
    unnamed x20, local copies, waits for them, and re-layouts  17.1 us
    reduce_scatter x1, waiting for transfers between devices, local(): lax.psum_scatter(up_part.astype(jnp.bfloat16), 'col', scatter_dimension=1...  15.4 us
  transfers between devices with their start and end apart: 10, of which 10 were waited for; matrix products, arithmetic and copies ran while one was open for 10% of the time, Pallas kernels for 0%

commit v1 on v0

v1 whole, which is shorter than its diff:
```python
import functools

import jax
import jax.numpy as jnp
from jax import lax
from jax.experimental import pallas as pl
from jax.experimental.pallas import tpu as pltpu
from jax.sharding import PartitionSpec as P

BF = jnp.bfloat16
F32 = jnp.float32
G = 4
MIB = 1024 * 1024


def here():
    row = lax.axis_index("row")
    return row // G, row % G, lax.axis_index("col"), lax.axis_index("depth")


def ring(pos, core):
    step = 1 - 2 * core
    return [pos, (pos - step + G) % G, (pos + step + G) % G, (pos + 2) % G]


def targets(pos, core):
    own, back, ahead, far = ring(pos, core)
    return [own, ahead, back, far]


def row_shift(kind, array, axis):
    pairs = []
    for y in range(G):
        for x in range(G):
            for core in range(2):
                step = {1: 1 - 2 * core, 2: 2 * core - 1, 3: 2}[kind]
                to_y = (y + step) % G if axis == "y" else y
                to_x = (x + step) % G if axis == "x" else x
                pairs.append(((y * G + x) * 2 + core, (to_y * G + to_x) * 2 + core))
    return lax.ppermute(array, ("row", "col"), pairs)


def depth_shift(kind, array):
    pairs = []
    for core in range(2):
        for z in range(G):
            step = {1: 1 - 2 * core, 2: 2 * core - 1}[kind]
            pairs.append((core * G + z, core * G + (z + step) % G))
    return lax.ppermute(array, ("col", "depth"), pairs)


def swap(array):
    return lax.ppermute(array, "col", [(0, 1), (1, 0)])


def transpose_groups(array):
    pairs = []
    for y in range(G):
        for x in range(G):
            for z in range(G):
                pairs.append(((y * G + x) * G + z, (z * G + x) * G + y))
    return lax.ppermute(array, ("row", "depth"), pairs)


def after(array, *others):
    return lax.optimization_barrier((array,) + others)[0]


def call(body, outs, n_in, scratch, flops, nbytes, out_space=pl.ANY, in_space=pl.ANY):
    return pl.pallas_call(
        body,
        out_shape=outs,
        in_specs=[pl.BlockSpec(memory_space=in_space)] * n_in,
        out_specs=jax.tree.map(lambda _: pl.BlockSpec(memory_space=out_space), outs),
        scratch_shapes=scratch,
        compiler_params=pltpu.CompilerParams(vmem_limit_bytes=48 * MIB),
        cost_estimate=pl.CostEstimate(flops=flops, bytes_accessed=nbytes, transcendentals=0),
    )


def shape(dims, dtype=BF):
    return jax.ShapeDtypeStruct(dims, dtype)


def start_all(copies):
    for item in copies:
        item.start()


def wait_all(copies):
    for item in copies:
        item.wait()


def place_body(axis, *refs):
    ins, out, sems = refs[:G], refs[G], refs[G + 1]
    y, x, core, _ = here()
    spots = ring(y if axis == "y" else x, core)
    copies = [pltpu.make_async_copy(ins[k], out.at[spots[k]], sems.at[k]) for k in range(G)]
    start_all(copies)
    wait_all(copies)


def place(axis, parts):
    tok, feat = parts[0].shape
    return call(
        functools.partial(place_body, axis),
        shape((G, tok, feat)),
        G,
        [pltpu.SemaphoreType.DMA((G,))],
        0,
        G * tok * feat * 4,
    )(*parts)


def wide(ref, chunk):
    return jnp.concatenate([ref[chunk, j] for j in range(G)], axis=1)


def split_rows(core, acc, keep, send, half):
    keep[...] = acc[pl.ds(pl.multiple_of(core * half, half), half), :]
    send[...] = acc[pl.ds(pl.multiple_of((1 - core) * half, half), half), :].astype(BF)


def gate_up_body(t0, t1, t2, t3, wg, wu, keep, send, tok, wgs, wus, acc_g, acc_u, sems):
    y, _, core, _ = here()
    spots = ring(y, core)
    loads = [
        pltpu.make_async_copy(ref, tok.at[spots[k]], sems.at[k])
        for k, ref in enumerate((t0, t1, t2, t3))
    ]
    depth = wg.shape[0] // G
    weights = []
    for k in range(G):
        rows = pl.ds(k * depth, depth)
        weights.append(
            [
                pltpu.make_async_copy(wg.at[rows], wgs.at[rows], sems.at[G + 2 * k]),
                pltpu.make_async_copy(wu.at[rows], wus.at[rows], sems.at[G + 2 * k + 1]),
            ]
        )
    start_all(loads)
    for pair in weights:
        start_all(pair)
    wait_all(loads)
    for k in range(G):
        wait_all(weights[k])
        left = wide(tok, k)
        rows = slice(k * depth, (k + 1) * depth)
        for acc, ws in ((acc_g, wgs), (acc_u, wus)):
            term = jnp.dot(left, ws[rows, :], preferred_element_type=F32)
            if k == 0:
                acc[...] = term
            else:
                acc[...] += term
    half = acc_g.shape[0] // 2
    split_rows(core, acc_g, keep.at[0], send.at[0], half)
    split_rows(core, acc_u, keep.at[1], send.at[1], half)


def gate_up(chunks, wg, wu):
    tok = chunks[0].shape[1]
    feats, hid = wg.shape
    return call(
        gate_up_body,
        (shape((2, tok // 2, hid), F32), shape((2, tok // 2, hid))),
        6,
        [
            pltpu.VMEM((G,) + chunks[0].shape, BF),
            pltpu.VMEM((feats, hid), BF),
            pltpu.VMEM((feats, hid), BF),
            pltpu.VMEM((tok, hid), F32),
            pltpu.VMEM((tok, hid), F32),
            pltpu.SemaphoreType.DMA((3 * G,)),
        ],
        4 * tok * feats * hid,
        4 * feats * hid,
        out_space=pltpu.VMEM,
    )(*chunks, wg, wu)


def d_act_body(c0, c1, c2, c3, wd, keep, send, rows_out, cot, wds, acc, flat, sems):
    _, x, core, _ = here()
    spots = ring(x, core)
    loads = [
        pltpu.make_async_copy(ref, cot.at[:, spots[k]], sems.at[k])
        for k, ref in enumerate((c0, c1, c2, c3))
    ]
    depth = wd.shape[1] // G
    weights = [
        pltpu.make_async_copy(
            wd.at[:, pl.ds(k * depth, depth)], wds.at[:, pl.ds(k * depth, depth)], sems.at[G + k]
        )
        for k in range(G)
    ]
    start_all(loads)
    start_all(weights)
    wait_all(loads)
    for k in range(G):
        weights[k].wait()
        left = wide(cot, k)
        cols = slice(k * depth, (k + 1) * depth)
        flat[:, cols] = left
        term = lax.dot_general(
            left, wds[:, cols], (((1,), (1,)), ((), ())), preferred_element_type=F32
        )
        if k == 0:
            acc[...] = term
        else:
            acc[...] += term
    out = pltpu.make_async_copy(flat, rows_out, sems.at[2 * G])
    out.start()
    split_rows(core, acc, keep, send, acc.shape[0] // 2)
    out.wait()


def d_act(chunks, wd):
    tok = chunks[0].shape[1]
    hid, feats = wd.shape
    outs = (shape((tok // 2, hid), F32), shape((tok // 2, hid)), shape((tok, feats)))
    vm, anyw = pl.BlockSpec(memory_space=pltpu.VMEM), pl.BlockSpec(memory_space=pl.ANY)
    return pl.pallas_call(
        d_act_body,
        out_shape=outs,
        in_specs=[anyw] * 5,
        out_specs=(vm, vm, anyw),
        scratch_shapes=[
            pltpu.VMEM((G, G) + chunks[0].shape[1:], BF),
            pltpu.VMEM((hid, feats), BF),
            pltpu.VMEM((tok, hid), F32),
            pltpu.VMEM((tok, feats), BF),
            pltpu.SemaphoreType.DMA((2 * G + 1,)),
        ],
        compiler_params=pltpu.CompilerParams(vmem_limit_bytes=48 * MIB),
        cost_estimate=pl.CostEstimate(
            flops=2 * tok * feats * hid, bytes_accessed=2 * feats * hid, transcendentals=0
        ),
    )(*chunks, wd)


def hidden_body(keep, recv, keep_d, recv_d, act, grads):
    gate = keep[0] + recv[0].astype(F32)
    up = keep[1] + recv[1].astype(F32)
    da = keep_d[...] + recv_d[...].astype(F32)
    sig = 1.0 / (1.0 + jnp.exp(-gate))
    silu = gate * sig
    act[...] = (silu * up).astype(BF)
    grads[0] = (da * up * sig * (1.0 + gate * (1.0 - sig))).astype(BF)
    grads[1] = (da * silu).astype(BF)


def hidden(keep, recv, keep_d, recv_d):
    _, half, hid = keep.shape
    tile = half // 4
    three = pl.BlockSpec((2, tile, hid), lambda i: (0, i, 0))
    two = pl.BlockSpec((tile, hid), lambda i: (i, 0))
    return pl.pallas_call(
        hidden_body,
        grid=(4,),
        out_shape=(shape((half, hid)), shape((2, half, hid))),
        in_specs=[three, three, two, two],
        out_specs=(two, three),
        cost_estimate=pl.CostEstimate(
            flops=20 * half * hid, bytes_accessed=24 * half * hid, transcendentals=half * hid
        ),
    )(keep, recv, keep_d, recv_d)


def out_body(own, other, wd, o0, o1, o2, o3, act, wds, res, sems):
    y, _, core, _ = here()
    half = own.shape[0]
    loads = [
        pltpu.make_async_copy(own, act.at[pl.ds(core * half, half)], sems.at[0]),
        pltpu.make_async_copy(other, act.at[pl.ds((1 - core) * half, half)], sems.at[1]),
    ]
    width = wd.shape[1] // G
    weights = [
        pltpu.make_async_copy(
            wd.at[:, pl.ds(k * width, width)], wds.at[:, pl.ds(k * width, width)], sems.at[2 + k]
        )
        for k in range(G)
    ]
    start_all(loads)
    start_all(weights)
    wait_all(loads)
    part = width // G
    for k in range(G):
        weights[k].wait()
        term = jnp.dot(
            act[...], wds[:, k * width : (k + 1) * width], preferred_element_type=F32
        ).astype(BF)
        for j in range(G):
            res[k, j] = term[:, j * part : (j + 1) * part]
    spots = targets(y, core)
    stores = [
        pltpu.make_async_copy(res.at[spots[k]], ref, sems.at[2 + G + k])
        for k, ref in enumerate((o0, o1, o2, o3))
    ]
    start_all(stores)
    wait_all(stores)


def out_parts(own, other, wd):
    half, hid = own.shape
    feats = wd.shape[1]
    tok = 2 * half
    part = feats // (G * G)
    return call(
        out_body,
        (shape((G, tok, part)),) * G,
        3,
        [
            pltpu.VMEM((tok, hid), BF),
            pltpu.VMEM((hid, feats), BF),
            pltpu.VMEM((G, G, tok, part), BF),
            pltpu.SemaphoreType.DMA((2 + 2 * G,)),
        ],
        2 * tok * feats * hid,
        2 * feats * hid,
    )(own, other, wd)


def d_tok_body(own, other, wg, wu, o0, o1, o2, o3, grads, wgs, wus, res, sems):
    _, x, core, _ = here()
    half = own.shape[1]
    loads = [
        pltpu.make_async_copy(own, grads.at[:, pl.ds(core * half, half)], sems.at[0]),
        pltpu.make_async_copy(other, grads.at[:, pl.ds((1 - core) * half, half)], sems.at[1]),
    ]
    width = wg.shape[0] // G
    weights = []
    for k in range(G):
        rows = pl.ds(k * width, width)
        weights.append(
            [
                pltpu.make_async_copy(wg.at[rows], wgs.at[rows], sems.at[2 + 2 * k]),
                pltpu.make_async_copy(wu.at[rows], wus.at[rows], sems.at[3 + 2 * k]),
            ]
        )
    start_all(loads)
    for pair in weights:
        start_all(pair)
    wait_all(loads)
    part = width // G
    dims = (((1,), (1,)), ((), ()))
    for k in range(G):
        wait_all(weights[k])
        rows = slice(k * width, (k + 1) * width)
        term = lax.dot_general(grads[0], wgs[rows, :], dims, preferred_element_type=F32)
        term += lax.dot_general(grads[1], wus[rows, :], dims, preferred_element_type=F32)
        term = term.astype(BF)
        for j in range(G):
            res[j, k] = term[:, j * part : (j + 1) * part]
    spots = targets(x, core)
    stores = [
        pltpu.make_async_copy(res.at[spots[k]], ref, sems.at[2 + 2 * G + k])
        for k, ref in enumerate((o0, o1, o2, o3))
    ]
    start_all(stores)
    wait_all(stores)


def d_tok_parts(own, other, wg, wu):
    _, half, hid = own.shape
    feats = wg.shape[0]
    tok = 2 * half
    part = feats // (G * G)
    return call(
        d_tok_body,
        (shape((G, tok, part)),) * G,
        4,
        [
            pltpu.VMEM((2, tok, hid), BF),
            pltpu.VMEM((feats, hid), BF),
            pltpu.VMEM((feats, hid), BF),
            pltpu.VMEM((G, G, tok, part), BF),
            pltpu.SemaphoreType.DMA((2 + 3 * G,)),
        ],
        4 * tok * feats * hid,
        4 * feats * hid,
    )(own, other, wg, wu)


def down_body(own, other, cot, b0, b1, b2, b3, act, cots, res, sems):
    _, _, core, z = here()
    half = own.shape[0]
    loads = [
        pltpu.make_async_copy(own, act.at[pl.ds(core * half, half)], sems.at[0]),
        pltpu.make_async_copy(other, act.at[pl.ds((1 - core) * half, half)], sems.at[1]),
    ]
    width = cot.shape[1] // G
    rights = [
        pltpu.make_async_copy(
            cot.at[:, pl.ds(k * width, width)], cots.at[:, pl.ds(k * width, width)], sems.at[2 + k]
        )
        for k in range(G)
    ]
    start_all(loads)
    start_all(rights)
    wait_all(loads)
    left = act[...].T
    block = res.shape[1]
    for k in range(G):
        rights[k].wait()
        cols = slice(k * width, (k + 1) * width)
        term = jnp.dot(left, cots[:, cols], preferred_element_type=F32).astype(BF)
        for j in range(G):
            res[j, :, cols] = term[j * block : (j + 1) * block, :]
    spots = targets(z, core)
    stores = [
        pltpu.make_async_copy(res.at[spots[k]], ref, sems.at[2 + G + k])
        for k, ref in enumerate((b0, b1, b2, b3))
    ]
    start_all(stores)
    wait_all(stores)


def down_parts(own, other, cot):
    half, hid = own.shape
    tok, feats = cot.shape
    return call(
        down_body,
        (shape((hid // G, feats)),) * G,
        3,
        [
            pltpu.VMEM((tok, hid), BF),
            pltpu.VMEM((tok, feats), BF),
            pltpu.VMEM((G, hid // G, feats), BF),
            pltpu.SemaphoreType.DMA((2 + 2 * G,)),
        ],
        2 * tok * feats * hid,
        2 * tok * feats,
    )(own, other, cot)


def grads_body(tok, p0, p1, p2, p3, p4, p5, p6, p7, gg, gu, toks, lefts, rights, sems):
    _, _, core, z = here()
    own, back, ahead, far = ring(z, core)
    half = p0.shape[1]
    feats = gg.shape[0]
    spots = [
        (own, core), (own, 1 - core),
        (back, core), (ahead, 1 - core),
        (back, 1 - core), (ahead, core),
        (far, core), (far, 1 - core),
    ]
    pieces = (p0, p1, p2, p3, p4, p5, p6, p7)
    load = pltpu.make_async_copy(tok, toks, sems.at[8])
    load.start()
    moves = []
    for k, (group, side) in enumerate(spots):
        moves.append(
            pltpu.make_async_copy(
                pieces[k],
                rights.at[:, pl.ds(pl.multiple_of(group * 2 * half + side * half, half), half)],
                sems.at[k],
            )
        )
    start_all(moves)
    load.wait()
    for group in range(G):
        lefts[:, group * 2 * half : (group + 1) * 2 * half] = toks[
            :, group * feats : (group + 1) * feats
        ].T
    wait_all(moves)
    rows = feats // 2
    for n, out in enumerate((gg, gu)):
        for r in range(2):
            cut = slice(r * rows, (r + 1) * rows)
            out[cut, :] = jnp.dot(
                lefts[cut, :], rights[n], preferred_element_type=F32
            ).astype(BF)


def weight_grads(tok, pieces):
    _, half, hid = pieces[0].shape
    feats = tok.shape[1] // G
    return call(
        grads_body,
        (shape((feats, hid)),) * 2,
        9,
        [
            pltpu.VMEM(tok.shape, BF),
            pltpu.VMEM((feats, 2 * G * half), BF),
            pltpu.VMEM((2, 2 * G * half, hid), BF),
            pltpu.SemaphoreType.DMA((9,)),
        ],
        8 * G * half * feats * hid,
        20 * half * hid,
        out_space=pltpu.VMEM,
    )(tok, *pieces)


def mid_sum_body(axis, a0, a1, a2, a3, o0, o1, o2, o3):
    y, x, core, _ = here()
    spots = targets(y if axis == "y" else x, core)
    for k, out in enumerate((o0, o1, o2, o3)):
        at = spots[k]
        total = a0[at].astype(F32) + a1[at].astype(F32) + (a2[at].astype(F32) + a3[at].astype(F32))
        out[...] = total.astype(BF)


def mid_sum(axis, parts):
    _, tok, part = parts[0].shape
    return call(
        functools.partial(mid_sum_body, axis),
        (shape((tok, part)),) * G,
        G,
        [],
        12 * tok * part,
        40 * tok * part,
        out_space=pltpu.VMEM,
        in_space=pltpu.VMEM,
    )(*parts)


def total_of(parts):
    total = parts[0].astype(F32)
    for item in parts[1:]:
        total = total + item.astype(F32)
    return total.astype(BF)


def gather_axis(first, array):
    return [array] + [row_shift(k, array, first) for k in (1, 2, 3)]


def local(tokens, w_gate, w_up, w_down, d_out):
    chunk_t = place("x", gather_axis("x", tokens))
    chunk_c = place("y", gather_axis("y", d_out))
    tok_chunks = gather_axis("y", chunk_t)
    cot_chunks = gather_axis("x", chunk_c)

    keep_gu, send_gu = gate_up(tok_chunks, w_gate, w_up)
    recv_gu = swap(send_gu)
    keep_d, send_d, cot_rows = d_act(cot_chunks, w_down)
    recv_d = swap(send_d)

    turned = after(transpose_groups(tokens), cot_chunks[1])
    turned_rows = lax.all_gather(turned, "row", axis=1, tiled=True)

    act_own, grads_own = hidden(keep_gu, recv_gu, keep_d, recv_d)
    act_other, grads_other = swap(act_own), swap(grads_own)

    near_own = depth_shift(1, grads_own)
    near_other = depth_shift(1, grads_other)
    far_own = depth_shift(1, near_own)

    outs = out_parts(act_own, act_other, w_down)
    out_got = [outs[0]] + [row_shift(k, outs[k], "y") for k in (1, 2, 3)]
    toks = d_tok_parts(grads_own, grads_other, w_gate, w_up)
    tok_got = [toks[0]] + [row_shift(k, toks[k], "x") for k in (1, 2, 3)]

    blocks = down_parts(act_own, act_other, cot_rows)
    relay = depth_shift(1, after(blocks[3], near_own, near_other))
    back = depth_shift(2, after(blocks[2], relay))
    ahead = depth_shift(1, total_of([blocks[1], relay]))

    out_mid = mid_sum("x", out_got)
    tok_mid = mid_sum("y", tok_got)
    output = total_of([out_mid[0]] + [row_shift(k, out_mid[k], "x") for k in (1, 2, 3)])
    d_tokens = total_of([tok_mid[0]] + [row_shift(k, tok_mid[k], "y") for k in (1, 2, 3)])

    pieces = [
        grads_own, grads_other,
        near_own, swap(near_own),
        near_other, swap(near_other),
        far_own, swap(far_own),
    ]
    grad_gate, grad_up = weight_grads(turned_rows, pieces)
    grad_down = total_of([blocks[0], ahead, back])
    return output, d_tokens, grad_gate, grad_up, grad_down


def solution(mesh):
    placed = (
        P("depth", ("col", "row")),
        P("col", "row"),
        P("col", "row"),
        P("row", "col"),
        P("depth", ("col", "row")),
    )
    return jax.shard_map(
        local,
        mesh=mesh,
        in_specs=placed,
        out_specs=(
            P("depth", ("col", "row")),
            P("depth", ("col", "row")),
            P(("col", "depth"), "row"),
            P(("col", "depth"), "row"),
            P(("row", "depth"), "col"),
        ),
        check_vma=False,
    )
```

time: 459 us -> 223 us (0.49)
  waiting for transfers between devices: 377 us -> 81.8 us
  starting transfers between devices: 0.41 us -> 61.3 us
  Pallas kernels: 0 us -> 43 us
  matrix products: 40 us -> 0 us
  blocking collectives: 7.74 us -> 0 us
    reduce_scatter x6 -> x0, waiting for transfers between devices: 162 us -> none  [the longest x1 43.1 us: local(): lax.psum_scatter(local_down.astype(jnp.bfloat16), 'depth', scatter_dimens...]
    unnamed x12 -> x1, waiting for transfers between devices: 120 us -> 0.02 us
    all_gather x2 -> x1, waiting for transfers between devices: 94.8 us -> 0.01 us  [local(): turned_rows = lax.all_gather(turned, 'row', axis=1, tiled=True)]
    ppermute x0 -> x38, waiting for transfers between devices: none -> 81.8 us  [the longest x24 71 us: row_shift(): return lax.ppermute(array, ('row', 'col'), pairs)]
    ppermute x0 -> x38, starting transfers between devices: none -> 61.2 us  [the longest x24 43.3 us: row_shift(): return lax.ppermute(array, ('row', 'col'), pairs)]
    pallas_call x0 -> x11, Pallas kernels: none -> 43 us  [the longest x1 7.96 us: weight_grads(): call(grads_body, (shape((feats, hid)),) * 2, 9, [pltpu.VMEM(tok.shape, BF...]
    dot_general x9 -> x0, matrix products: 40 us -> none  [the longest x3 13.7 us: contract_rows(): lax.dot_general(left, right, (((0,), (0,)), ((), ())), preferred_element_...]
    all_gather x3 -> x0, blocking collectives: 7.74 us -> none  [the longest x1 2.76 us: local(): lax.all_gather(d_gate_share, 'col', axis=1, tiled=True)]
  transfers between devices with their start and end apart: 10 -> 39, of which waited for: 10 -> 19; matrix products, arithmetic and copies ran while one was open for 10% -> 1% of each run, Pallas kernels for 0% -> 19%
where the time goes in v1:
time: 223 us; the launch traced here: 221 us
  waiting for transfers between devices  81.8 us (37%)
  starting transfers between devices  61.3 us (27%)
  Pallas kernels  43 us (19%)
  local copies, waits for them, and re-layouts  14.6 us (7%)
  between operations  14.2 us (6%)
  other arithmetic  5.69 us (3%)
    ppermute x24, waiting for transfers between devices, row_shift(): return lax.ppermute(array, ('row', 'col'), pairs)  71 us
    ppermute x24, starting transfers between devices, row_shift(): return lax.ppermute(array, ('row', 'col'), pairs)  43.3 us
    unnamed x38, local copies, waits for them, and re-layouts  14.6 us
    ppermute x6, starting transfers between devices, depth_shift(): return lax.ppermute(array, ('col', 'depth'), pairs)  14.3 us
    pallas_call x1, Pallas kernels, weight_grads(): call(grads_body, (shape((feats, hid)),) * 2, 9, [pltpu.VMEM(tok.shape, BF...  7.96 us
    ppermute x6, waiting for transfers between devices, depth_shift(): return lax.ppermute(array, ('col', 'depth'), pairs)  7.93 us
    pallas_call x1, Pallas kernels, d_tok_parts(): call(d_tok_body, (shape((G, tok, part)),) * G, 4, [pltpu.VMEM((2, tok, hi...  7.16 us
    pallas_call x1, Pallas kernels, gate_up(): call(gate_up_body, (shape((2, tok // 2, hid), F32), shape((2, tok // 2, h...  6.98 us
  transfers between devices with their start and end apart: 39, of which 19 were waited for; matrix products, arithmetic and copies ran while one was open for 1% of the time, Pallas kernels for 19%

profile of v1, /device:TPU:0, one launch (start us, length us, event | category | flops | bytes accessed | tf_op | source)
XLA Modules:
  0.0 220.5 jit_solution(7993107773690707891)
XLA Ops:
  7.2 1.6 collective-permute-start
  8.9 1.7 collective-permute-start.1
  10.5 1.9 collective-permute-start.2
  12.4 1.3 collective-permute-done.refs_1_
  14.0 4.3 %collective-permute-done.2.refs_3_ = bf16[512,128]{1,0:T(8,128)(2,1)S(1)} collective-permute-done((bf16[512,128]{1,0:T(8,128)(2,1)}, bf16[512,128]{1,0:T(8,128)(2,1)S(1)}, u32[]{:S(2)}, u32[]{:S(2)}) %collective-permute-start.2) | collective-permute-done | bytes 131104 | tf_op jit(solution)/shard_map/ppermute | solution.py:40
  20.0 1.6 collective-permute-start.3
  21.6 1.7 collective-permute-start.4
  23.3 2.0 collective-permute-start.5
  25.9 2.6 %collective-permute-start.8 = (bf16[512,128]{1,0:T(8,128)(2,1)}, bf16[512,128]{1,0:T(8,128)(2,1)S(1)}, u32[]{:S(2)}, u32[]{:S(2)}) collective-permute-start(bf16[512,128]{1,0:T(8,128)(2,1)} %refs_0_.3), channel_id=1, source_target_pairs={{0,96},{4,36},{8,104},{12,44},{16,112},{20,52},{24,120},{28,60},{3... | collective-permute-start | bytes 393224 | tf_op jit(solution)/shard_map/ppermute | solution.py:40
  28.5 20.2 %collective-permute-done.7.refs_1_ = bf16[512,128]{1,0:T(8,128)(2,1)S(1)} collective-permute-done((bf16[512,128]{1,0:T(8,128)(2,1)}, bf16[512,128]{1,0:T(8,128)(2,1)S(1)}, u32[]{:S(2)}, u32[]{:S(2)}) %collective-permute-start.7) | collective-permute-done | bytes 131104 | tf_op jit(solution)/shard_map/ppermute | solution.py:40
  48.7 2.1 collective-permute-start.9
  50.8 4.6 %collective-permute-done.9.refs_3_ = bf16[512,128]{1,0:T(8,128)(2,1)S(1)} collective-permute-done((bf16[512,128]{1,0:T(8,128)(2,1)}, bf16[512,128]{1,0:T(8,128)(2,1)S(1)}, u32[]{:S(2)}, u32[]{:S(2)}) %collective-permute-start.9) | collective-permute-done | bytes 131104 | tf_op jit(solution)/shard_map/ppermute | solution.py:40
  57.0 3.3 %collective-permute-start.10 = (bf16[4,512,128]{2,1,0:T(8,128)(2,1)S(1)}, bf16[4,512,128]{2,1,0:T(8,128)(2,1)S(1)}, u32[]{:S(2)}, u32[]{:S(2)}) collective-permute-start(bf16[4,512,128]{2,1,0:T(8,128)(2,1)S(1)} %shard_map.94.c0), channel_id=1, source_target_pairs={{0,8},{4,28},{8,16},{12,4},{16,24},{20,12},{24,0},{28,20},{32,40},... | collective-permute-start | bytes 1572872 | tf_op jit(solution)/shard_map/ppermute | solution.py:40
  60.3 2.1 collective-permute-start.12
  62.4 7.0 %shard_map.93 = (f32[2,256,896]{2,1,0:T(8,128)S(1)}, bf16[2,256,896]{2,1,0:T(8,128)(2,1)S(1)}) custom-call(bf16[4,512,128]{2,1,0:T(8,128)(2,1)S(1)} %shard_map.92.t0, bf16[4,512,128]{2,1,0:T(8,128)(2,1)S(1)} %collective-permute-done.3.t1, bf16[4,512,128]{2,1,0:T(8,128)(2,1)S(1)} %collective-permute-done.4.t2, ...), custom_call_target="tpu_custom_call" | custom-call | flops 3758096384 | bytes 7340032 | tf_op jit(solution)/shard_map/pallas_call | solution.py:164
  69.4 1.2 copy-done
  70.6 10.5 %collective-permute-done.10.c1 = bf16[4,512,128]{2,1,0:T(8,128)(2,1)S(1)} collective-permute-done((bf16[4,512,128]{2,1,0:T(8,128)(2,1)S(1)}, bf16[4,512,128]{2,1,0:T(8,128)(2,1)S(1)}, u32[]{:S(2)}, u32[]{:S(2)}) %collective-permute-start.10) | collective-permute-done | bytes 524320 | tf_op jit(solution)/shard_map/ppermute | solution.py:40
  81.2 4.3 %shard_map.95 = (f32[256,896]{1,0:T(8,128)S(1)}, bf16[256,896]{1,0:T(8,128)(2,1)S(1)}, bf16[512,2048]{1,0:T(8,128)(2,1)S(1)}) custom-call(bf16[4,512,128]{2,1,0:T(8,128)(2,1)S(1)} %shard_map.94.c0, bf16[4,512,128]{2,1,0:T(8,128)(2,1)S(1)} %collective-permute-done.10.c1, bf16[4,512,128]{2,1,0:T(8,128)(2,1)S(1)} %collective-permute-done.11.c2, ...), custom_call_target="tpu_custom_call" | custom-call | flops 1879048192 | bytes 3670016 | tf_op jit(solution)/shard_map/pallas_call | solution.py:222
  86.5 1.3 copy-done.15
  90.7 4.2 %shard_map.96 = (bf16[256,896]{1,0:T(8,128)(2,1)}, bf16[2,256,896]{2,1,0:T(8,128)(2,1)}) custom-call(f32[2,256,896]{2,1,0:T(8,128)} %copy-done, bf16[2,256,896]{2,1,0:T(8,128)(2,1)} %copy-done.16, f32[256,896]{1,0:T(8,128)} %copy-done.1, bf16[256,896]{1,0:T(8,128)(2,1)} %copy-done.17), custom_call_target="tpu_custom_call" | custom-call | flops 4587520 | bytes 5505024 | tf_op jit(solution)/shard_map/pallas_call | solution.py:257
  95.7 3.4 %collective-permute-start.29 = (bf16[2,256,896]{2,1,0:T(8,128)(2,1)}, bf16[2,256,896]{2,1,0:T(8,128)(2,1)S(1)}, u32[]{:S(2)}, u32[]{:S(2)}) collective-permute-start(bf16[2,256,896]{2,1,0:T(8,128)(2,1)} %get-tuple-element.50.own.p0), channel_id=1, source_target_pairs={{0,1},{1,2},{2,3},{3,0},{4,7},{5,4},{6,5},{7,6},{8,9},{9,10},{10,1... | collective-permute-start | bytes 2752520 | tf_op jit(solution)/shard_map/ppermute | solution.py:49
  99.1 5.0 %collective-permute-start.31 = (bf16[2,256,896]{2,1,0:T(8,128)(2,1)S(1)}, bf16[2,256,896]{2,1,0:T(8,128)(2,1)S(1)}, u32[]{:S(2)}, u32[]{:S(2)}) collective-permute-start(bf16[2,256,896]{2,1,0:T(8,128)(2,1)S(1)} %collective-permute-done.21.other.p1), channel_id=1, source_target_pairs={{0,1},{1,2},{2,3},{3,0},{4,7},{5,4},{6,5},{7,6},{8,9},{9,10},{10,1... | collective-permute-start | bytes 2752520 | tf_op jit(solution)/shard_map/ppermute | solution.py:49
  104.1 2.2 collective-permute-start.14
  106.3 1.7 collective-permute-done.14.other
  109.0 4.8 %shard_map.97 = (bf16[4,512,128]{2,1,0:T(8,128)(2,1)S(1)}, bf16[4,512,128]{2,1,0:T(8,128)(2,1)S(1)}, bf16[4,512,128]{2,1,0:T(8,128)(2,1)S(1)}, bf16[4,512,128]{2,1,0:T(8,128)(2,1)S(1)}) custom-call(bf16[256,896]{1,0:T(8,128)(2,1)S(1)} %copy-done.14, bf16[256,896]{1,0:T(8,128)(2,1)S(1)} %collective-permute-done.14.other, bf16[896,2048]{1,0:T(8,128)(2,1)} %wd.3), custom_call_target="tpu_custom_call" | custom-call | flops 1879048192 | bytes 3670016 | tf_op jit(solution)/shard_map/pallas_call | solution.py:308
  113.9 3.2 %collective-permute-start.16 = (bf16[4,512,128]{2,1,0:T(8,128)(2,1)S(1)}, bf16[4,512,128]{2,1,0:T(8,128)(2,1)S(1)}, u32[]{:S(2)}, u32[]{:S(2)}) collective-permute-start(bf16[4,512,128]{2,1,0:T(8,128)(2,1)S(1)} %get-tuple-element.44), channel_id=1, source_target_pairs={{0,96},{4,36},{8,104},{12,44},{16,112},{20,52},{24,120},{28,60},{3... | collective-permute-start | bytes 1572872 | tf_op jit(solution)/shard_map/ppermute | solution.py:40
  117.1 5.7 %shard_map.102 = (bf16[224,2048]{1,0:T(8,128)(2,1)S(1)}, bf16[224,2048]{1,0:T(8,128)(2,1)S(1)}, bf16[224,2048]{1,0:T(8,128)(2,1)}, bf16[224,2048]{1,0:T(8,128)(2,1)S(1)}) custom-call(bf16[256,896]{1,0:T(8,128)(2,1)S(1)} %copy-done.14, bf16[256,896]{1,0:T(8,128)(2,1)S(1)} %collective-permute-done.14.other, bf16[512,2048]{1,0:T(8,128)(2,1)} %copy-done.15), custom_call_target="tpu_custom_call" | custom-call | flops 1879048192 | bytes 2097152 | tf_op jit(solution)/shard_map/pallas_call | solution.py:421
  122.8 2.0 collective-permute-start.33
  124.8 3.0 %collective-permute-done.31.p4 = bf16[2,256,896]{2,1,0:T(8,128)(2,1)S(1)} collective-permute-done((bf16[2,256,896]{2,1,0:T(8,128)(2,1)S(1)}, bf16[2,256,896]{2,1,0:T(8,128)(2,1)S(1)}, u32[]{:S(2)}, u32[]{:S(2)}) %collective-permute-start.31) | collective-permute-done | bytes 917536 | tf_op jit(solution)/shard_map/ppermute | solution.py:49
  127.9 7.2 %shard_map.99 = (bf16[4,512,128]{2,1,0:T(8,128)(2,1)S(1)}, bf16[4,512,128]{2,1,0:T(8,128)(2,1)S(1)}, bf16[4,512,128]{2,1,0:T(8,128)(2,1)S(1)}, bf16[4,512,128]{2,1,0:T(8,128)(2,1)S(1)}) custom-call(bf16[2,256,896]{2,1,0:T(8,128)(2,1)S(1)} %copy-done.5, bf16[2,256,896]{2,1,0:T(8,128)(2,1)S(1)} %collective-permute-done.21.other.p1, bf16[2048,896]{1,0:T(8,128)(2,1)} %wg.3, ...), custom_call_target="tpu_custom_call" | custom-call | flops 3758096384 | bytes 7340032 | tf_op jit(solution)/shard_map/pallas_call | solution.py:368
  135.0 2.6 %collective-permute-done.15.a1 = bf16[4,512,128]{2,1,0:T(8,128)(2,1)S(1)} collective-permute-done((bf16[4,512,128]{2,1,0:T(8,128)(2,1)S(1)}, bf16[4,512,128]{2,1,0:T(8,128)(2,1)S(1)}, u32[]{:S(2)}, u32[]{:S(2)}) %collective-permute-start.15) | collective-permute-done | bytes 524320 | tf_op jit(solution)/shard_map/ppermute | solution.py:40
  137.6 2.4 %collective-permute-start.22 = (bf16[4,512,128]{2,1,0:T(8,128)(2,1)S(1)}, bf16[4,512,128]{2,1,0:T(8,128)(2,1)S(1)}, u32[]{:S(2)}, u32[]{:S(2)}) collective-permute-start(bf16[4,512,128]{2,1,0:T(8,128)(2,1)S(1)} %get-tuple-element.52), channel_id=1, source_target_pairs={{0,8},{4,28},{8,16},{12,4},{16,24},{20,12},{24,0},{28,20},{32,40},... | collective-permute-start | bytes 1572872 | tf_op jit(solution)/shard_map/ppermute | solution.py:40
  140.0 1.8 collective-permute-start.23
  141.8 4.3 %collective-permute-done.17.a3 = bf16[4,512,128]{2,1,0:T(8,128)(2,1)S(1)} collective-permute-done((bf16[4,512,128]{2,1,0:T(8,128)(2,1)S(1)}, bf16[4,512,128]{2,1,0:T(8,128)(2,1)S(1)}, u32[]{:S(2)}, u32[]{:S(2)}) %collective-permute-start.17) | collective-permute-done | bytes 524320 | tf_op jit(solution)/shard_map/ppermute | solution.py:40
  146.3 12.5 %collective-permute-done.22.a1 = bf16[4,512,128]{2,1,0:T(8,128)(2,1)S(1)} collective-permute-done((bf16[4,512,128]{2,1,0:T(8,128)(2,1)S(1)}, bf16[4,512,128]{2,1,0:T(8,128)(2,1)S(1)}, u32[]{:S(2)}, u32[]{:S(2)}) %collective-permute-start.22) | collective-permute-done | bytes 524320 | tf_op jit(solution)/shard_map/ppermute | solution.py:40
  158.8 12.0 %collective-permute-start.18 = (bf16[512,128]{1,0:T(8,128)(2,1)S(1)}, bf16[512,128]{1,0:T(8,128)(2,1)S(1)}, u32[]{:S(2)}, u32[]{:S(2)}) collective-permute-start(bf16[512,128]{1,0:T(8,128)(2,1)S(1)} %get-tuple-element.47), channel_id=1, source_target_pairs={{0,8},{4,28},{8,16},{12,4},{16,24},{20,12},{24,0},{28,20},{32,40},... | collective-permute-start | bytes 393224 | tf_op jit(solution)/shard_map/ppermute | solution.py:40
  170.8 2.0 collective-permute-done.24.a3
  172.8 2.6 %collective-permute-start.20 = (bf16[512,128]{1,0:T(8,128)(2,1)S(1)}, bf16[512,128]{1,0:T(8,128)(2,1)S(1)}, u32[]{:S(2)}, u32[]{:S(2)}) collective-permute-start(bf16[512,128]{1,0:T(8,128)(2,1)S(1)} %get-tuple-element.49), channel_id=1, source_target_pairs={{0,16},{4,20},{8,24},{12,28},{16,0},{20,4},{24,8},{28,12},{32,48},... | collective-permute-start | bytes 393224 | tf_op jit(solution)/shard_map/ppermute | solution.py:40
  175.7 1.2 collective-permute-done.19
  176.9 3.1 %collective-permute-done.20 = bf16[512,128]{1,0:T(8,128)(2,1)S(1)} collective-permute-done((bf16[512,128]{1,0:T(8,128)(2,1)S(1)}, bf16[512,128]{1,0:T(8,128)(2,1)S(1)}, u32[]{:S(2)}, u32[]{:S(2)}) %collective-permute-start.20) | collective-permute-done | bytes 131104 | tf_op jit(solution)/shard_map/ppermute | solution.py:40
  180.0 1.8 collective-permute-done.25
  182.4 1.4 add_convert_fusion.1
  183.8 2.2 %collective-permute-done.26 = bf16[512,128]{1,0:T(8,128)(2,1)S(1)} collective-permute-done((bf16[512,128]{1,0:T(8,128)(2,1)S(1)}, bf16[512,128]{1,0:T(8,128)(2,1)S(1)}, u32[]{:S(2)}, u32[]{:S(2)}) %collective-permute-start.26) | collective-permute-done | bytes 131104 | tf_op jit(solution)/shard_map/ppermute | solution.py:40
  186.1 3.8 %collective-permute-start.36 = (bf16[224,2048]{1,0:T(8,128)(2,1)}, bf16[224,2048]{1,0:T(8,128)(2,1)}, u32[]{:S(2)}, u32[]{:S(2)}) collective-permute-start(bf16[224,2048]{1,0:T(8,128)(2,1)} %add_convert_fusion.1), channel_id=1, source_target_pairs={{0,1},{1,2},{2,3},{3,0},{4,7},{5,4},{6,5},{7,6},{8,9},{9,10},{10,1... | collective-permute-start | bytes 2752520 | tf_op jit(solution)/shard_map/ppermute | solution.py:49
  193.2 1.2 copy-done.7
  197.9 8.0 %shard_map.101 = (bf16[512,896]{1,0:T(8,128)(2,1)}, bf16[512,896]{1,0:T(8,128)(2,1)}) custom-call(bf16[512,2048]{1,0:T(8,128)(2,1)} %all-gather.2.cloned.1.call-done.tok, bf16[2,256,896]{2,1,0:T(8,128)(2,1)S(1)} %copy-done.5, bf16[2,256,896]{2,1,0:T(8,128)(2,1)S(1)} %collective-permute-done.21.other.p1, bf16[2,256,896]{2,1,0:T(8,128)(2,1)S(1)} %copy-done.7, ...), custom_call_target="tpu_custom_call" | custom-call | flops 3758096384 | bytes 4587520 | tf_op jit(solution)/shard_map/pallas_call | solution.py:478
  205.9 4.3 %collective-permute-done.36 = bf16[224,2048]{1,0:T(8,128)(2,1)} collective-permute-done((bf16[224,2048]{1,0:T(8,128)(2,1)}, bf16[224,2048]{1,0:T(8,128)(2,1)}, u32[]{:S(2)}, u32[]{:S(2)}) %collective-permute-start.36) | collective-permute-done | bytes 917536 | tf_op jit(solution)/shard_map/ppermute | solution.py:49
  210.8 2.8 %add_convert_fusion = bf16[224,2048]{1,0:T(8,128)(2,1)} fusion(bf16[224,2048]{1,0:T(8,128)(2,1)} %collective-permute-done.37, bf16[224,2048]{1,0:T(8,128)(2,1)} %collective-permute-done.36, bf16[224,2048]{1,0:T(8,128)(2,1)S(1)} %get-tuple-element.63), kind=kLoop, calls=%fused_computation | loop fusion | flops 2752512 | bytes 3670016 | tf_op jit(solution)/shard_map/convert_element_type | solution.py:521
  (84 shorter events, 18.7 us)
Async XLA Ops:
  7.2 186.1 %all-gather.2.cloned.1.call-start = ((), (), s32[]{:S(2)}) async-start(), calls=%async_computation | async-start | bytes 2228224 | tf_op jit(solution)/shard_map/all_gather | solution.py:540
  7.2 6.5 %collective-permute-start = (bf16[512,128]{1,0:T(8,128)(2,1)}, bf16[512,128]{1,0:T(8,128)(2,1)S(1)}, u32[]{:S(2)}, u32[]{:S(2)}) collective-permute-start(bf16[512,128]{1,0:T(8,128)(2,1)} %refs_0_.2), channel_id=1, source_target_pairs={{0,8},{4,28},{8,16},{12,4},{16,24},{20,12},{24,0},{28,20},{32,40},... | collective-permute-start | bytes 393224 | tf_op jit(solution)/shard_map/ppermute | solution.py:40
  8.9 5.2 %collective-permute-start.1 = (bf16[512,128]{1,0:T(8,128)(2,1)}, bf16[512,128]{1,0:T(8,128)(2,1)S(1)}, u32[]{:S(2)}, u32[]{:S(2)}) collective-permute-start(bf16[512,128]{1,0:T(8,128)(2,1)} %refs_0_.2), channel_id=1, source_target_pairs={{0,24},{4,12},{8,0},{12,20},{16,8},{20,28},{24,16},{28,4},{32,56},... | collective-permute-start | bytes 393224 | tf_op jit(solution)/shard_map/ppermute | solution.py:40
  10.5 7.8 %collective-permute-start.2 = (bf16[512,128]{1,0:T(8,128)(2,1)}, bf16[512,128]{1,0:T(8,128)(2,1)S(1)}, u32[]{:S(2)}, u32[]{:S(2)}) collective-permute-start(bf16[512,128]{1,0:T(8,128)(2,1)} %refs_0_.2), channel_id=1, source_target_pairs={{0,16},{4,20},{8,24},{12,28},{16,0},{20,4},{24,8},{28,12},{32,48},... | collective-permute-start | bytes 393224 | tf_op jit(solution)/shard_map/ppermute | solution.py:40
  20.0 40.3 %collective-permute-start.3 = (bf16[4,512,128]{2,1,0:T(8,128)(2,1)S(1)}, bf16[4,512,128]{2,1,0:T(8,128)(2,1)S(1)}, u32[]{:S(2)}, u32[]{:S(2)}) collective-permute-start(bf16[4,512,128]{2,1,0:T(8,128)(2,1)S(1)} %shard_map.92.t0), channel_id=1, source_target_pairs={{0,32},{4,100},{8,40},{12,108},{16,48},{20,116},{24,56},{28,124},{... | collective-permute-start | bytes 1572872 | tf_op jit(solution)/shard_map/ppermute | solution.py:40
  21.6 40.8 %collective-permute-start.4 = (bf16[4,512,128]{2,1,0:T(8,128)(2,1)S(1)}, bf16[4,512,128]{2,1,0:T(8,128)(2,1)S(1)}, u32[]{:S(2)}, u32[]{:S(2)}) collective-permute-start(bf16[4,512,128]{2,1,0:T(8,128)(2,1)S(1)} %shard_map.92.t0), channel_id=1, source_target_pairs={{0,96},{4,36},{8,104},{12,44},{16,112},{20,52},{24,120},{28,60},{3... | collective-permute-start | bytes 1572872 | tf_op jit(solution)/shard_map/ppermute | solution.py:40
  23.3 39.2 %collective-permute-start.5 = (bf16[4,512,128]{2,1,0:T(8,128)(2,1)S(1)}, bf16[4,512,128]{2,1,0:T(8,128)(2,1)S(1)}, u32[]{:S(2)}, u32[]{:S(2)}) collective-permute-start(bf16[4,512,128]{2,1,0:T(8,128)(2,1)S(1)} %shard_map.92.t0), channel_id=1, source_target_pairs={{0,64},{4,68},{8,72},{12,76},{16,80},{20,84},{24,88},{28,92},{32,9... | collective-permute-start | bytes 1572872 | tf_op jit(solution)/shard_map/ppermute | solution.py:40
  25.2 23.5 %collective-permute-start.7 = (bf16[512,128]{1,0:T(8,128)(2,1)}, bf16[512,128]{1,0:T(8,128)(2,1)S(1)}, u32[]{:S(2)}, u32[]{:S(2)}) collective-permute-start(bf16[512,128]{1,0:T(8,128)(2,1)} %refs_0_.3), channel_id=1, source_target_pairs={{0,32},{4,100},{8,40},{12,108},{16,48},{20,116},{24,56},{28,124},{... | collective-permute-start | bytes 393224 | tf_op jit(solution)/shard_map/ppermute | solution.py:40
  25.9 24.9 %collective-permute-start.8 = (bf16[512,128]{1,0:T(8,128)(2,1)}, bf16[512,128]{1,0:T(8,128)(2,1)S(1)}, u32[]{:S(2)}, u32[]{:S(2)}) collective-permute-start(bf16[512,128]{1,0:T(8,128)(2,1)} %refs_0_.3), channel_id=1, source_target_pairs={{0,96},{4,36},{8,104},{12,44},{16,112},{20,52},{24,120},{28,60},{3... | collective-permute-start | bytes 393224 | tf_op jit(solution)/shard_map/ppermute | solution.py:40
  48.7 6.7 %collective-permute-start.9 = (bf16[512,128]{1,0:T(8,128)(2,1)}, bf16[512,128]{1,0:T(8,128)(2,1)S(1)}, u32[]{:S(2)}, u32[]{:S(2)}) collective-permute-start(bf16[512,128]{1,0:T(8,128)(2,1)} %refs_0_.3), channel_id=1, source_target_pairs={{0,64},{4,68},{8,72},{12,76},{16,80},{20,84},{24,88},{28,92},{32,9... | collective-permute-start | bytes 393224 | tf_op jit(solution)/shard_map/ppermute | solution.py:40
  57.0 24.2 %collective-permute-start.10 = (bf16[4,512,128]{2,1,0:T(8,128)(2,1)S(1)}, bf16[4,512,128]{2,1,0:T(8,128)(2,1)S(1)}, u32[]{:S(2)}, u32[]{:S(2)}) collective-permute-start(bf16[4,512,128]{2,1,0:T(8,128)(2,1)S(1)} %shard_map.94.c0), channel_id=1, source_target_pairs={{0,8},{4,28},{8,16},{12,4},{16,24},{20,12},{24,0},{28,20},{32,40},... | collective-permute-start | bytes 1572872 | tf_op jit(solution)/shard_map/ppermute | solution.py:40
  60.3 20.9 %collective-permute-start.11 = (bf16[4,512,128]{2,1,0:T(8,128)(2,1)S(1)}, bf16[4,512,128]{2,1,0:T(8,128)(2,1)S(1)}, u32[]{:S(2)}, u32[]{:S(2)}) collective-permute-start(bf16[4,512,128]{2,1,0:T(8,128)(2,1)S(1)} %shard_map.94.c0), channel_id=1, source_target_pairs={{0,24},{4,12},{8,0},{12,20},{16,8},{20,28},{24,16},{28,4},{32,56},... | collective-permute-start | bytes 1572872 | tf_op jit(solution)/shard_map/ppermute | solution.py:40
  60.3 20.9 %collective-permute-start.12 = (bf16[4,512,128]{2,1,0:T(8,128)(2,1)S(1)}, bf16[4,512,128]{2,1,0:T(8,128)(2,1)S(1)}, u32[]{:S(2)}, u32[]{:S(2)}) collective-permute-start(bf16[4,512,128]{2,1,0:T(8,128)(2,1)S(1)} %shard_map.94.c0), channel_id=1, source_target_pairs={{0,16},{4,20},{8,24},{12,28},{16,0},{20,4},{24,8},{28,12},{32,48},... | collective-permute-start | bytes 1572872 | tf_op jit(solution)/shard_map/ppermute | solution.py:40
  69.4 1.2 copy-start
  70.6 17.2 %copy-start.4 = (bf16[512,128]{1,0:T(8,128)(2,1)S(1)}, bf16[512,128]{1,0:T(8,128)(2,1)}, u32[]{:S(2)}) copy-start(bf16[512,128]{1,0:T(8,128)(2,1)} %refs_0_.2) | copy-start | bytes 393220
  70.6 19.0 %collective-permute-start.6 = (bf16[2,256,896]{2,1,0:T(8,128)(2,1)S(1)}, bf16[2,256,896]{2,1,0:T(8,128)(2,1)S(1)}, u32[]{:S(2)}, u32[]{:S(2)}) collective-permute-start(bf16[2,256,896]{2,1,0:T(8,128)(2,1)S(1)} %get-tuple-element.38), channel_id=1, source_target_pairs={{0,4},{4,0},{1,5},{5,1},{2,6},{6,2},{3,7},{7,3},{8,12},{12,8},{9,1... | collective-permute-start | bytes 2752520 | tf_op jit(solution)/shard_map/ppermute | solution.py:53
  86.5 1.3 copy-start.15
  87.8 1.8 collective-permute-start.13
  87.8 7.2 %collective-permute-start.28 = (bf16[512,128]{1,0:T(8,128)(2,1)S(1)}, bf16[512,128]{1,0:T(8,128)(2,1)S(1)}, u32[]{:S(2)}, u32[]{:S(2)}) collective-permute-start(bf16[512,128]{1,0:T(8,128)(2,1)S(1)} %copy-done.4), channel_id=1, source_target_pairs={{0,0},{1,32},{2,64},{3,96},{8,8},{9,40},{10,72},{11,104},{16,16},{... | collective-permute-start | bytes 393224 | tf_op jit(solution)/shard_map/ppermute | solution.py:62
  94.9 4.2 %collective-permute-start.21 = (bf16[2,256,896]{2,1,0:T(8,128)(2,1)}, bf16[2,256,896]{2,1,0:T(8,128)(2,1)S(1)}, u32[]{:S(2)}, u32[]{:S(2)}) collective-permute-start(bf16[2,256,896]{2,1,0:T(8,128)(2,1)} %get-tuple-element.50.own.p0), channel_id=1, source_target_pairs={{0,4},{4,0},{1,5},{5,1},{2,6},{6,2},{3,7},{7,3},{8,12},{12,8},{9,1... | collective-permute-start | bytes 2752520 | tf_op jit(solution)/shard_map/ppermute | solution.py:53
  95.7 27.1 %collective-permute-start.29 = (bf16[2,256,896]{2,1,0:T(8,128)(2,1)}, bf16[2,256,896]{2,1,0:T(8,128)(2,1)S(1)}, u32[]{:S(2)}, u32[]{:S(2)}) collective-permute-start(bf16[2,256,896]{2,1,0:T(8,128)(2,1)} %get-tuple-element.50.own.p0), channel_id=1, source_target_pairs={{0,1},{1,2},{2,3},{3,0},{4,7},{5,4},{6,5},{7,6},{8,9},{9,10},{10,1... | collective-permute-start | bytes 2752520 | tf_op jit(solution)/shard_map/ppermute | solution.py:49
  99.1 28.8 %collective-permute-start.31 = (bf16[2,256,896]{2,1,0:T(8,128)(2,1)S(1)}, bf16[2,256,896]{2,1,0:T(8,128)(2,1)S(1)}, u32[]{:S(2)}, u32[]{:S(2)}) collective-permute-start(bf16[2,256,896]{2,1,0:T(8,128)(2,1)S(1)} %collective-permute-done.21.other.p1), channel_id=1, source_target_pairs={{0,1},{1,2},{2,3},{3,0},{4,7},{5,4},{6,5},{7,6},{8,9},{9,10},{10,1... | collective-permute-start | bytes 2752520 | tf_op jit(solution)/shard_map/ppermute | solution.py:49
  104.1 3.8 %collective-permute-start.14 = (bf16[256,896]{1,0:T(8,128)(2,1)}, bf16[256,896]{1,0:T(8,128)(2,1)S(1)}, u32[]{:S(2)}, u32[]{:S(2)}) collective-permute-start(bf16[256,896]{1,0:T(8,128)(2,1)} %get-tuple-element.41.own), channel_id=1, source_target_pairs={{0,4},{4,0},{1,5},{5,1},{2,6},{6,2},{3,7},{7,3},{8,12},{12,8},{9,1... | collective-permute-start | bytes 1376264 | tf_op jit(solution)/shard_map/ppermute | solution.py:53
  113.8 23.8 %collective-permute-start.15 = (bf16[4,512,128]{2,1,0:T(8,128)(2,1)S(1)}, bf16[4,512,128]{2,1,0:T(8,128)(2,1)S(1)}, u32[]{:S(2)}, u32[]{:S(2)}) collective-permute-start(bf16[4,512,128]{2,1,0:T(8,128)(2,1)S(1)} %get-tuple-element.43), channel_id=1, source_target_pairs={{0,32},{4,100},{8,40},{12,108},{16,48},{20,116},{24,56},{28,124},{... | collective-permute-start | bytes 1572872 | tf_op jit(solution)/shard_map/ppermute | solution.py:40
  113.9 26.1 %collective-permute-start.16 = (bf16[4,512,128]{2,1,0:T(8,128)(2,1)S(1)}, bf16[4,512,128]{2,1,0:T(8,128)(2,1)S(1)}, u32[]{:S(2)}, u32[]{:S(2)}) collective-permute-start(bf16[4,512,128]{2,1,0:T(8,128)(2,1)S(1)} %get-tuple-element.44), channel_id=1, source_target_pairs={{0,96},{4,36},{8,104},{12,44},{16,112},{20,52},{24,120},{28,60},{3... | collective-permute-start | bytes 1572872 | tf_op jit(solution)/shard_map/ppermute | solution.py:40
  117.1 28.9 %collective-permute-start.17 = (bf16[4,512,128]{2,1,0:T(8,128)(2,1)S(1)}, bf16[4,512,128]{2,1,0:T(8,128)(2,1)S(1)}, u32[]{:S(2)}, u32[]{:S(2)}) collective-permute-start(bf16[4,512,128]{2,1,0:T(8,128)(2,1)S(1)} %get-tuple-element.45), channel_id=1, source_target_pairs={{0,64},{4,68},{8,72},{12,76},{16,80},{20,84},{24,88},{28,92},{32,9... | collective-permute-start | bytes 1572872 | tf_op jit(solution)/shard_map/ppermute | solution.py:40
  117.1 10.7 %copy-start.5 = (bf16[2,256,896]{2,1,0:T(8,128)(2,1)S(1)}, bf16[2,256,896]{2,1,0:T(8,128)(2,1)}, u32[]{:S(2)}) copy-start(bf16[2,256,896]{2,1,0:T(8,128)(2,1)} %get-tuple-element.50.own.p0) | copy-start | bytes 2752516
  122.8 54.1 %copy-start.6 = (bf16[2,256,896]{2,1,0:T(8,128)(2,1)}, bf16[2,256,896]{2,1,0:T(8,128)(2,1)S(1)}, u32[]{:S(2)}) copy-start(bf16[2,256,896]{2,1,0:T(8,128)(2,1)S(1)} %collective-permute-done.29.p2) | copy-start | bytes 2752516
  122.8 59.0 %collective-permute-start.33 = (bf16[2,256,896]{2,1,0:T(8,128)(2,1)S(1)}, bf16[2,256,896]{2,1,0:T(8,128)(2,1)}, u32[]{:S(2)}, u32[]{:S(2)}) collective-permute-start(bf16[2,256,896]{2,1,0:T(8,128)(2,1)S(1)} %collective-permute-done.29.p2), channel_id=1, source_target_pairs={{0,1},{1,2},{2,3},{3,0},{4,7},{5,4},{6,5},{7,6},{8,9},{9,10},{10,1... | collective-permute-start | bytes 2752520 | tf_op jit(solution)/shard_map/ppermute | solution.py:49
  127.8 54.0 %copy-start.8 = (bf16[2,256,896]{2,1,0:T(8,128)(2,1)}, bf16[2,256,896]{2,1,0:T(8,128)(2,1)S(1)}, u32[]{:S(2)}) copy-start(bf16[2,256,896]{2,1,0:T(8,128)(2,1)S(1)} %collective-permute-done.31.p4) | copy-start | bytes 2752516
  127.8 54.1 %collective-permute-start.35 = (bf16[224,2048]{1,0:T(8,128)(2,1)S(1)}, bf16[224,2048]{1,0:T(8,128)(2,1)S(1)}, u32[]{:S(2)}, u32[]{:S(2)}) collective-permute-start(bf16[224,2048]{1,0:T(8,128)(2,1)S(1)} %get-tuple-element.66), channel_id=1, source_target_pairs={{0,1},{1,2},{2,3},{3,0},{4,7},{5,4},{6,5},{7,6},{8,9},{9,10},{10,1... | collective-permute-start | bytes 2752520 | tf_op jit(solution)/shard_map/ppermute | solution.py:49
  137.6 21.2 %collective-permute-start.22 = (bf16[4,512,128]{2,1,0:T(8,128)(2,1)S(1)}, bf16[4,512,128]{2,1,0:T(8,128)(2,1)S(1)}, u32[]{:S(2)}, u32[]{:S(2)}) collective-permute-start(bf16[4,512,128]{2,1,0:T(8,128)(2,1)S(1)} %get-tuple-element.52), channel_id=1, source_target_pairs={{0,8},{4,28},{8,16},{12,4},{16,24},{20,12},{24,0},{28,20},{32,40},... | collective-permute-start | bytes 1572872 | tf_op jit(solution)/shard_map/ppermute | solution.py:40
  140.0 30.8 %collective-permute-start.23 = (bf16[4,512,128]{2,1,0:T(8,128)(2,1)S(1)}, bf16[4,512,128]{2,1,0:T(8,128)(2,1)S(1)}, u32[]{:S(2)}, u32[]{:S(2)}) collective-permute-start(bf16[4,512,128]{2,1,0:T(8,128)(2,1)S(1)} %get-tuple-element.53), channel_id=1, source_target_pairs={{0,24},{4,12},{8,0},{12,20},{16,8},{20,28},{24,16},{28,4},{32,56},... | collective-permute-start | bytes 1572872 | tf_op jit(solution)/shard_map/ppermute | solution.py:40
  146.0 26.7 %collective-permute-start.24 = (bf16[4,512,128]{2,1,0:T(8,128)(2,1)S(1)}, bf16[4,512,128]{2,1,0:T(8,128)(2,1)S(1)}, u32[]{:S(2)}, u32[]{:S(2)}) collective-permute-start(bf16[4,512,128]{2,1,0:T(8,128)(2,1)S(1)} %get-tuple-element.54), channel_id=1, source_target_pairs={{0,16},{4,20},{8,24},{12,28},{16,0},{20,4},{24,8},{28,12},{32,48},... | collective-permute-start | bytes 1572872 | tf_op jit(solution)/shard_map/ppermute | solution.py:40
  158.8 16.9 %collective-permute-start.18 = (bf16[512,128]{1,0:T(8,128)(2,1)S(1)}, bf16[512,128]{1,0:T(8,128)(2,1)S(1)}, u32[]{:S(2)}, u32[]{:S(2)}) collective-permute-start(bf16[512,128]{1,0:T(8,128)(2,1)S(1)} %get-tuple-element.47), channel_id=1, source_target_pairs={{0,8},{4,28},{8,16},{12,4},{16,24},{20,12},{24,0},{28,20},{32,40},... | collective-permute-start | bytes 393224 | tf_op jit(solution)/shard_map/ppermute | solution.py:40
  170.8 6.1 %collective-permute-start.19 = (bf16[512,128]{1,0:T(8,128)(2,1)S(1)}, bf16[512,128]{1,0:T(8,128)(2,1)S(1)}, u32[]{:S(2)}, u32[]{:S(2)}) collective-permute-start(bf16[512,128]{1,0:T(8,128)(2,1)S(1)} %get-tuple-element.48), channel_id=1, source_target_pairs={{0,24},{4,12},{8,0},{12,20},{16,8},{20,28},{24,16},{28,4},{32,56},... | collective-permute-start | bytes 393224 | tf_op jit(solution)/shard_map/ppermute | solution.py:40
  172.8 7.3 %collective-permute-start.20 = (bf16[512,128]{1,0:T(8,128)(2,1)S(1)}, bf16[512,128]{1,0:T(8,128)(2,1)S(1)}, u32[]{:S(2)}, u32[]{:S(2)}) collective-permute-start(bf16[512,128]{1,0:T(8,128)(2,1)S(1)} %get-tuple-element.49), channel_id=1, source_target_pairs={{0,16},{4,20},{8,24},{12,28},{16,0},{20,4},{24,8},{28,12},{32,48},... | collective-permute-start | bytes 393224 | tf_op jit(solution)/shard_map/ppermute | solution.py:40
  175.6 6.2 %collective-permute-start.25 = (bf16[512,128]{1,0:T(8,128)(2,1)S(1)}, bf16[512,128]{1,0:T(8,128)(2,1)S(1)}, u32[]{:S(2)}, u32[]{:S(2)}) collective-permute-start(bf16[512,128]{1,0:T(8,128)(2,1)S(1)} %get-tuple-element.56), channel_id=1, source_target_pairs={{0,32},{4,100},{8,40},{12,108},{16,48},{20,116},{24,56},{28,124},{... | collective-permute-start | bytes 393224 | tf_op jit(solution)/shard_map/ppermute | solution.py:40
  176.9 14.5 %collective-permute-start.30 = (bf16[2,256,896]{2,1,0:T(8,128)(2,1)S(1)}, bf16[2,256,896]{2,1,0:T(8,128)(2,1)S(1)}, u32[]{:S(2)}, u32[]{:S(2)}) collective-permute-start(bf16[2,256,896]{2,1,0:T(8,128)(2,1)S(1)} %collective-permute-done.29.p2), channel_id=1, source_target_pairs={{0,4},{4,0},{1,5},{5,1},{2,6},{6,2},{3,7},{7,3},{8,12},{12,8},{9,1... | collective-permute-start | bytes 2752520 | tf_op jit(solution)/shard_map/ppermute | solution.py:53
  180.0 6.0 %collective-permute-start.26 = (bf16[512,128]{1,0:T(8,128)(2,1)S(1)}, bf16[512,128]{1,0:T(8,128)(2,1)S(1)}, u32[]{:S(2)}, u32[]{:S(2)}) collective-permute-start(bf16[512,128]{1,0:T(8,128)(2,1)S(1)} %get-tuple-element.57), channel_id=1, source_target_pairs={{0,96},{4,36},{8,104},{12,44},{16,112},{20,52},{24,120},{28,60},{3... | collective-permute-start | bytes 393224 | tf_op jit(solution)/shard_map/ppermute | solution.py:40
  181.8 8.1 %collective-permute-start.27 = (bf16[512,128]{1,0:T(8,128)(2,1)S(1)}, bf16[512,128]{1,0:T(8,128)(2,1)S(1)}, u32[]{:S(2)}, u32[]{:S(2)}) collective-permute-start(bf16[512,128]{1,0:T(8,128)(2,1)S(1)} %get-tuple-element.58), channel_id=1, source_target_pairs={{0,64},{4,68},{8,72},{12,76},{16,80},{20,84},{24,88},{28,92},{32,9... | collective-permute-start | bytes 393224 | tf_op jit(solution)/shard_map/ppermute | solution.py:40
  181.9 10.4 %collective-permute-start.32 = (bf16[2,256,896]{2,1,0:T(8,128)(2,1)S(1)}, bf16[2,256,896]{2,1,0:T(8,128)(2,1)S(1)}, u32[]{:S(2)}, u32[]{:S(2)}) collective-permute-start(bf16[2,256,896]{2,1,0:T(8,128)(2,1)S(1)} %collective-permute-done.31.p4), channel_id=1, source_target_pairs={{0,4},{4,0},{1,5},{5,1},{2,6},{6,2},{3,7},{7,3},{8,12},{12,8},{9,1... | collective-permute-start | bytes 2752520 | tf_op jit(solution)/shard_map/ppermute | solution.py:53
  182.0 11.3 %collective-permute-start.34 = (bf16[2,256,896]{2,1,0:T(8,128)(2,1)}, bf16[2,256,896]{2,1,0:T(8,128)(2,1)}, u32[]{:S(2)}, u32[]{:S(2)}) collective-permute-start(bf16[2,256,896]{2,1,0:T(8,128)(2,1)} %collective-permute-done.33.p6), channel_id=1, source_target_pairs={{0,4},{4,0},{1,5},{5,1},{2,6},{6,2},{3,7},{7,3},{8,12},{12,8},{9,1... | collective-permute-start | bytes 2752520 | tf_op jit(solution)/shard_map/ppermute | solution.py:53
  186.1 24.1 %collective-permute-start.36 = (bf16[224,2048]{1,0:T(8,128)(2,1)}, bf16[224,2048]{1,0:T(8,128)(2,1)}, u32[]{:S(2)}, u32[]{:S(2)}) collective-permute-start(bf16[224,2048]{1,0:T(8,128)(2,1)} %add_convert_fusion.1), channel_id=1, source_target_pairs={{0,1},{1,2},{2,3},{3,0},{4,7},{5,4},{6,5},{7,6},{8,9},{9,10},{10,1... | collective-permute-start | bytes 2752520 | tf_op jit(solution)/shard_map/ppermute | solution.py:49
  189.9 20.9 %collective-permute-start.37 = (bf16[224,2048]{1,0:T(8,128)(2,1)}, bf16[224,2048]{1,0:T(8,128)(2,1)}, u32[]{:S(2)}, u32[]{:S(2)}) collective-permute-start(bf16[224,2048]{1,0:T(8,128)(2,1)} %get-tuple-element.68), channel_id=1, source_target_pairs={{0,3},{1,0},{2,1},{3,2},{4,5},{5,6},{6,7},{7,4},{8,11},{9,8},{10,9... | collective-permute-start | bytes 2752520 | tf_op jit(solution)/shard_map/ppermute | solution.py:49
  193.2 1.2 copy-start.7
  194.4 1.2 copy-start.9
  196.8 1.2 copy-start.13
  (10 other events, 9.3 us)
Sparse Core Ops, SparseCore 0:
  95.8 65.8 all-gather.1

commit v2 on v1

v2 whole, which is shorter than its diff:
```python
import functools

import jax
import jax.numpy as jnp
from jax import lax
from jax.experimental import pallas as pl
from jax.experimental.pallas import tpu as pltpu
from jax.sharding import PartitionSpec as P

BF = jnp.bfloat16
F32 = jnp.float32
G = 4
MIB = 1024 * 1024
VM = pltpu.VMEM
HB = pltpu.HBM


def here():
    row = lax.axis_index("row")
    return row // G, row % G, lax.axis_index("col"), lax.axis_index("depth")


def plane_spots(phase, outgoing):
    y, x, core, _ = here()
    pos = jnp.where(core == phase, x, y)
    ahead, back, far = (pos + 1) % G, (pos + G - 1) % G, (pos + 2) % G
    return [pos, ahead, back, far] if outgoing else [pos, back, ahead, far]


def plane_at(core, k, j):
    return jnp.where(core == 0, k, j), jnp.where(core == 0, j, k)


def ring(pos, core):
    step = 1 - 2 * core
    return [pos, (pos - step + G) % G, (pos + step + G) % G, (pos + 2) % G]


def targets(pos, core):
    own, back, ahead, far = ring(pos, core)
    return [own, ahead, back, far]


def plane_shift(kind, array, phase):
    step = {1: 1, 2: G - 1, 3: 2}[kind]
    pairs = []
    for y in range(G):
        for x in range(G):
            for core in range(2):
                along_x = (core == 0) == (phase == 0)
                to_y = y if along_x else (y + step) % G
                to_x = (x + step) % G if along_x else x
                pairs.append(((y * G + x) * 2 + core, (to_y * G + to_x) * 2 + core))
    return lax.ppermute(array, ("row", "col"), pairs)


def depth_shift(kind, array):
    pairs = []
    for core in range(2):
        for z in range(G):
            step = {1: 1 - 2 * core, 2: 2 * core - 1, 3: 2}[kind]
            pairs.append((core * G + z, core * G + (z + step) % G))
    return lax.ppermute(array, ("col", "depth"), pairs)


def swap(array):
    return lax.ppermute(array, "col", [(0, 1), (1, 0)])


def after(array, *others):
    return lax.optimization_barrier((array,) + others)[0]


def spec(space):
    return pl.BlockSpec(memory_space=space)


def keep_out(array):
    return pltpu.with_memory_space_constraint(array, HB)


COST = 50


def call(body, outs, ins, scratch, flops, nbytes, out_spaces=None, limit=24):
    if out_spaces is None:
        out_spaces = (pl.ANY,) * len(outs)
    return pl.pallas_call(
        body,
        out_shape=outs,
        in_specs=[spec(space) for space in ins],
        out_specs=tuple(spec(space) for space in out_spaces),
        scratch_shapes=scratch,
        compiler_params=pltpu.CompilerParams(vmem_limit_bytes=limit * MIB),
        cost_estimate=pl.CostEstimate(
            flops=flops // COST, bytes_accessed=nbytes // COST, transcendentals=0
        ),
    )


def shape(dims, dtype=BF):
    return jax.ShapeDtypeStruct(dims, dtype)


def start_all(copies):
    for item in copies:
        item.start()


def wait_all(copies):
    for item in copies:
        item.wait()


def place_body(p0, p1, p2, p3, tok, cot):
    spots = plane_spots(0, False)
    for k, ref in enumerate((p0, p1, p2, p3)):
        tok[spots[k]] = ref[0]
        cot[spots[k]] = ref[1]


def place(parts):
    _, tok, feat = parts[0].shape
    return call(
        place_body,
        (shape((G, tok, feat)), shape((G, tok, feat))),
        (VM,) * G,
        [],
        0,
        G * tok * feat * 8,
        (VM, VM),
    )(*parts)


def pick_body(c0, c1, c2, c3, o0, o1, o2, o3, tok, sems, out_sems):
    _, _, core, z = here()
    spots = plane_spots(1, False)
    loads = [
        pltpu.make_async_copy(ref, tok.at[spots[k]], sems.at[k])
        for k, ref in enumerate((c0, c1, c2, c3))
    ]
    start_all(loads)
    groups = targets(z, core)
    stores = [
        pltpu.make_async_copy(
            tok.at[plane_at(core, groups[k], j)], ref.at[j], out_sems.at[k, j]
        )
        for k, ref in enumerate((o0, o1, o2, o3))
        for j in range(G)
    ]
    wait_all(loads)
    start_all(stores)
    wait_all(stores)


def pick(chunks):
    _, tok, part = chunks[0].shape
    return call(
        pick_body,
        (shape((G, tok, part)),) * G,
        (pl.ANY,) * G,
        [
            pltpu.VMEM((G, G, tok, part), BF),
            pltpu.SemaphoreType.DMA((G,)),
            pltpu.SemaphoreType.DMA((G, G)),
        ],
        0,
        4 * G * G * tok * part,
        limit=16,
    )(*chunks)


def wide(core, ref, chunk):
    return jnp.concatenate([ref[plane_at(core, chunk, j)] for j in range(G)], axis=1)


def keep_rows(core, acc, keep, sem):
    half = keep.shape[0]
    return pltpu.make_async_copy(
        acc.at[pl.ds(pl.multiple_of(core * half, half), half), :], keep, sem
    )


def send_rows(core, acc, stage, send, sem):
    half = send.shape[0]
    stage[...] = acc[pl.ds(pl.multiple_of((1 - core) * half, half), half), :].astype(BF)
    return pltpu.make_async_copy(stage, send, sem)


def gate_up_body(t0, t1, t2, t3, wg, wu, keep, send, tok, wgs, wus, acc_g, acc_u, stage, sems):
    core = lax.axis_index("col")
    spots = plane_spots(1, False)
    loads = [
        pltpu.make_async_copy(ref, tok.at[spots[k]], sems.at[k])
        for k, ref in enumerate((t0, t1, t2, t3))
    ]
    depth = wg.shape[0] // G
    weights = []
    for k in range(G):
        rows = pl.ds(k * depth, depth)
        weights.append(
            [
                pltpu.make_async_copy(wg.at[rows], wgs.at[rows], sems.at[G + 2 * k]),
                pltpu.make_async_copy(wu.at[rows], wus.at[rows], sems.at[G + 2 * k + 1]),
            ]
        )
    start_all(loads)
    for pair in weights:
        start_all(pair)
    wait_all(loads)
    for k in range(G):
        wait_all(weights[k])
        left = wide(core, tok, k)
        rows = slice(k * depth, (k + 1) * depth)
        for acc, ws in ((acc_g, wgs), (acc_u, wus)):
            term = jnp.dot(left, ws[rows, :], preferred_element_type=F32)
            if k == 0:
                acc[...] = term
            else:
                acc[...] += term
    kept = [
        keep_rows(core, acc_g, keep.at[0], sems.at[0]),
        keep_rows(core, acc_u, keep.at[1], sems.at[1]),
    ]
    start_all(kept)
    for n, acc in enumerate((acc_g, acc_u)):
        sent = send_rows(core, acc, stage.at[n], send.at[n], sems.at[2 + n])
        sent.start()
        kept.append(sent)
    wait_all(kept)


def gate_up(chunks, wg, wu):
    tok = chunks[0].shape[1]
    feats, hid = wg.shape
    return call(
        gate_up_body,
        (shape((2, tok // 2, hid), F32), shape((2, tok // 2, hid))),
        (pl.ANY,) * G + (HB, HB),
        [
            pltpu.VMEM((G,) + chunks[0].shape, BF),
            pltpu.VMEM((feats, hid), BF),
            pltpu.VMEM((feats, hid), BF),
            pltpu.VMEM((tok, hid), F32),
            pltpu.VMEM((tok, hid), F32),
            pltpu.VMEM((2, tok // 2, hid), BF),
            pltpu.SemaphoreType.DMA((3 * G,)),
        ],
        4 * tok * feats * hid,
        4 * feats * hid,
        (HB, pl.ANY),
    )(*chunks, keep_out(wg), keep_out(wu))


def d_act_body(c0, c1, c2, c3, wd, keep, send, cot, wds, acc, stage, sems):
    core = lax.axis_index("col")
    spots = plane_spots(1, False)
    loads = [
        pltpu.make_async_copy(ref, cot.at[spots[k]], sems.at[k])
        for k, ref in enumerate((c0, c1, c2, c3))
    ]
    depth = wd.shape[1] // G
    weights = [
        pltpu.make_async_copy(
            wd.at[:, pl.ds(k * depth, depth)], wds.at[:, pl.ds(k * depth, depth)], sems.at[G + k]
        )
        for k in range(G)
    ]
    start_all(weights)
    start_all(loads)
    wait_all(loads)
    for k in range(G):
        weights[k].wait()
        left = wide(core, cot, k)
        cols = slice(k * depth, (k + 1) * depth)
        term = lax.dot_general(
            left, wds[:, cols], (((1,), (1,)), ((), ())), preferred_element_type=F32
        )
        if k == 0:
            acc[...] = term
        else:
            acc[...] += term
    kept = keep_rows(core, acc, keep, sems.at[0])
    kept.start()
    sent = send_rows(core, acc, stage, send, sems.at[1])
    sent.start()
    kept.wait()
    sent.wait()


def d_act(chunks, wd):
    tok = chunks[0].shape[1]
    hid, feats = wd.shape
    return call(
        d_act_body,
        (shape((tok // 2, hid), F32), shape((tok // 2, hid))),
        (pl.ANY,) * G + (HB,),
        [
            pltpu.VMEM((G,) + chunks[0].shape, BF),
            pltpu.VMEM((hid, feats), BF),
            pltpu.VMEM((tok, hid), F32),
            pltpu.VMEM((tok // 2, hid), BF),
            pltpu.SemaphoreType.DMA((2 * G,)),
        ],
        2 * tok * feats * hid,
        2 * feats * hid,
        (HB, pl.ANY),
    )(*chunks, keep_out(wd))


TILES = 4


def hidden_body(keep, recv, keep_d, recv_d, shares, grads, ks, rs, kds, rds, res, sems):
    tile = keep_d.shape[0] // TILES
    loads, stores = [], []
    for t in range(TILES):
        at = pl.ds(t * tile, tile)
        loads.append(
            [
                pltpu.make_async_copy(keep.at[:, at], ks.at[:, at], sems.at[t, 0]),
                pltpu.make_async_copy(recv.at[:, at], rs.at[:, at], sems.at[t, 1]),
                pltpu.make_async_copy(keep_d.at[at], kds.at[at], sems.at[t, 2]),
                pltpu.make_async_copy(recv_d.at[at], rds.at[at], sems.at[t, 3]),
            ]
        )
        stores.append(
            [
                pltpu.make_async_copy(res.at[:, at], shares.at[:, at], sems.at[t, 4]),
                pltpu.make_async_copy(res.at[pl.ds(1, 2), at], grads.at[:, at], sems.at[t, 5]),
            ]
        )
    for item in loads:
        start_all(item)
    for t in range(TILES):
        wait_all(loads[t])

        @pl.loop(0, tile // 16)
        def _(i):
            rows = pl.ds(pl.multiple_of(t * tile + i * 16, 16), 16)
            gate = ks[0, rows, :] + rs[0, rows, :].astype(F32)
            up = ks[1, rows, :] + rs[1, rows, :].astype(F32)
            da = kds[rows, :] + rds[rows, :].astype(F32)
            sig = 1.0 / (1.0 + jnp.exp(-gate))
            silu = gate * sig
            res[0, rows, :] = (silu * up).astype(BF)
            res[1, rows, :] = (da * up * sig * (1.0 + gate * (1.0 - sig))).astype(BF)
            res[2, rows, :] = (da * silu).astype(BF)

        start_all(stores[t])
    for item in stores:
        wait_all(item)


def hidden(keep, recv, keep_d, recv_d):
    _, half, hid = keep.shape
    return call(
        hidden_body,
        (shape((3, half, hid)), shape((2, half, hid))),
        (HB,) * 4,
        [
            pltpu.VMEM((2, half, hid), F32),
            pltpu.VMEM((2, half, hid), BF),
            pltpu.VMEM((half, hid), F32),
            pltpu.VMEM((half, hid), BF),
            pltpu.VMEM((3, half, hid), BF),
            pltpu.SemaphoreType.DMA((TILES, 6)),
        ],
        20 * half * hid,
        24 * half * hid,
    )(keep_out(keep), keep_out(recv), keep_out(keep_d), keep_out(recv_d))


def out_body(own, other, wd, o0, o1, o2, o3, copied, act, wds, res, held, sems):
    core = lax.axis_index("col")
    half = own.shape[1]
    loads = [
        pltpu.make_async_copy(own.at[0], act.at[pl.ds(core * half, half)], sems.at[0]),
        pltpu.make_async_copy(other.at[0], act.at[pl.ds((1 - core) * half, half)], sems.at[1]),
    ]
    moved = [
        pltpu.make_async_copy(other.at[pl.ds(1, 2)], held, sems.at[2 + 2 * G]),
        pltpu.make_async_copy(held, copied, sems.at[3 + 2 * G]),
    ]
    width = wd.shape[1] // G
    weights = [
        pltpu.make_async_copy(
            wd.at[:, pl.ds(k * width, width)], wds.at[:, pl.ds(k * width, width)], sems.at[2 + k]
        )
        for k in range(G)
    ]
    start_all(loads)
    start_all(weights)
    moved[0].start()
    wait_all(loads)
    part = width // G
    for k in range(G):
        weights[k].wait()
        term = jnp.dot(
            act[...], wds[:, k * width : (k + 1) * width], preferred_element_type=F32
        ).astype(BF)
        for j in range(G):
            res[plane_at(core, k, j)] = term[:, j * part : (j + 1) * part]
    moved[0].wait()
    moved[1].start()
    spots = plane_spots(1, True)
    stores = [
        pltpu.make_async_copy(res.at[spots[k]], ref, sems.at[2 + G + k])
        for k, ref in enumerate((o0, o1, o2, o3))
    ]
    start_all(stores)
    wait_all(stores)
    moved[1].wait()


def out_parts(own, other, wd):
    _, half, hid = own.shape
    feats = wd.shape[1]
    tok = 2 * half
    part = feats // (G * G)
    return call(
        out_body,
        (shape((G, tok, part)),) * G + (shape((2, half, hid)),),
        (pl.ANY, pl.ANY, HB),
        [
            pltpu.VMEM((tok, hid), BF),
            pltpu.VMEM((hid, feats), BF),
            pltpu.VMEM((G, G, tok, part), BF),
            pltpu.VMEM((2, half, hid), BF),
            pltpu.SemaphoreType.DMA((4 + 2 * G,)),
        ],
        2 * tok * feats * hid,
        2 * feats * hid,
    )(own, other, keep_out(wd))


def d_tok_body(own, other, wg, wu, o0, o1, o2, o3, grads, wgs, wus, res, sems):
    core = lax.axis_index("col")
    half = own.shape[1]
    loads = [
        pltpu.make_async_copy(
            own.at[pl.ds(1, 2)], grads.at[:, pl.ds(core * half, half)], sems.at[0]
        ),
        pltpu.make_async_copy(
            other.at[pl.ds(1, 2)], grads.at[:, pl.ds((1 - core) * half, half)], sems.at[1]
        ),
    ]
    width = wg.shape[0] // G
    weights = []
    for k in range(G):
        rows = pl.ds(k * width, width)
        weights.append(
            [
                pltpu.make_async_copy(wg.at[rows], wgs.at[rows], sems.at[2 + 2 * k]),
                pltpu.make_async_copy(wu.at[rows], wus.at[rows], sems.at[3 + 2 * k]),
            ]
        )
    start_all(loads)
    for pair in weights:
        start_all(pair)
    wait_all(loads)
    part = width // G
    dims = (((1,), (1,)), ((), ()))
    for k in range(G):
        wait_all(weights[k])
        rows = slice(k * width, (k + 1) * width)
        term = lax.dot_general(grads[0], wgs[rows, :], dims, preferred_element_type=F32)
        term += lax.dot_general(grads[1], wus[rows, :], dims, preferred_element_type=F32)
        term = term.astype(BF)
        for j in range(G):
            res[plane_at(core, k, j)] = term[:, j * part : (j + 1) * part]
    spots = plane_spots(1, True)
    stores = [
        pltpu.make_async_copy(res.at[spots[k]], ref, sems.at[2 + 2 * G + k])
        for k, ref in enumerate((o0, o1, o2, o3))
    ]
    start_all(stores)
    wait_all(stores)


def d_tok_parts(own, other, wg, wu):
    _, half, hid = own.shape
    feats = wg.shape[0]
    tok = 2 * half
    part = feats // (G * G)
    return call(
        d_tok_body,
        (shape((G, tok, part)),) * G,
        (pl.ANY, pl.ANY, HB, HB),
        [
            pltpu.VMEM((2, tok, hid), BF),
            pltpu.VMEM((feats, hid), BF),
            pltpu.VMEM((feats, hid), BF),
            pltpu.VMEM((G, G, tok, part), BF),
            pltpu.SemaphoreType.DMA((2 + 3 * G,)),
        ],
        4 * tok * feats * hid,
        4 * feats * hid,
    )(own, other, keep_out(wg), keep_out(wu))


def down_body(own, other, c0, c1, c2, c3, b0, b1, b2, b3, act, cot, res, sems):
    _, _, core, z = here()
    half = own.shape[1]
    spots = plane_spots(1, False)
    loads = [
        pltpu.make_async_copy(own.at[0], act.at[pl.ds(core * half, half)], sems.at[0]),
        pltpu.make_async_copy(other.at[0], act.at[pl.ds((1 - core) * half, half)], sems.at[1]),
    ]
    rights = [
        pltpu.make_async_copy(ref, cot.at[spots[k]], sems.at[2 + k])
        for k, ref in enumerate((c0, c1, c2, c3))
    ]
    start_all(loads)
    start_all(rights)
    wait_all(loads)
    left = act[...].T
    wait_all(rights)
    block = res.shape[1]
    width = res.shape[2] // G
    for k in range(G):
        cols = slice(k * width, (k + 1) * width)
        term = jnp.dot(left, wide(core, cot, k), preferred_element_type=F32).astype(BF)
        for j in range(G):
            res[j, :, cols] = term[j * block : (j + 1) * block, :]
    spots = targets(z, core)
    stores = [
        pltpu.make_async_copy(res.at[spots[k]], ref, sems.at[2 + G + k])
        for k, ref in enumerate((b0, b1, b2, b3))
    ]
    start_all(stores)
    wait_all(stores)


def down_parts(own, other, chunks):
    _, half, hid = own.shape
    _, tok, part = chunks[0].shape
    feats = G * G * part
    return call(
        down_body,
        (shape((hid // G, feats)),) * G,
        (pl.ANY,) * (2 + G),
        [
            pltpu.VMEM((tok, hid), BF),
            pltpu.VMEM((G,) + chunks[0].shape, BF),
            pltpu.VMEM((G, hid // G, feats), BF),
            pltpu.SemaphoreType.DMA((2 + 2 * G,)),
        ],
        2 * tok * feats * hid,
        2 * tok * feats,
    )(own, other, *chunks)


def grads_body(t0, t1, t2, t3, p0, p1, p2, p3, p4, p5, p6, p7, gg, gu, toks, lefts, rights, sems):
    _, _, core, z = here()
    own, back, ahead, far = ring(z, core)
    half = p0.shape[1]
    feats = gg.shape[0]
    spots = [
        (own, core), (own, 1 - core),
        (back, core), (ahead, 1 - core),
        (back, 1 - core), (ahead, core),
        (far, core), (far, 1 - core),
    ]
    pieces = (p0, p1, p2, p3, p4, p5, p6, p7)
    places = ring(z, core)
    loads = [
        pltpu.make_async_copy(ref, toks.at[places[k]], sems.at[8 + k])
        for k, ref in enumerate((t0, t1, t2, t3))
    ]
    start_all(loads)
    moves = []
    for k, (group, side) in enumerate(spots):
        moves.append(
            pltpu.make_async_copy(
                pieces[k],
                rights.at[:, pl.ds(pl.multiple_of(group * 2 * half + side * half, half), half)],
                sems.at[k],
            )
        )
    start_all(moves)
    wait_all(loads)
    for group in range(G):
        lefts[:, group * 2 * half : (group + 1) * 2 * half] = jnp.concatenate(
            [toks[group, j] for j in range(G)], axis=1
        ).T
    wait_all(moves)
    rows = feats // 2
    for n, out in enumerate((gg, gu)):
        for r in range(2):
            cut = slice(r * rows, (r + 1) * rows)
            out[cut, :] = jnp.dot(
                lefts[cut, :], rights[n], preferred_element_type=F32
            ).astype(BF)


def weight_grads(chunks, pieces):
    _, half, hid = pieces[0].shape
    _, tok, part = chunks[0].shape
    feats = G * part
    return call(
        grads_body,
        (shape((feats, hid)),) * 2,
        (pl.ANY,) * 6 + (HB,) * 6,
        [
            pltpu.VMEM((G, G, tok, part), BF),
            pltpu.VMEM((feats, 2 * G * half), BF),
            pltpu.VMEM((2, 2 * G * half, hid), BF),
            pltpu.SemaphoreType.DMA((12,)),
        ],
        8 * G * half * feats * hid,
        20 * half * hid,
        (VM, VM),
        30,
    )(*chunks, *pieces[:2], *map(keep_out, pieces[2:]))


def mid_sum_body(a0, a1, a2, a3, b0, b1, b2, b3, o0, o1, o2, o3):
    spots = plane_spots(0, True)
    for k, out in enumerate((o0, o1, o2, o3)):
        at = spots[k]
        for n, (p, q, r, s) in enumerate(((a0, a1, a2, a3), (b0, b1, b2, b3))):
            total = p[at].astype(F32) + q[at].astype(F32) + (r[at].astype(F32) + s[at].astype(F32))
            out[n] = total.astype(BF)


def mid_sum(first, second):
    _, tok, part = first[0].shape
    return call(
        mid_sum_body,
        (shape((2, tok, part)),) * G,
        (VM,) * (2 * G),
        [],
        24 * tok * part,
        80 * tok * part,
        (VM,) * G,
    )(*first, *second)


def last_sum_body(p0, p1, p2, p3, out, tok):
    for n, ref in enumerate((out, tok)):
        total = p0[n].astype(F32) + p1[n].astype(F32) + (p2[n].astype(F32) + p3[n].astype(F32))
        ref[...] = total.astype(BF)


def last_sum(parts):
    _, tok, part = parts[0].shape
    return call(
        last_sum_body,
        (shape((tok, part)),) * 2,
        (VM,) * G,
        [],
        8 * tok * part,
        20 * tok * part,
        (VM, VM),
    )(*parts)


def total_body(count, *refs):
    ins, out, slots, res, sems = refs[:count], refs[count], *refs[count + 1 :]
    tile = out.shape[0] // 2
    loads, stores = [], []
    for t in range(2):
        at = pl.ds(t * tile, tile)
        loads.append(
            [
                pltpu.make_async_copy(ref.at[at], slots.at[n, at], sems.at[t, n])
                for n, ref in enumerate(ins)
            ]
        )
        stores.append(pltpu.make_async_copy(res.at[at], out.at[at], sems.at[t, count]))
    for item in loads:
        start_all(item)
    for t in range(2):
        wait_all(loads[t])

        @pl.loop(0, tile // 16)
        def _(i):
            rows = pl.ds(pl.multiple_of(t * tile + i * 16, 16), 16)
            total = slots[0, rows, :].astype(F32)
            for n in range(1, count):
                total = total + slots[n, rows, :].astype(F32)
            res[rows, :] = total.astype(BF)

        stores[t].start()
    wait_all(stores)


def total_of(parts):
    rows, cols = parts[0].shape
    count = len(parts)
    return call(
        functools.partial(total_body, count),
        (shape((rows, cols)),),
        (pl.ANY,) * count,
        [
            pltpu.VMEM((count, rows, cols), BF),
            pltpu.VMEM((rows, cols), BF),
            pltpu.SemaphoreType.DMA((2, count + 1)),
        ],
        count * rows * cols,
        2 * (count + 1) * rows * cols,
    )(*parts)[0]


def plane_gather(phase, array):
    return [array] + [plane_shift(k, array, phase) for k in (1, 2, 3)]


def local(tokens, w_gate, w_up, w_down, d_out):
    first = plane_gather(0, jnp.stack([tokens, d_out]))
    chunk_t, chunk_c = place(first)
    tok_chunks = plane_gather(1, chunk_t)
    cot_chunks = [chunk_c] + [
        plane_shift(k, after(chunk_c, tok_chunks[k]), 1) for k in (1, 2, 3)
    ]
    picked = pick(tok_chunks)
    group1, group2 = depth_shift(1, picked[1]), depth_shift(2, picked[2])

    keep_gu, send_gu = gate_up([after(tok_chunks[0], picked[0])] + tok_chunks[1:], w_gate, w_up)
    keep_d, send_d = d_act(
        [after(cot_chunks[0], keep_gu, group1)] + cot_chunks[1:], w_down
    )
    group3 = depth_shift(3, after(picked[3], group1, group2))
    recv_gu, recv_d = swap(after(send_gu, send_d)), swap(send_d)

    own, grads_own = hidden(keep_gu, recv_gu, keep_d, recv_d)
    other = swap(own)
    near_own = depth_shift(1, after(grads_own, group2))

    *outs, grads_other = out_parts(after(own, group2), other, w_down)
    blocks = down_parts(own, other, [after(cot_chunks[0], outs[0])] + cot_chunks[1:])
    near_other = depth_shift(1, after(grads_other, blocks[0], group3))
    toks = d_tok_parts(after(own, blocks[0], group3), other, w_gate, w_up)

    out_got = [plane_shift(k, outs[k], 1) for k in (1, 2, 3)]
    stage = lax.optimization_barrier((near_own, toks, out_got))
    near_own, toks, out_got = stage
    far_own = depth_shift(1, near_own)
    relay = depth_shift(1, after(blocks[3], near_other))
    tok_got = [plane_shift(k, toks[k], 1) for k in (1, 2, 3)]

    joined = total_of([blocks[1], relay])
    ahead = depth_shift(1, joined)
    back = depth_shift(2, after(blocks[2], far_own))

    middle = mid_sum([after(outs[0], joined, far_own)] + out_got, [toks[0]] + tok_got)
    last = [plane_shift(k, middle[k], 0) for k in (1, 2, 3)]
    swapped = [swap(after(item, far_own)) for item in (near_own, near_other, far_own)]

    pieces = [
        grads_own, grads_other,
        near_own, swapped[0],
        near_other, swapped[1],
        far_own, swapped[2],
    ]
    grad_gate, grad_up = weight_grads([picked[0], group1, group2, group3], pieces)
    output, d_tokens = last_sum([after(middle[0], grad_gate)] + last)
    grad_down = total_of([after(blocks[0], grad_gate), back, ahead])
    return output, d_tokens, grad_gate, grad_up, grad_down


def solution(mesh):
    placed = (
        P("depth", ("col", "row")),
        P("col", "row"),
        P("col", "row"),
        P("row", "col"),
        P("depth", ("col", "row")),
    )
    return jax.shard_map(
        local,
        mesh=mesh,
        in_specs=placed,
        out_specs=(
            P("depth", ("col", "row")),
            P("depth", ("col", "row")),
            P(("col", "depth"), "row"),
            P(("col", "depth"), "row"),
            P(("row", "depth"), "col"),
        ),
        check_vma=False,
    )
```

time: 223 us -> 159 us (0.71)
  waiting for transfers between devices: 81.8 us -> 58.9 us
  starting transfers between devices: 61.3 us -> 44.7 us
  between operations: 14.2 us -> 1.04 us
  local copies, waits for them, and re-layouts: 14.6 us -> 3.42 us
  Pallas kernels: 43 us -> 49.6 us
  other arithmetic: 5.69 us -> 0.99 us
    ppermute x25 -> x18, waiting for transfers between devices: 71 us -> 22 us  [plane_shift(): return lax.ppermute(array, ('row', 'col'), pairs)]
    ppermute x6 -> x9, waiting for transfers between devices: 7.93 us -> 34.3 us  [depth_shift(): return lax.ppermute(array, ('col', 'depth'), pairs)]
    ppermute x25 -> x18, starting transfers between devices: 44 us -> 28.3 us  [plane_shift(): return lax.ppermute(array, ('row', 'col'), pairs)]
    unnamed x38 -> x20, local copies, waits for them, and re-layouts: 14.6 us -> 3.42 us
    pallas_call x10 -> x12, Pallas kernels: 36 us -> 41.9 us  [the longest x1 8.53 us: weight_grads(): call(grads_body, (shape((feats, hid)),) * 2, (pl.ANY,) * 6 + (HB,) * 6, [...]
    convert_element_type x4 -> x0, other arithmetic: 5.69 us -> none  [total_of(): return total.astype(BF)]
    ppermute x6 -> x9, starting transfers between devices: 14.3 us -> 15.1 us  [depth_shift(): return lax.ppermute(array, ('col', 'depth'), pairs)]
  transfers between devices with their start and end apart: 39 -> 33, of which waited for: 19 -> 16; matrix products, arithmetic and copies ran while one was open for 1% -> 0% of each run, Pallas kernels for 19% -> 25%
where the time goes in v2:
time: 159 us
  waiting for transfers between devices  58.9 us (37%)
  Pallas kernels  49.6 us (31%)
  starting transfers between devices  44.7 us (28%)
  local copies, waits for them, and re-layouts  3.42 us (2%)
    ppermute x9, waiting for transfers between devices, depth_shift(): return lax.ppermute(array, ('col', 'depth'), pairs)  34.3 us
    ppermute x18, starting transfers between devices, plane_shift(): return lax.ppermute(array, ('row', 'col'), pairs)  28.3 us
    ppermute x18, waiting for transfers between devices, plane_shift(): return lax.ppermute(array, ('row', 'col'), pairs)  22 us
    ppermute x9, starting transfers between devices, depth_shift(): return lax.ppermute(array, ('col', 'depth'), pairs)  15.1 us
    pallas_call x1, Pallas kernels, weight_grads(): call(grads_body, (shape((feats, hid)),) * 2, (pl.ANY,) * 6 + (HB,) * 6, [...  8.53 us
    pallas_call x1, Pallas kernels, gate_up(): call(gate_up_body, (shape((2, tok // 2, hid), F32), shape((2, tok // 2, h...  7.7 us
    pallas_call x1, Pallas kernels, d_tok_parts(): call(d_tok_body, (shape((G, tok, part)),) * G, (pl.ANY, pl.ANY, HB, HB),...  7.12 us
    pallas_call x1, Pallas kernels, out_parts(): call(out_body, (shape((G, tok, part)),) * G + (shape((2, half, hid)),), (...  5.06 us
  transfers between devices with their start and end apart: 33, of which 16 were waited for; matrix products, arithmetic and copies ran while one was open for 0% of the time, Pallas kernels for 25%

profile of v2, /device:TPU:0, one launch (start us, length us, event | category | flops | bytes accessed | tf_op | source)
XLA Modules:
  0.0 158.7 jit_solution(5022123304010844385)
XLA Ops:
  0.6 1.0 pad_maximum_fusion.p0
  1.6 3.2 %collective-permute-start.2 = (bf16[2,512,128]{2,1,0:T(8,128)(2,1)S(1)}, bf16[2,512,128]{2,1,0:T(8,128)(2,1)S(1)}, u32[]{:S(2)}, u32[]{:S(2)}) collective-permute-start(bf16[2,512,128]{2,1,0:T(8,128)(2,1)S(1)} %pad_maximum_fusion.p0), channel_id=1, source_target_pairs={{0,16},{4,68},{8,24},{12,76},{16,0},{20,84},{24,8},{28,92},{32,48}... | collective-permute-start | bytes 786440 | tf_op jit(solution)/shard_map/ppermute | solution.py:54
  4.8 1.1 collective-permute-start.1
  6.0 0.9 collective-permute-start
  6.8 2.7 %collective-permute-done.2.p3 = bf16[2,512,128]{2,1,0:T(8,128)(2,1)S(1)} collective-permute-done((bf16[2,512,128]{2,1,0:T(8,128)(2,1)S(1)}, bf16[2,512,128]{2,1,0:T(8,128)(2,1)S(1)}, u32[]{:S(2)}, u32[]{:S(2)}) %collective-permute-start.2) | collective-permute-done | bytes 262176 | tf_op jit(solution)/shard_map/ppermute | solution.py:54
  9.6 3.0 %collective-permute-done.1.p2 = bf16[2,512,128]{2,1,0:T(8,128)(2,1)S(1)} collective-permute-done((bf16[2,512,128]{2,1,0:T(8,128)(2,1)S(1)}, bf16[2,512,128]{2,1,0:T(8,128)(2,1)S(1)}, u32[]{:S(2)}, u32[]{:S(2)}) %collective-permute-start.1) | collective-permute-done | bytes 262176 | tf_op jit(solution)/shard_map/ppermute | solution.py:54
  12.6 1.0 collective-permute-done.p1
  13.7 3.3 %collective-permute-start.5 = (bf16[4,512,128]{2,1,0:T(8,128)(2,1)S(1)}, bf16[4,512,128]{2,1,0:T(8,128)(2,1)S(1)}, u32[]{:S(2)}, u32[]{:S(2)}) collective-permute-start(bf16[4,512,128]{2,1,0:T(8,128)(2,1)S(1)} %get-tuple-element.68.c0.t0), channel_id=1, source_target_pairs={{0,64},{4,20},{8,72},{12,28},{16,80},{20,4},{24,88},{28,12},{32,96... | collective-permute-start | bytes 1572872 | tf_op jit(solution)/shard_map/ppermute | solution.py:54
  16.9 1.1 collective-permute-start.4
  18.0 1.0 collective-permute-start.3
  19.0 5.6 %collective-permute-done.5.c3.t3 = bf16[4,512,128]{2,1,0:T(8,128)(2,1)S(1)} collective-permute-done((bf16[4,512,128]{2,1,0:T(8,128)(2,1)S(1)}, bf16[4,512,128]{2,1,0:T(8,128)(2,1)S(1)}, u32[]{:S(2)}, u32[]{:S(2)}) %collective-permute-start.5) | collective-permute-done | bytes 524320 | tf_op jit(solution)/shard_map/ppermute | solution.py:54
  24.5 3.2 %collective-permute-start.9 = (bf16[4,512,128]{2,1,0:T(8,128)(2,1)S(1)}, bf16[4,512,128]{2,1,0:T(8,128)(2,1)S(1)}, u32[]{:S(2)}, u32[]{:S(2)}) collective-permute-start(bf16[4,512,128]{2,1,0:T(8,128)(2,1)S(1)} %get-tuple-element.84.c0), channel_id=1, source_target_pairs={{0,64},{4,20},{8,72},{12,28},{16,80},{20,4},{24,88},{28,12},{32,96... | collective-permute-start | bytes 1572872 | tf_op jit(solution)/shard_map/ppermute | solution.py:54
  27.7 2.7 %collective-permute-done.4.c2.t2 = bf16[4,512,128]{2,1,0:T(8,128)(2,1)S(1)} collective-permute-done((bf16[4,512,128]{2,1,0:T(8,128)(2,1)S(1)}, bf16[4,512,128]{2,1,0:T(8,128)(2,1)S(1)}, u32[]{:S(2)}, u32[]{:S(2)}) %collective-permute-start.4) | collective-permute-done | bytes 524320 | tf_op jit(solution)/shard_map/ppermute | solution.py:54
  30.4 3.4 %shard_map.93 = (bf16[4,512,128]{2,1,0:T(8,128)(2,1)S(1)}, bf16[4,512,128]{2,1,0:T(8,128)(2,1)S(1)}, bf16[4,512,128]{2,1,0:T(8,128)(2,1)S(1)}, bf16[4,512,128]{2,1,0:T(8,128)(2,1)S(1)}) custom-call(bf16[4,512,128]{2,1,0:T(8,128)(2,1)S(1)} %get-tuple-element.68.c0.t0, bf16[4,512,128]{2,1,0:T(8,128)(2,1)S(1)} %collective-permute-done.3.c1.t1, ...), custom_call_target="tpu_custom_call" | custom-call | bytes 83886 | tf_op jit(solution)/shard_map/pallas_call | solution.py:158
  33.8 2.0 %collective-permute-start.6 = (bf16[4,512,128]{2,1,0:T(8,128)(2,1)S(1)}, bf16[4,512,128]{2,1,0:T(8,128)(2,1)S(1)}, u32[]{:S(2)}, u32[]{:S(2)}) collective-permute-start(bf16[4,512,128]{2,1,0:T(8,128)(2,1)S(1)} %get-tuple-element.72), channel_id=1, source_target_pairs={{0,1},{1,2},{2,3},{3,0},{4,7},{5,4},{6,5},{7,6},{8,9},{9,10},{10,1... | collective-permute-start | bytes 1572872 | tf_op jit(solution)/shard_map/ppermute | solution.py:63
  35.8 2.6 %collective-permute-start.8 = (bf16[4,512,128]{2,1,0:T(8,128)(2,1)S(1)}, bf16[4,512,128]{2,1,0:T(8,128)(2,1)S(1)}, u32[]{:S(2)}, u32[]{:S(2)}) collective-permute-start(bf16[4,512,128]{2,1,0:T(8,128)(2,1)S(1)} %get-tuple-element.84.c0), channel_id=1, source_target_pairs={{0,96},{4,28},{8,104},{12,4},{16,112},{20,12},{24,120},{28,20},{32... | collective-permute-start | bytes 1572872 | tf_op jit(solution)/shard_map/ppermute | solution.py:54
  38.4 7.7 %shard_map.94 = (f32[2,256,896]{2,1,0:T(8,128)S(1)}, bf16[2,256,896]{2,1,0:T(8,128)(2,1)S(1)}) custom-call(bf16[4,512,128]{2,1,0:T(8,128)(2,1)S(1)} %get-tuple-element.68.c0.t0, bf16[4,512,128]{2,1,0:T(8,128)(2,1)S(1)} %collective-permute-done.3.c1.t1, bf16[4,512,128]{2,1,0:T(8,128)(2,1)S(1)} %collective-permute-done.4.c2.t2, ...), custom_call_target="tpu_custom_call" | custom-call | flops 75161928 | bytes 146800 | tf_op jit(solution)/shard_map/pallas_call | solution.py:236
  46.2 1.3 copy-done
  47.4 1.4 collective-permute-done.7.c1
  48.8 4.4 %shard_map.95 = (f32[256,896]{1,0:T(8,128)S(1)}, bf16[256,896]{1,0:T(8,128)(2,1)S(1)}) custom-call(bf16[4,512,128]{2,1,0:T(8,128)(2,1)S(1)} %get-tuple-element.84.c0, bf16[4,512,128]{2,1,0:T(8,128)(2,1)S(1)} %collective-permute-done.7.c1, bf16[4,512,128]{2,1,0:T(8,128)(2,1)S(1)} %collective-permute-done.8.c2, ...), custom_call_target="tpu_custom_call" | custom-call | flops 37580964 | bytes 73400 | tf_op jit(solution)/shard_map/pallas_call | solution.py:294
  53.3 0.9 copy-done.1
  54.7 2.6 %collective-permute-done.11.recv_d = bf16[256,896]{1,0:T(8,128)(2,1)S(1)} collective-permute-done((bf16[256,896]{1,0:T(8,128)(2,1)S(1)}, bf16[256,896]{1,0:T(8,128)(2,1)S(1)}, u32[]{:S(2)}, u32[]{:S(2)}) %collective-permute-start.11) | collective-permute-done | bytes 458784 | tf_op jit(solution)/shard_map/ppermute | solution.py:67
  58.4 3.0 %shard_map.96 = (bf16[3,256,896]{2,1,0:T(8,128)(2,1)S(1)}, bf16[2,256,896]{2,1,0:T(8,128)(2,1)S(1)}) custom-call(f32[2,256,896]{2,1,0:T(8,128)} %copy-done, bf16[2,256,896]{2,1,0:T(8,128)(2,1)} %copy-done.8, f32[256,896]{1,0:T(8,128)} %copy-done.1, bf16[256,896]{1,0:T(8,128)(2,1)} %copy-done.9), custom_call_target="tpu_custom_call" | custom-call | flops 91750 | bytes 110100 | tf_op jit(solution)/shard_map/pallas_call | solution.py:357
  61.6 2.2 %collective-permute-start.12 = (bf16[4,512,128]{2,1,0:T(8,128)(2,1)S(1)}, bf16[4,512,128]{2,1,0:T(8,128)(2,1)S(1)}, u32[]{:S(2)}, u32[]{:S(2)}) collective-permute-start(bf16[4,512,128]{2,1,0:T(8,128)(2,1)S(1)} %get-tuple-element.81), channel_id=1, source_target_pairs={{0,3},{1,0},{2,1},{3,2},{4,5},{5,6},{6,7},{7,4},{8,11},{9,8},{10,9... | collective-permute-start | bytes 1572872 | tf_op jit(solution)/shard_map/ppermute | solution.py:63
  63.8 7.0 %collective-permute-done.12.t2 = bf16[4,512,128]{2,1,0:T(8,128)(2,1)S(1)} collective-permute-done((bf16[4,512,128]{2,1,0:T(8,128)(2,1)S(1)}, bf16[4,512,128]{2,1,0:T(8,128)(2,1)S(1)}, u32[]{:S(2)}, u32[]{:S(2)}) %collective-permute-start.12) | collective-permute-done | bytes 524320 | tf_op jit(solution)/shard_map/ppermute | solution.py:63
  70.8 3.6 %collective-permute-start.14 = (bf16[4,512,128]{2,1,0:T(8,128)(2,1)S(1)}, bf16[4,512,128]{2,1,0:T(8,128)(2,1)S(1)}, u32[]{:S(2)}, u32[]{:S(2)}) collective-permute-start(bf16[4,512,128]{2,1,0:T(8,128)(2,1)S(1)} %get-tuple-element.90), channel_id=1, source_target_pairs={{0,2},{1,3},{2,0},{3,1},{4,6},{5,7},{6,4},{7,5},{8,10},{9,11},{10,... | collective-permute-start | bytes 1572872 | tf_op jit(solution)/shard_map/ppermute | solution.py:63
  75.0 5.1 %shard_map.97 = (bf16[4,512,128]{2,1,0:T(8,128)(2,1)S(1)}, bf16[4,512,128]{2,1,0:T(8,128)(2,1)S(1)}, bf16[4,512,128]{2,1,0:T(8,128)(2,1)S(1)}, bf16[4,512,128]{2,1,0:T(8,128)(2,1)S(1)}, bf16[2,256,896]{2,1,0:T(8,128)(2,1)S(1)}) custom-call(bf16[3,256,896]{2,1,0:T(8,128)(2,1)S(1)} %get-tuple-element.95.own, ...), custom_call_target="tpu_custom_call" | custom-call | flops 37580964 | bytes 73400 | tf_op jit(solution)/shard_map/pallas_call | solution.py:421
  80.1 4.1 %shard_map.98 = (bf16[224,2048]{1,0:T(8,128)(2,1)S(1)}, bf16[224,2048]{1,0:T(8,128)(2,1)S(1)}, bf16[224,2048]{1,0:T(8,128)(2,1)S(1)}, bf16[224,2048]{1,0:T(8,128)(2,1)S(1)}) custom-call(bf16[3,256,896]{2,1,0:T(8,128)(2,1)S(1)} %get-tuple-element.95.own, bf16[3,256,896]{2,1,0:T(8,128)(2,1)S(1)} %collective-permute-done.13.other, ...), custom_call_target="tpu_custom_call" | custom-call | flops 37580964 | bytes 41943 | tf_op jit(solution)/shard_map/pallas_call | solution.py:539
  84.3 2.4 %collective-permute-done.14.t3 = bf16[4,512,128]{2,1,0:T(8,128)(2,1)S(1)} collective-permute-done((bf16[4,512,128]{2,1,0:T(8,128)(2,1)S(1)}, bf16[4,512,128]{2,1,0:T(8,128)(2,1)S(1)}, u32[]{:S(2)}, u32[]{:S(2)}) %collective-permute-start.14) | collective-permute-done | bytes 524320 | tf_op jit(solution)/shard_map/ppermute | solution.py:63
  86.6 2.4 %collective-permute-start.15 = (bf16[2,256,896]{2,1,0:T(8,128)(2,1)S(1)}, bf16[2,256,896]{2,1,0:T(8,128)(2,1)S(1)}, u32[]{:S(2)}, u32[]{:S(2)}) collective-permute-start(bf16[2,256,896]{2,1,0:T(8,128)(2,1)S(1)} %get-tuple-element.91.p1), channel_id=1, source_target_pairs={{0,1},{1,2},{2,3},{3,0},{4,7},{5,4},{6,5},{7,6},{8,9},{9,10},{10,1... | collective-permute-start | bytes 2752520 | tf_op jit(solution)/shard_map/ppermute | solution.py:63
  89.0 3.2 %collective-permute-start.19 = (bf16[4,512,128]{2,1,0:T(8,128)(2,1)S(1)}, bf16[4,512,128]{2,1,0:T(8,128)(2,1)S(1)}, u32[]{:S(2)}, u32[]{:S(2)}) collective-permute-start(bf16[4,512,128]{2,1,0:T(8,128)(2,1)S(1)} %get-tuple-element.101), channel_id=1, source_target_pairs={{0,96},{4,28},{8,104},{12,4},{16,112},{20,12},{24,120},{28,20},{32... | collective-permute-start | bytes 1572872 | tf_op jit(solution)/shard_map/ppermute | solution.py:54
  92.4 7.1 %shard_map.100 = (bf16[4,512,128]{2,1,0:T(8,128)(2,1)S(1)}, bf16[4,512,128]{2,1,0:T(8,128)(2,1)S(1)}, bf16[4,512,128]{2,1,0:T(8,128)(2,1)S(1)}, bf16[4,512,128]{2,1,0:T(8,128)(2,1)S(1)}) custom-call(bf16[3,256,896]{2,1,0:T(8,128)(2,1)S(1)} %get-tuple-element.95.own, bf16[3,256,896]{2,1,0:T(8,128)(2,1)S(1)} %collective-permute-done.13.other, ...), custom_call_target="tpu_custom_call" | custom-call | flops 75161928 | bytes 146800 | tf_op jit(solution)/shard_map/pallas_call | solution.py:486
  99.5 5.1 %collective-permute-done.19.a2 = bf16[4,512,128]{2,1,0:T(8,128)(2,1)S(1)} collective-permute-done((bf16[4,512,128]{2,1,0:T(8,128)(2,1)S(1)}, bf16[4,512,128]{2,1,0:T(8,128)(2,1)S(1)}, u32[]{:S(2)}, u32[]{:S(2)}) %collective-permute-start.19) | collective-permute-done | bytes 524320 | tf_op jit(solution)/shard_map/ppermute | solution.py:54
  105.3 0.8 collective-permute-done.15.p4
  106.2 1.9 %collective-permute-start.16 = (bf16[224,2048]{1,0:T(8,128)(2,1)S(1)}, bf16[224,2048]{1,0:T(8,128)(2,1)S(1)}, u32[]{:S(2)}, u32[]{:S(2)}) collective-permute-start(bf16[224,2048]{1,0:T(8,128)(2,1)S(1)} %get-tuple-element.92), channel_id=1, source_target_pairs={{0,1},{1,2},{2,3},{3,0},{4,7},{5,4},{6,5},{7,6},{8,9},{9,10},{10,1... | collective-permute-start | bytes 2752520 | tf_op jit(solution)/shard_map/ppermute | solution.py:63
  108.1 1.4 collective-permute-start.22
  109.5 1.8 %collective-permute-start.23 = (bf16[4,512,128]{2,1,0:T(8,128)(2,1)S(1)}, bf16[4,512,128]{2,1,0:T(8,128)(2,1)S(1)}, u32[]{:S(2)}, u32[]{:S(2)}) collective-permute-start(bf16[4,512,128]{2,1,0:T(8,128)(2,1)S(1)} %get-tuple-element.110), channel_id=1, source_target_pairs={{0,96},{4,28},{8,104},{12,4},{16,112},{20,12},{24,120},{28,20},{32... | collective-permute-start | bytes 1572872 | tf_op jit(solution)/shard_map/ppermute | solution.py:54
  111.3 1.4 collective-permute-start.24
  112.7 7.0 %collective-permute-done.21.p6 = bf16[2,256,896]{2,1,0:T(8,128)(2,1)S(1)} collective-permute-done((bf16[2,256,896]{2,1,0:T(8,128)(2,1)S(1)}, bf16[2,256,896]{2,1,0:T(8,128)(2,1)S(1)}, u32[]{:S(2)}, u32[]{:S(2)}) %collective-permute-start.21) | collective-permute-done | bytes 917536 | tf_op jit(solution)/shard_map/ppermute | solution.py:63
  120.3 9.3 %collective-permute-done.16.refs_1_ = bf16[224,2048]{1,0:T(8,128)(2,1)S(1)} collective-permute-done((bf16[224,2048]{1,0:T(8,128)(2,1)S(1)}, bf16[224,2048]{1,0:T(8,128)(2,1)S(1)}, u32[]{:S(2)}, u32[]{:S(2)}) %collective-permute-start.16) | collective-permute-done | bytes 917536 | tf_op jit(solution)/shard_map/ppermute | solution.py:63
  129.6 2.0 %shard_map.99 = bf16[224,2048]{1,0:T(8,128)(2,1)S(1)} custom-call(bf16[224,2048]{1,0:T(8,128)(2,1)S(1)} %get-tuple-element.85.refs_0_, bf16[224,2048]{1,0:T(8,128)(2,1)S(1)} %collective-permute-done.16.refs_1_), custom_call_target="tpu_custom_call" | custom-call | flops 18350 | bytes 55050 | tf_op jit(solution)/shard_map/pallas_call | solution.py:692
  132.0 1.7 %collective-permute-start.32 = (bf16[224,2048]{1,0:T(8,128)(2,1)S(1)}, bf16[224,2048]{1,0:T(8,128)(2,1)S(1)}, u32[]{:S(2)}, u32[]{:S(2)}) collective-permute-start(bf16[224,2048]{1,0:T(8,128)(2,1)S(1)} %shard_map.99), channel_id=1, source_target_pairs={{0,1},{1,2},{2,3},{3,0},{4,7},{5,4},{6,5},{7,6},{8,9},{9,10},{10,1... | collective-permute-start | bytes 2752520 | tf_op jit(solution)/shard_map/ppermute | solution.py:63
  134.7 2.8 %collective-permute-start.29 = (bf16[2,512,128]{2,1,0:T(8,128)(2,1)S(1)}, bf16[2,512,128]{2,1,0:T(8,128)(2,1)S(1)}, u32[]{:S(2)}, u32[]{:S(2)}) collective-permute-start(bf16[2,512,128]{2,1,0:T(8,128)(2,1)S(1)} %get-tuple-element.119), channel_id=1, source_target_pairs={{0,24},{4,100},{8,0},{12,108},{16,8},{20,116},{24,16},{28,124},{32... | collective-permute-start | bytes 786440 | tf_op jit(solution)/shard_map/ppermute | solution.py:54
  138.4 8.5 %shard_map.102 = (bf16[512,896]{1,0:T(8,128)(2,1)}, bf16[512,896]{1,0:T(8,128)(2,1)}) custom-call(bf16[4,512,128]{2,1,0:T(8,128)(2,1)S(1)} %get-tuple-element.67.t0, bf16[4,512,128]{2,1,0:T(8,128)(2,1)S(1)} %collective-permute-done.6.t1, bf16[4,512,128]{2,1,0:T(8,128)(2,1)S(1)} %collective-permute-done.12.t2, ...), custom_call_target="tpu_custom_call" | custom-call | flops 75161928 | bytes 91750 | tf_op jit(solution)/shard_map/pallas_call | solution.py:601
  147.0 0.8 shard_map.103
  147.8 6.9 %collective-permute-done.31.refs_1_ = bf16[224,2048]{1,0:T(8,128)(2,1)S(1)} collective-permute-done((bf16[224,2048]{1,0:T(8,128)(2,1)S(1)}, bf16[224,2048]{1,0:T(8,128)(2,1)S(1)}, u32[]{:S(2)}, u32[]{:S(2)}) %collective-permute-start.31) | collective-permute-done | bytes 917536 | tf_op jit(solution)/shard_map/ppermute | solution.py:63
  154.7 0.9 collective-permute-done.32.refs_2_
  155.6 2.9 %shard_map.104 = bf16[224,2048]{1,0:T(8,128)(2,1)} custom-call(bf16[224,2048]{1,0:T(8,128)(2,1)S(1)} %get-tuple-element.124.refs_0_, bf16[224,2048]{1,0:T(8,128)(2,1)S(1)} %collective-permute-done.31.refs_1_, bf16[224,2048]{1,0:T(8,128)(2,1)S(1)} %collective-permute-done.32.refs_2_), custom_call_target="tpu_custom_call" | custom-call | flops 27525 | bytes 73400 | tf_op jit(solution)/shard_map/pallas_call | solution.py:692
  (52 shorter events, 6.4 us)
Async XLA Ops:
  1.6 8.0 %collective-permute-start.2 = (bf16[2,512,128]{2,1,0:T(8,128)(2,1)S(1)}, bf16[2,512,128]{2,1,0:T(8,128)(2,1)S(1)}, u32[]{:S(2)}, u32[]{:S(2)}) collective-permute-start(bf16[2,512,128]{2,1,0:T(8,128)(2,1)S(1)} %pad_maximum_fusion.p0), channel_id=1, source_target_pairs={{0,16},{4,68},{8,24},{12,76},{16,0},{20,84},{24,8},{28,92},{32,48}... | collective-permute-start | bytes 786440 | tf_op jit(solution)/shard_map/ppermute | solution.py:54
  4.8 7.8 %collective-permute-start.1 = (bf16[2,512,128]{2,1,0:T(8,128)(2,1)S(1)}, bf16[2,512,128]{2,1,0:T(8,128)(2,1)S(1)}, u32[]{:S(2)}, u32[]{:S(2)}) collective-permute-start(bf16[2,512,128]{2,1,0:T(8,128)(2,1)S(1)} %pad_maximum_fusion.p0), channel_id=1, source_target_pairs={{0,24},{4,100},{8,0},{12,108},{16,8},{20,116},{24,16},{28,124},{32... | collective-permute-start | bytes 786440 | tf_op jit(solution)/shard_map/ppermute | solution.py:54
  6.0 7.6 %collective-permute-start = (bf16[2,512,128]{2,1,0:T(8,128)(2,1)S(1)}, bf16[2,512,128]{2,1,0:T(8,128)(2,1)S(1)}, u32[]{:S(2)}, u32[]{:S(2)}) collective-permute-start(bf16[2,512,128]{2,1,0:T(8,128)(2,1)S(1)} %pad_maximum_fusion.p0), channel_id=1, source_target_pairs={{0,8},{4,36},{8,16},{12,44},{16,24},{20,52},{24,0},{28,60},{32,40}... | collective-permute-start | bytes 786440 | tf_op jit(solution)/shard_map/ppermute | solution.py:54
  13.7 10.9 %collective-permute-start.5 = (bf16[4,512,128]{2,1,0:T(8,128)(2,1)S(1)}, bf16[4,512,128]{2,1,0:T(8,128)(2,1)S(1)}, u32[]{:S(2)}, u32[]{:S(2)}) collective-permute-start(bf16[4,512,128]{2,1,0:T(8,128)(2,1)S(1)} %get-tuple-element.68.c0.t0), channel_id=1, source_target_pairs={{0,64},{4,20},{8,72},{12,28},{16,80},{20,4},{24,88},{28,12},{32,96... | collective-permute-start | bytes 1572872 | tf_op jit(solution)/shard_map/ppermute | solution.py:54
  16.9 13.5 %collective-permute-start.4 = (bf16[4,512,128]{2,1,0:T(8,128)(2,1)S(1)}, bf16[4,512,128]{2,1,0:T(8,128)(2,1)S(1)}, u32[]{:S(2)}, u32[]{:S(2)}) collective-permute-start(bf16[4,512,128]{2,1,0:T(8,128)(2,1)S(1)} %get-tuple-element.68.c0.t0), channel_id=1, source_target_pairs={{0,96},{4,28},{8,104},{12,4},{16,112},{20,12},{24,120},{28,20},{32... | collective-permute-start | bytes 1572872 | tf_op jit(solution)/shard_map/ppermute | solution.py:54
  18.0 12.4 %collective-permute-start.3 = (bf16[4,512,128]{2,1,0:T(8,128)(2,1)S(1)}, bf16[4,512,128]{2,1,0:T(8,128)(2,1)S(1)}, u32[]{:S(2)}, u32[]{:S(2)}) collective-permute-start(bf16[4,512,128]{2,1,0:T(8,128)(2,1)S(1)} %get-tuple-element.68.c0.t0), channel_id=1, source_target_pairs={{0,32},{4,12},{8,40},{12,20},{16,48},{20,28},{24,56},{28,4},{32,64... | collective-permute-start | bytes 1572872 | tf_op jit(solution)/shard_map/ppermute | solution.py:54
  24.5 22.9 %collective-permute-start.9 = (bf16[4,512,128]{2,1,0:T(8,128)(2,1)S(1)}, bf16[4,512,128]{2,1,0:T(8,128)(2,1)S(1)}, u32[]{:S(2)}, u32[]{:S(2)}) collective-permute-start(bf16[4,512,128]{2,1,0:T(8,128)(2,1)S(1)} %get-tuple-element.84.c0), channel_id=1, source_target_pairs={{0,64},{4,20},{8,72},{12,28},{16,80},{20,4},{24,88},{28,12},{32,96... | collective-permute-start | bytes 1572872 | tf_op jit(solution)/shard_map/ppermute | solution.py:54
  33.8 13.6 %collective-permute-start.6 = (bf16[4,512,128]{2,1,0:T(8,128)(2,1)S(1)}, bf16[4,512,128]{2,1,0:T(8,128)(2,1)S(1)}, u32[]{:S(2)}, u32[]{:S(2)}) collective-permute-start(bf16[4,512,128]{2,1,0:T(8,128)(2,1)S(1)} %get-tuple-element.72), channel_id=1, source_target_pairs={{0,1},{1,2},{2,3},{3,0},{4,7},{5,4},{6,5},{7,6},{8,9},{9,10},{10,1... | collective-permute-start | bytes 1572872 | tf_op jit(solution)/shard_map/ppermute | solution.py:63
  35.8 11.6 %collective-permute-start.8 = (bf16[4,512,128]{2,1,0:T(8,128)(2,1)S(1)}, bf16[4,512,128]{2,1,0:T(8,128)(2,1)S(1)}, u32[]{:S(2)}, u32[]{:S(2)}) collective-permute-start(bf16[4,512,128]{2,1,0:T(8,128)(2,1)S(1)} %get-tuple-element.84.c0), channel_id=1, source_target_pairs={{0,96},{4,28},{8,104},{12,4},{16,112},{20,12},{24,120},{28,20},{32... | collective-permute-start | bytes 1572872 | tf_op jit(solution)/shard_map/ppermute | solution.py:54
  38.4 10.4 %collective-permute-start.7 = (bf16[4,512,128]{2,1,0:T(8,128)(2,1)S(1)}, bf16[4,512,128]{2,1,0:T(8,128)(2,1)S(1)}, u32[]{:S(2)}, u32[]{:S(2)}) collective-permute-start(bf16[4,512,128]{2,1,0:T(8,128)(2,1)S(1)} %get-tuple-element.84.c0), channel_id=1, source_target_pairs={{0,32},{4,12},{8,40},{12,20},{16,48},{20,28},{24,56},{28,4},{32,64... | collective-permute-start | bytes 1572872 | tf_op jit(solution)/shard_map/ppermute | solution.py:54
  46.2 1.3 copy-start
  53.3 0.9 copy-start.1
  54.2 3.1 %collective-permute-start.10 = (bf16[2,256,896]{2,1,0:T(8,128)(2,1)S(1)}, bf16[2,256,896]{2,1,0:T(8,128)(2,1)S(1)}, u32[]{:S(2)}, u32[]{:S(2)}) collective-permute-start(bf16[2,256,896]{2,1,0:T(8,128)(2,1)S(1)} %get-tuple-element.78), channel_id=1, source_target_pairs={{0,4},{4,0},{1,5},{5,1},{2,6},{6,2},{3,7},{7,3},{8,12},{12,8},{9,1... | collective-permute-start | bytes 2752520 | tf_op jit(solution)/shard_map/ppermute | solution.py:67
  54.2 3.1 %collective-permute-start.11 = (bf16[256,896]{1,0:T(8,128)(2,1)S(1)}, bf16[256,896]{1,0:T(8,128)(2,1)S(1)}, u32[]{:S(2)}, u32[]{:S(2)}) collective-permute-start(bf16[256,896]{1,0:T(8,128)(2,1)S(1)} %get-tuple-element.77), channel_id=1, source_target_pairs={{0,4},{4,0},{1,5},{5,1},{2,6},{6,2},{3,7},{7,3},{8,12},{12,8},{9,1... | collective-permute-start | bytes 1376264 | tf_op jit(solution)/shard_map/ppermute | solution.py:67
  57.3 0.8 copy-start.9
  57.3 1.1 copy-start.8
  61.4 13.7 %collective-permute-start.13 = (bf16[3,256,896]{2,1,0:T(8,128)(2,1)S(1)}, bf16[3,256,896]{2,1,0:T(8,128)(2,1)S(1)}, u32[]{:S(2)}, u32[]{:S(2)}) collective-permute-start(bf16[3,256,896]{2,1,0:T(8,128)(2,1)S(1)} %get-tuple-element.95.own), channel_id=1, source_target_pairs={{0,4},{4,0},{1,5},{5,1},{2,6},{6,2},{3,7},{7,3},{8,12},{12,8},{9,1... | collective-permute-start | bytes 4128776 | tf_op jit(solution)/shard_map/ppermute | solution.py:67
  61.6 9.2 %collective-permute-start.12 = (bf16[4,512,128]{2,1,0:T(8,128)(2,1)S(1)}, bf16[4,512,128]{2,1,0:T(8,128)(2,1)S(1)}, u32[]{:S(2)}, u32[]{:S(2)}) collective-permute-start(bf16[4,512,128]{2,1,0:T(8,128)(2,1)S(1)} %get-tuple-element.81), channel_id=1, source_target_pairs={{0,3},{1,0},{2,1},{3,2},{4,5},{5,6},{6,7},{7,4},{8,11},{9,8},{10,9... | collective-permute-start | bytes 1572872 | tf_op jit(solution)/shard_map/ppermute | solution.py:63
  70.8 15.9 %collective-permute-start.14 = (bf16[4,512,128]{2,1,0:T(8,128)(2,1)S(1)}, bf16[4,512,128]{2,1,0:T(8,128)(2,1)S(1)}, u32[]{:S(2)}, u32[]{:S(2)}) collective-permute-start(bf16[4,512,128]{2,1,0:T(8,128)(2,1)S(1)} %get-tuple-element.90), channel_id=1, source_target_pairs={{0,2},{1,3},{2,0},{3,1},{4,6},{5,7},{6,4},{7,5},{8,10},{9,11},{10,... | collective-permute-start | bytes 1572872 | tf_op jit(solution)/shard_map/ppermute | solution.py:63
  74.3 25.2 %collective-permute-start.17 = (bf16[2,256,896]{2,1,0:T(8,128)(2,1)S(1)}, bf16[2,256,896]{2,1,0:T(8,128)(2,1)S(1)}, u32[]{:S(2)}, u32[]{:S(2)}) collective-permute-start(bf16[2,256,896]{2,1,0:T(8,128)(2,1)S(1)} %get-tuple-element.94.p0), channel_id=1, source_target_pairs={{0,1},{1,2},{2,3},{3,0},{4,7},{5,4},{6,5},{7,6},{8,9},{9,10},{10,1... | collective-permute-start | bytes 2752520 | tf_op jit(solution)/shard_map/ppermute | solution.py:63
  86.6 19.6 %collective-permute-start.15 = (bf16[2,256,896]{2,1,0:T(8,128)(2,1)S(1)}, bf16[2,256,896]{2,1,0:T(8,128)(2,1)S(1)}, u32[]{:S(2)}, u32[]{:S(2)}) collective-permute-start(bf16[2,256,896]{2,1,0:T(8,128)(2,1)S(1)} %get-tuple-element.91.p1), channel_id=1, source_target_pairs={{0,1},{1,2},{2,3},{3,0},{4,7},{5,4},{6,5},{7,6},{8,9},{9,10},{10,1... | collective-permute-start | bytes 2752520 | tf_op jit(solution)/shard_map/ppermute | solution.py:63
  89.0 10.5 %collective-permute-start.18 = (bf16[4,512,128]{2,1,0:T(8,128)(2,1)S(1)}, bf16[4,512,128]{2,1,0:T(8,128)(2,1)S(1)}, u32[]{:S(2)}, u32[]{:S(2)}) collective-permute-start(bf16[4,512,128]{2,1,0:T(8,128)(2,1)S(1)} %get-tuple-element.100), channel_id=1, source_target_pairs={{0,32},{4,12},{8,40},{12,20},{16,48},{20,28},{24,56},{28,4},{32,64... | collective-permute-start | bytes 1572872 | tf_op jit(solution)/shard_map/ppermute | solution.py:54
  89.0 15.6 %collective-permute-start.19 = (bf16[4,512,128]{2,1,0:T(8,128)(2,1)S(1)}, bf16[4,512,128]{2,1,0:T(8,128)(2,1)S(1)}, u32[]{:S(2)}, u32[]{:S(2)}) collective-permute-start(bf16[4,512,128]{2,1,0:T(8,128)(2,1)S(1)} %get-tuple-element.101), channel_id=1, source_target_pairs={{0,96},{4,28},{8,104},{12,4},{16,112},{20,12},{24,120},{28,20},{32... | collective-permute-start | bytes 1572872 | tf_op jit(solution)/shard_map/ppermute | solution.py:54
  92.3 12.9 %collective-permute-start.20 = (bf16[4,512,128]{2,1,0:T(8,128)(2,1)S(1)}, bf16[4,512,128]{2,1,0:T(8,128)(2,1)S(1)}, u32[]{:S(2)}, u32[]{:S(2)}) collective-permute-start(bf16[4,512,128]{2,1,0:T(8,128)(2,1)S(1)} %get-tuple-element.102), channel_id=1, source_target_pairs={{0,64},{4,20},{8,72},{12,28},{16,80},{20,4},{24,88},{28,12},{32,96... | collective-permute-start | bytes 1572872 | tf_op jit(solution)/shard_map/ppermute | solution.py:54
  99.5 38.8 %copy-start.2 = (bf16[2,256,896]{2,1,0:T(8,128)(2,1)}, bf16[2,256,896]{2,1,0:T(8,128)(2,1)S(1)}, u32[]{:S(2)}) copy-start(bf16[2,256,896]{2,1,0:T(8,128)(2,1)S(1)} %collective-permute-done.17.p2) | copy-start | bytes 2752516
  105.1 14.6 %collective-permute-start.21 = (bf16[2,256,896]{2,1,0:T(8,128)(2,1)S(1)}, bf16[2,256,896]{2,1,0:T(8,128)(2,1)S(1)}, u32[]{:S(2)}, u32[]{:S(2)}) collective-permute-start(bf16[2,256,896]{2,1,0:T(8,128)(2,1)S(1)} %collective-permute-done.17.p2), channel_id=1, source_target_pairs={{0,1},{1,2},{2,3},{3,0},{4,7},{5,4},{6,5},{7,6},{8,9},{9,10},{10,1... | collective-permute-start | bytes 2752520 | tf_op jit(solution)/shard_map/ppermute | solution.py:63
  106.2 32.1 %copy-start.3 = (bf16[2,256,896]{2,1,0:T(8,128)(2,1)}, bf16[2,256,896]{2,1,0:T(8,128)(2,1)S(1)}, u32[]{:S(2)}) copy-start(bf16[2,256,896]{2,1,0:T(8,128)(2,1)S(1)} %collective-permute-done.15.p4) | copy-start | bytes 2752516
  106.2 23.4 %collective-permute-start.16 = (bf16[224,2048]{1,0:T(8,128)(2,1)S(1)}, bf16[224,2048]{1,0:T(8,128)(2,1)S(1)}, u32[]{:S(2)}, u32[]{:S(2)}) collective-permute-start(bf16[224,2048]{1,0:T(8,128)(2,1)S(1)} %get-tuple-element.92), channel_id=1, source_target_pairs={{0,1},{1,2},{2,3},{3,0},{4,7},{5,4},{6,5},{7,6},{8,9},{9,10},{10,1... | collective-permute-start | bytes 2752520 | tf_op jit(solution)/shard_map/ppermute | solution.py:63
  108.1 11.6 %collective-permute-start.22 = (bf16[4,512,128]{2,1,0:T(8,128)(2,1)S(1)}, bf16[4,512,128]{2,1,0:T(8,128)(2,1)S(1)}, u32[]{:S(2)}, u32[]{:S(2)}) collective-permute-start(bf16[4,512,128]{2,1,0:T(8,128)(2,1)S(1)} %get-tuple-element.109), channel_id=1, source_target_pairs={{0,32},{4,12},{8,40},{12,20},{16,48},{20,28},{24,56},{28,4},{32,64... | collective-permute-start | bytes 1572872 | tf_op jit(solution)/shard_map/ppermute | solution.py:54
  109.5 22.0 %collective-permute-start.23 = (bf16[4,512,128]{2,1,0:T(8,128)(2,1)S(1)}, bf16[4,512,128]{2,1,0:T(8,128)(2,1)S(1)}, u32[]{:S(2)}, u32[]{:S(2)}) collective-permute-start(bf16[4,512,128]{2,1,0:T(8,128)(2,1)S(1)} %get-tuple-element.110), channel_id=1, source_target_pairs={{0,96},{4,28},{8,104},{12,4},{16,112},{20,12},{24,120},{28,20},{32... | collective-permute-start | bytes 1572872 | tf_op jit(solution)/shard_map/ppermute | solution.py:54
  111.3 20.6 %collective-permute-start.24 = (bf16[4,512,128]{2,1,0:T(8,128)(2,1)S(1)}, bf16[4,512,128]{2,1,0:T(8,128)(2,1)S(1)}, u32[]{:S(2)}, u32[]{:S(2)}) collective-permute-start(bf16[4,512,128]{2,1,0:T(8,128)(2,1)S(1)} %get-tuple-element.111), channel_id=1, source_target_pairs={{0,64},{4,20},{8,72},{12,28},{16,80},{20,4},{24,88},{28,12},{32,96... | collective-permute-start | bytes 1572872 | tf_op jit(solution)/shard_map/ppermute | solution.py:54
  119.7 18.5 %copy-start.4 = (bf16[2,256,896]{2,1,0:T(8,128)(2,1)}, bf16[2,256,896]{2,1,0:T(8,128)(2,1)S(1)}, u32[]{:S(2)}) copy-start(bf16[2,256,896]{2,1,0:T(8,128)(2,1)S(1)} %collective-permute-done.21.p6) | copy-start | bytes 2752516
  119.7 14.4 %collective-permute-start.25 = (bf16[2,256,896]{2,1,0:T(8,128)(2,1)S(1)}, bf16[2,256,896]{2,1,0:T(8,128)(2,1)S(1)}, u32[]{:S(2)}, u32[]{:S(2)}) collective-permute-start(bf16[2,256,896]{2,1,0:T(8,128)(2,1)S(1)} %collective-permute-done.17.p2), channel_id=1, source_target_pairs={{0,4},{4,0},{1,5},{5,1},{2,6},{6,2},{3,7},{7,3},{8,12},{12,8},{9,1... | collective-permute-start | bytes 2752520 | tf_op jit(solution)/shard_map/ppermute | solution.py:67
  119.7 15.0 %collective-permute-start.26 = (bf16[2,256,896]{2,1,0:T(8,128)(2,1)S(1)}, bf16[2,256,896]{2,1,0:T(8,128)(2,1)S(1)}, u32[]{:S(2)}, u32[]{:S(2)}) collective-permute-start(bf16[2,256,896]{2,1,0:T(8,128)(2,1)S(1)} %collective-permute-done.15.p4), channel_id=1, source_target_pairs={{0,4},{4,0},{1,5},{5,1},{2,6},{6,2},{3,7},{7,3},{8,12},{12,8},{9,1... | collective-permute-start | bytes 2752520 | tf_op jit(solution)/shard_map/ppermute | solution.py:67
  129.6 7.9 %collective-permute-start.27 = (bf16[2,256,896]{2,1,0:T(8,128)(2,1)S(1)}, bf16[2,256,896]{2,1,0:T(8,128)(2,1)S(1)}, u32[]{:S(2)}, u32[]{:S(2)}) collective-permute-start(bf16[2,256,896]{2,1,0:T(8,128)(2,1)S(1)} %collective-permute-done.21.p6), channel_id=1, source_target_pairs={{0,4},{4,0},{1,5},{5,1},{2,6},{6,2},{3,7},{7,3},{8,12},{12,8},{9,1... | collective-permute-start | bytes 2752520 | tf_op jit(solution)/shard_map/ppermute | solution.py:67
  131.6 23.1 %collective-permute-start.31 = (bf16[224,2048]{1,0:T(8,128)(2,1)S(1)}, bf16[224,2048]{1,0:T(8,128)(2,1)S(1)}, u32[]{:S(2)}, u32[]{:S(2)}) collective-permute-start(bf16[224,2048]{1,0:T(8,128)(2,1)S(1)} %get-tuple-element.126), channel_id=1, source_target_pairs={{0,3},{1,0},{2,1},{3,2},{4,5},{5,6},{6,7},{7,4},{8,11},{9,8},{10,9... | collective-permute-start | bytes 2752520 | tf_op jit(solution)/shard_map/ppermute | solution.py:63
  132.0 23.6 %collective-permute-start.32 = (bf16[224,2048]{1,0:T(8,128)(2,1)S(1)}, bf16[224,2048]{1,0:T(8,128)(2,1)S(1)}, u32[]{:S(2)}, u32[]{:S(2)}) collective-permute-start(bf16[224,2048]{1,0:T(8,128)(2,1)S(1)} %shard_map.99), channel_id=1, source_target_pairs={{0,1},{1,2},{2,3},{3,0},{4,7},{5,4},{6,5},{7,6},{8,9},{9,10},{10,1... | collective-permute-start | bytes 2752520 | tf_op jit(solution)/shard_map/ppermute | solution.py:63
  134.2 4.1 %copy-start.5 = (bf16[2,256,896]{2,1,0:T(8,128)(2,1)}, bf16[2,256,896]{2,1,0:T(8,128)(2,1)S(1)}, u32[]{:S(2)}) copy-start(bf16[2,256,896]{2,1,0:T(8,128)(2,1)S(1)} %collective-permute-done.25.p3) | copy-start | bytes 2752516
  134.2 12.8 %collective-permute-start.28 = (bf16[2,512,128]{2,1,0:T(8,128)(2,1)S(1)}, bf16[2,512,128]{2,1,0:T(8,128)(2,1)S(1)}, u32[]{:S(2)}, u32[]{:S(2)}) collective-permute-start(bf16[2,512,128]{2,1,0:T(8,128)(2,1)S(1)} %get-tuple-element.118), channel_id=1, source_target_pairs={{0,8},{4,36},{8,16},{12,44},{16,24},{20,52},{24,0},{28,60},{32,40}... | collective-permute-start | bytes 786440 | tf_op jit(solution)/shard_map/ppermute | solution.py:54
  134.7 3.5 %copy-start.6 = (bf16[2,256,896]{2,1,0:T(8,128)(2,1)}, bf16[2,256,896]{2,1,0:T(8,128)(2,1)S(1)}, u32[]{:S(2)}) copy-start(bf16[2,256,896]{2,1,0:T(8,128)(2,1)S(1)} %collective-permute-done.26.p5) | copy-start | bytes 2752516
  134.7 12.2 %collective-permute-start.29 = (bf16[2,512,128]{2,1,0:T(8,128)(2,1)S(1)}, bf16[2,512,128]{2,1,0:T(8,128)(2,1)S(1)}, u32[]{:S(2)}, u32[]{:S(2)}) collective-permute-start(bf16[2,512,128]{2,1,0:T(8,128)(2,1)S(1)} %get-tuple-element.119), channel_id=1, source_target_pairs={{0,24},{4,100},{8,0},{12,108},{16,8},{20,116},{24,16},{28,124},{32... | collective-permute-start | bytes 786440 | tf_op jit(solution)/shard_map/ppermute | solution.py:54
  137.5 0.9 copy-start.7
  137.5 9.5 %collective-permute-start.30 = (bf16[2,512,128]{2,1,0:T(8,128)(2,1)S(1)}, bf16[2,512,128]{2,1,0:T(8,128)(2,1)S(1)}, u32[]{:S(2)}, u32[]{:S(2)}) collective-permute-start(bf16[2,512,128]{2,1,0:T(8,128)(2,1)S(1)} %get-tuple-element.120), channel_id=1, source_target_pairs={{0,16},{4,68},{8,24},{12,76},{16,0},{20,84},{24,8},{28,92},{32,48}... | collective-permute-start | bytes 786440 | tf_op jit(solution)/shard_map/ppermute | solution.py:54

commit v3 on v2

v3 whole, which is shorter than its diff:
```python
import functools

import jax
import jax.numpy as jnp
from jax import lax
from jax.experimental import pallas as pl
from jax.experimental.pallas import tpu as pltpu
from jax.sharding import PartitionSpec as P

BF = jnp.bfloat16
F32 = jnp.float32
G = 4
MIB = 1024 * 1024
VM = pltpu.VMEM
HB = pltpu.HBM


def here():
    row = lax.axis_index("row")
    return row // G, row % G, lax.axis_index("col"), lax.axis_index("depth")


def plane_spots(phase, outgoing):
    y, x, core, _ = here()
    pos = jnp.where(core == phase, x, y)
    ahead, back, far = (pos + 1) % G, (pos + G - 1) % G, (pos + 2) % G
    return [pos, ahead, back, far] if outgoing else [pos, back, ahead, far]


def plane_at(core, k, j):
    return jnp.where(core == 0, k, j), jnp.where(core == 0, j, k)


def ring(pos, core):
    step = 1 - 2 * core
    return [pos, (pos - step + G) % G, (pos + step + G) % G, (pos + 2) % G]


def targets(pos, core):
    own, back, ahead, far = ring(pos, core)
    return [own, ahead, back, far]


def plane_shift(kind, array, phase):
    step = {1: 1, 2: G - 1, 3: 2}[kind]
    pairs = []
    for y in range(G):
        for x in range(G):
            for core in range(2):
                along_x = (core == 0) == (phase == 0)
                to_y = y if along_x else (y + step) % G
                to_x = (x + step) % G if along_x else x
                pairs.append(((y * G + x) * 2 + core, (to_y * G + to_x) * 2 + core))
    return lax.ppermute(array, ("row", "col"), pairs)


def depth_shift(kind, array):
    pairs = []
    for core in range(2):
        for z in range(G):
            step = {1: 1 - 2 * core, 2: 2 * core - 1, 3: 2}[kind]
            pairs.append((core * G + z, core * G + (z + step) % G))
    return lax.ppermute(array, ("col", "depth"), pairs)


def swap(array):
    return lax.ppermute(array, "col", [(0, 1), (1, 0)])


def after(array, *others):
    return lax.optimization_barrier((array,) + others)[0]


def spec(space):
    return pl.BlockSpec(memory_space=space)


def keep_out(array):
    return pltpu.with_memory_space_constraint(array, HB)


COST = 50


def call(body, outs, ins, scratch, flops, nbytes, out_spaces=None, limit=24):
    if out_spaces is None:
        out_spaces = (pl.ANY,) * len(outs)
    return pl.pallas_call(
        body,
        out_shape=outs,
        in_specs=[spec(space) for space in ins],
        out_specs=tuple(spec(space) for space in out_spaces),
        scratch_shapes=scratch,
        compiler_params=pltpu.CompilerParams(vmem_limit_bytes=limit * MIB),
        cost_estimate=pl.CostEstimate(
            flops=flops // COST, bytes_accessed=nbytes // COST, transcendentals=0
        ),
    )


def shape(dims, dtype=BF):
    return jax.ShapeDtypeStruct(dims, dtype)


def start_all(copies):
    for item in copies:
        item.start()


def wait_all(copies):
    for item in copies:
        item.wait()


def place_body(p0, p1, p2, p3, tok, cot):
    spots = plane_spots(0, False)
    for k, ref in enumerate((p0, p1, p2, p3)):
        tok[spots[k]] = ref[0]
        cot[spots[k]] = ref[1]


def place(parts):
    _, tok, feat = parts[0].shape
    return call(
        place_body,
        (shape((G, tok, feat)), shape((G, tok, feat))),
        (VM,) * G,
        [],
        0,
        G * tok * feat * 8,
        (VM, VM),
    )(*parts)


def pick_body(c0, c1, c2, c3, o0, o1, o2, o3, sems):
    y, _, core, z = here()
    ins, outs = (c0, c1, c2, c3), (o0, o1, o2, o3)
    gap = (y - z + G) % G
    came, goes = (0, -1, 1, 2), (0, 1, -1, 2)
    for d in range(G):

        @pl.when((core == 0) & (gap == d))
        def _(d=d):
            copies = []
            for m in range(G):
                k = next(k for k in range(G) if (d + came[k] - goes[m]) % G == 0)
                copies.append(pltpu.make_async_copy(ins[k], outs[m], sems.at[m]))
            start_all(copies)
            wait_all(copies)

    @pl.when(core == 1)
    def _():
        spots = plane_spots(1, False)
        groups = targets(z, core)
        copies = [
            pltpu.make_async_copy(ins[k].at[groups[m]], outs[m].at[spots[k]], sems.at[G + m * G + k])
            for m in range(G)
            for k in range(G)
        ]
        start_all(copies)
        wait_all(copies)


def pick(chunks):
    _, tok, part = chunks[0].shape
    return call(
        pick_body,
        (shape((G, tok, part)),) * G,
        (pl.ANY,) * G,
        [pltpu.SemaphoreType.DMA((G + G * G,))],
        0,
        4 * G * G * tok * part,
        limit=16,
    )(*chunks)


def wide(ref):
    return jnp.concatenate([ref[j] for j in range(G)], axis=1)


def feature(core, spot, j, part):
    at = jnp.where(core == 0, spot * G + j, j * G + spot) * part
    return pl.ds(pl.multiple_of(at, part), part)


def slot_loads(source, target, sems, axis):
    core = lax.axis_index("col")
    spots = plane_spots(1, False)
    part = source.shape[axis] // (G * G)
    copies = []
    for k in range(G):
        row = []
        for j in range(G):
            src, dst = feature(core, spots[k], j, part), pl.ds((k * G + j) * part, part)
            if axis == 0:
                pair = source.at[src], target.at[dst]
            else:
                pair = source.at[:, src], target.at[:, dst]
            row.append(pltpu.make_async_copy(*pair, sems.at[k, j]))
        copies.append(row)
    return copies


def in_order(core, own, other):
    first = jnp.where(core == 0, own, other)
    second = jnp.where(core == 0, other, own)
    return jnp.concatenate([first, second], axis=0)


def keep_rows(core, acc, keep, sem):
    half = keep.shape[0]
    return pltpu.make_async_copy(
        acc.at[pl.ds(pl.multiple_of(core * half, half), half), :], keep, sem
    )


def send_rows(core, acc, stage, send, sem):
    half = send.shape[0]
    stage[...] = acc[pl.ds(pl.multiple_of((1 - core) * half, half), half), :].astype(BF)
    return pltpu.make_async_copy(stage, send, sem)


def weights_body(wg, wu, wd, wgs, wus, wds, w_sems):
    loads = [
        slot_loads(wg, wgs, w_sems.at[0], 0),
        slot_loads(wu, wus, w_sems.at[1], 0),
        slot_loads(wd, wds, w_sems.at[2], 1),
    ]
    for item in loads:
        for row in item:
            start_all(row)
    for item in loads:
        for row in item:
            wait_all(row)


def slot_weights(wg, wu, wd):
    return call(
        weights_body,
        (shape(wg.shape), shape(wu.shape), shape(wd.shape)),
        (HB,) * 3,
        [pltpu.SemaphoreType.DMA((3, G, G))],
        0,
        12 * wg.shape[0] * wg.shape[1],
        (VM,) * 3,
        limit=16,
    )(keep_out(wg), keep_out(wu), keep_out(wd))


def gate_up_body(t0, t1, t2, t3, wg, wu, keep, send, acc_g, acc_u, stage, sems):
    core = lax.axis_index("col")
    depth = wg.shape[0] // G
    for k, ref in enumerate((t0, t1, t2, t3)):
        left = wide(ref)
        rows = slice(k * depth, (k + 1) * depth)
        for acc, ws in ((acc_g, wg), (acc_u, wu)):
            term = jnp.dot(left, ws[rows, :], preferred_element_type=F32)
            if k == 0:
                acc[...] = term
            else:
                acc[...] += term
    kept = [
        keep_rows(core, acc_g, keep.at[0], sems.at[0]),
        keep_rows(core, acc_u, keep.at[1], sems.at[1]),
    ]
    start_all(kept)
    for n, acc in enumerate((acc_g, acc_u)):
        sent = send_rows(core, acc, stage.at[n], send.at[n], sems.at[2 + n])
        sent.start()
        kept.append(sent)
    wait_all(kept)


def gate_up(chunks, wg, wu):
    tok = chunks[0].shape[1]
    feats, hid = wg.shape
    return call(
        gate_up_body,
        (shape((2, tok // 2, hid), F32), shape((2, tok // 2, hid))),
        (VM,) * (G + 2),
        [
            pltpu.VMEM((tok, hid), F32),
            pltpu.VMEM((tok, hid), F32),
            pltpu.VMEM((2, tok // 2, hid), BF),
            pltpu.SemaphoreType.DMA((4,)),
        ],
        4 * tok * feats * hid,
        4 * feats * hid,
    )(*chunks, wg, wu)


def d_act_body(c0, c1, c2, c3, wd, earlier, keep, send, acc, sems):
    core = lax.axis_index("col")
    depth = wd.shape[1] // G
    send[:2] = earlier[...]
    for k, ref in enumerate((c0, c1, c2, c3)):
        cols = slice(k * depth, (k + 1) * depth)
        term = lax.dot_general(
            wide(ref), wd[:, cols], (((1,), (1,)), ((), ())), preferred_element_type=F32
        )
        if k == 0:
            acc[...] = term
        else:
            acc[...] += term
    kept = keep_rows(core, acc, keep, sems.at[0])
    kept.start()
    half = send.shape[1]
    send[2] = acc[pl.ds(pl.multiple_of((1 - core) * half, half), half), :].astype(BF)
    kept.wait()


def d_act(chunks, wd, earlier):
    tok = chunks[0].shape[1]
    hid, feats = wd.shape
    return call(
        d_act_body,
        (shape((tok // 2, hid), F32), shape((3, tok // 2, hid))),
        (VM,) * (G + 2),
        [
            pltpu.VMEM((tok, hid), F32),
            pltpu.SemaphoreType.DMA((1,)),
        ],
        2 * tok * feats * hid,
        2 * feats * hid,
        (pl.ANY, VM),
    )(*chunks, wd, earlier)


def hidden_body(keep, keep_d, recv, shares, grads):
    @pl.loop(0, keep_d.shape[0] // 16)
    def _(i):
        rows = pl.ds(pl.multiple_of(i * 16, 16), 16)
        gate = keep[0, rows, :] + recv[0, rows, :].astype(F32)
        up = keep[1, rows, :] + recv[1, rows, :].astype(F32)
        da = keep_d[rows, :] + recv[2, rows, :].astype(F32)
        sig = 1.0 / (1.0 + jnp.exp(-gate))
        silu = gate * sig
        shares[0, rows, :] = (silu * up).astype(BF)
        dg = (da * up * sig * (1.0 + gate * (1.0 - sig))).astype(BF)
        du = (da * silu).astype(BF)
        shares[1, rows, :] = dg
        shares[2, rows, :] = du
        grads[0, rows, :] = dg
        grads[1, rows, :] = du


def hidden(keep, keep_d, recv):
    _, half, hid = keep.shape
    return call(
        hidden_body,
        (shape((3, half, hid)), shape((2, half, hid))),
        (VM,) * 3,
        [],
        20 * half * hid,
        24 * half * hid,
        (VM, VM),
        limit=16,
    )(keep, keep_d, recv)


OUTGOING = (0, 2, 1, 3)


def out_body(own, other, wd, o0, o1, o2, o3, copied, act):
    core = lax.axis_index("col")
    act[...] = in_order(core, own[0], other[0])
    copied[...] = other[1:]
    width = wd.shape[1] // G
    part = width // G
    for k, ref in zip(OUTGOING, (o0, o1, o2, o3)):
        term = jnp.dot(
            act[...], wd[:, k * width : (k + 1) * width], preferred_element_type=F32
        ).astype(BF)
        for j in range(G):
            ref[j] = term[:, j * part : (j + 1) * part]


def out_parts(own, other, wd):
    _, half, hid = own.shape
    feats = wd.shape[1]
    tok = 2 * half
    part = feats // (G * G)
    return call(
        out_body,
        (shape((G, tok, part)),) * G + (shape((2, half, hid)),),
        (VM,) * 3,
        [pltpu.VMEM((tok, hid), BF)],
        2 * tok * feats * hid,
        2 * feats * hid,
        (VM,) * 5,
    )(own, other, wd)


def d_tok_body(own, other, wg, wu, o0, o1, o2, o3, grads):
    core = lax.axis_index("col")
    for n in range(2):
        grads[n] = in_order(core, own[1 + n], other[1 + n])
    width = wg.shape[0] // G
    part = width // G
    dims = (((1,), (1,)), ((), ()))
    for k, ref in zip(OUTGOING, (o0, o1, o2, o3)):
        rows = slice(k * width, (k + 1) * width)
        term = lax.dot_general(grads[0], wg[rows, :], dims, preferred_element_type=F32)
        term += lax.dot_general(grads[1], wu[rows, :], dims, preferred_element_type=F32)
        term = term.astype(BF)
        for j in range(G):
            ref[j] = term[:, j * part : (j + 1) * part]


def d_tok_parts(own, other, wg, wu):
    _, half, hid = own.shape
    feats = wg.shape[0]
    tok = 2 * half
    part = feats // (G * G)
    return call(
        d_tok_body,
        (shape((G, tok, part)),) * G,
        (VM,) * 4,
        [pltpu.VMEM((2, tok, hid), BF)],
        4 * tok * feats * hid,
        4 * feats * hid,
        (VM,) * G,
    )(own, other, wg, wu)


def down_body(own, other, c0, c1, c2, c3, b0, b1, b2, b3, turned):
    _, _, core, z = here()
    turned[...] = in_order(core, own[0], other[0]).T
    block = b0.shape[0]
    groups = targets(z, core)
    left = jnp.concatenate(
        [turned[pl.ds(pl.multiple_of(groups[m] * block, block), block), :] for m in range(G)],
        axis=0,
    )
    spots = plane_spots(1, False)
    part = b0.shape[1] // (G * G)
    for k, ref in enumerate((c0, c1, c2, c3)):
        term = jnp.dot(left, wide(ref), preferred_element_type=F32).astype(BF)
        for j in range(G):
            cols = feature(core, spots[k], j, part)
            for m, out in enumerate((b0, b1, b2, b3)):
                out[:, cols] = term[m * block : (m + 1) * block, j * part : (j + 1) * part]


def down_parts(own, other, chunks):
    _, half, hid = own.shape
    _, tok, part = chunks[0].shape
    feats = G * G * part
    return call(
        down_body,
        (shape((hid // G, feats)),) * G,
        (VM,) * (2 + G),
        [pltpu.VMEM((hid, tok), BF)],
        2 * tok * feats * hid,
        2 * tok * feats,
        (VM,) * G,
    )(own, other, *chunks)


def grads_body(t0, t1, t2, t3, p0, p1, p2, p3, p4, p5, p6, p7, gg, gu, acc_g, acc_u):
    core = lax.axis_index("col")
    groups = ((t0, p0, p1), (t1, p2, p4), (t2, p5, p3), (t3, p6, p7))
    for k, (tok, same, cross) in enumerate(groups):
        left = wide(tok).T
        for n, acc in enumerate((acc_g, acc_u)):
            right = in_order(core, same[n], cross[n])
            term = jnp.dot(left, right, preferred_element_type=F32)
            if k == 0:
                acc[...] = term
            else:
                acc[...] += term
    gg[...] = acc_g[...].astype(BF)
    gu[...] = acc_u[...].astype(BF)


def weight_grads(chunks, pieces):
    _, half, hid = pieces[0].shape
    feats = G * chunks[0].shape[2]
    return call(
        grads_body,
        (shape((feats, hid)),) * 2,
        (VM,) * 12,
        [pltpu.VMEM((feats, hid), F32)] * 2,
        8 * G * half * feats * hid,
        20 * half * hid,
        (VM, VM),
        32,
    )(*chunks, *pieces)


def mid_sum_body(a0, a1, a2, a3, b0, b1, b2, b3, o0, o1, o2, o3):
    spots = plane_spots(0, True)
    for k, out in enumerate((o0, o1, o2, o3)):
        at = spots[k]
        for n, (p, q, r, s) in enumerate(((a0, a1, a2, a3), (b0, b1, b2, b3))):
            total = p[at].astype(F32) + q[at].astype(F32) + (r[at].astype(F32) + s[at].astype(F32))
            out[n] = total.astype(BF)


def mid_sum(first, second):
    _, tok, part = first[0].shape
    return call(
        mid_sum_body,
        (shape((2, tok, part)),) * G,
        (VM,) * (2 * G),
        [],
        24 * tok * part,
        80 * tok * part,
        (VM,) * G,
    )(*first, *second)


def last_sum_body(p0, p1, p2, p3, out, tok):
    for n, ref in enumerate((out, tok)):
        total = p0[n].astype(F32) + p1[n].astype(F32) + (p2[n].astype(F32) + p3[n].astype(F32))
        ref[...] = total.astype(BF)


def last_sum(parts):
    _, tok, part = parts[0].shape
    return call(
        last_sum_body,
        (shape((tok, part)),) * 2,
        (VM,) * G,
        [],
        8 * tok * part,
        20 * tok * part,
        (VM, VM),
    )(*parts)


PARTS = 2


def total_body(count, *refs):
    ins, out, slots, res, sems = refs[:count], refs[count], *refs[count + 1 :]
    tile = out.shape[0] // PARTS
    loads, stores = [], []
    for t in range(PARTS):
        at = pl.ds(t * tile, tile)
        loads.append(
            [
                pltpu.make_async_copy(ref.at[at], slots.at[n, at], sems.at[t, n])
                for n, ref in enumerate(ins)
            ]
        )
        stores.append(pltpu.make_async_copy(res.at[at], out.at[at], sems.at[t, count]))
    for item in loads:
        start_all(item)
    for t in range(PARTS):
        wait_all(loads[t])

        @pl.loop(0, tile // 16)
        def _(i):
            rows = pl.ds(pl.multiple_of(t * tile + i * 16, 16), 16)
            total = slots[0, rows, :].astype(F32)
            for n in range(1, count):
                total = total + slots[n, rows, :].astype(F32)
            res[rows, :] = total.astype(BF)

        stores[t].start()
    wait_all(stores)


def total_of(parts):
    rows, cols = parts[0].shape
    count = len(parts)
    return call(
        functools.partial(total_body, count),
        (shape((rows, cols)),),
        (pl.ANY,) * count,
        [
            pltpu.VMEM((count, rows, cols), BF),
            pltpu.VMEM((rows, cols), BF),
            pltpu.SemaphoreType.DMA((PARTS, count + 1)),
        ],
        count * rows * cols,
        2 * (count + 1) * rows * cols,
    )(*parts)[0]


def plane_gather(phase, array):
    return [array] + [plane_shift(k, array, phase) for k in (1, 2, 3)]


def local(tokens, w_gate, w_up, w_down, d_out):
    first = plane_gather(0, jnp.stack([tokens, d_out]))
    chunk_t, chunk_c = place(first)
    tok_chunks = plane_gather(1, chunk_t)
    cot_chunks = [chunk_c] + [
        plane_shift(k, after(chunk_c, tok_chunks[k]), 1) for k in (1, 2, 3)
    ]
    w_gate, w_up, w_down = slot_weights(w_gate, w_up, w_down)
    picked = pick(tok_chunks)
    group1, group2 = depth_shift(1, picked[1]), depth_shift(2, picked[2])

    keep_gu, send_gu = gate_up([after(tok_chunks[0], picked[0])] + tok_chunks[1:], w_gate, w_up)
    keep_d, send = d_act(
        [after(cot_chunks[0], group1, group2)] + cot_chunks[1:], w_down, send_gu
    )
    group3 = depth_shift(3, after(picked[3], group1, group2))
    own, grads_own = hidden(keep_gu, keep_d, swap(send))
    other = swap(own)
    near_own = depth_shift(1, grads_own)

    *outs, grads_other = out_parts(own, other, w_down)
    near_other = depth_shift(1, after(grads_other, group3))
    blocks = down_parts(own, other, [after(cot_chunks[0], outs[0])] + cot_chunks[1:])
    toks = d_tok_parts(after(own, blocks[0]), other, w_gate, w_up)

    out_got = [plane_shift(k, outs[k], 1) for k in (1, 2, 3)]
    near_own, toks, out_got = lax.optimization_barrier((near_own, toks, out_got))
    far_own = depth_shift(1, near_own)
    relay = depth_shift(1, after(blocks[3], near_own))
    tok_got = [plane_shift(k, toks[k], 1) for k in (1, 2, 3)]

    joined = total_of([after(blocks[1], near_other), relay])
    ahead = depth_shift(1, joined)
    back = depth_shift(2, after(blocks[2], joined))

    middle = mid_sum([after(outs[0], joined)] + out_got, [toks[0]] + tok_got)
    last = [plane_shift(k, middle[k], 0) for k in (1, 2, 3)]
    swapped = [
        swap(after(item, far_own, joined, *tok_got)) for item in (near_own, near_other, far_own)
    ]

    pieces = [
        grads_own, grads_other,
        near_own, swapped[0],
        near_other, swapped[1],
        far_own, swapped[2],
    ]
    grad_gate, grad_up = weight_grads([picked[0], group1, group2, group3], pieces)
    output, d_tokens = last_sum([after(middle[0], grad_gate)] + last)
    grad_down = total_of([after(blocks[0], grad_gate), back, ahead])
    return output, d_tokens, grad_gate, grad_up, grad_down


def solution(mesh):
    placed = (
        P("depth", ("col", "row")),
        P("col", "row"),
        P("col", "row"),
        P("row", "col"),
        P("depth", ("col", "row")),
    )
    return jax.shard_map(
        local,
        mesh=mesh,
        in_specs=placed,
        out_specs=(
            P("depth", ("col", "row")),
            P("depth", ("col", "row")),
            P(("col", "depth"), "row"),
            P(("col", "depth"), "row"),
            P(("row", "depth"), "col"),
        ),
        check_vma=False,
    )
```

time: 159 us -> 142 us (0.89)
  Pallas kernels: 49.6 us -> 35.9 us
  waiting for transfers between devices: 58.9 us -> 63.7 us
  starting transfers between devices: 44.7 us -> 40.2 us
  local copies, waits for them, and re-layouts: 3.42 us -> 0 us
    pallas_call x6 -> x7, Pallas kernels: 30.6 us -> 21.6 us  [the longest x1 5.48 us: weight_grads(): call(grads_body, (shape((feats, hid)),) * 2, (VM,) * 12, [pltpu.VMEM((fea...]
    ppermute x9, waiting for transfers between devices: 34.3 us -> 40.2 us  [depth_shift(): return lax.ppermute(array, ('col', 'depth'), pairs)]
    ppermute x9, starting transfers between devices: 15.1 us -> 11.1 us  [depth_shift(): return lax.ppermute(array, ('col', 'depth'), pairs)]
    unnamed x20 -> x0, local copies, waits for them, and re-layouts: 3.42 us -> none
    pallas_call x1, Pallas kernels: 5.06 us -> 2.38 us  [out_parts(): call(out_body, (shape((G, tok, part)),) * G + (shape((2, half, hid)),), (...]
    pallas_call x1, Pallas kernels: 7.7 us -> 5.64 us  [gate_up(): call(gate_up_body, (shape((2, tok // 2, hid), F32), shape((2, tok // 2, h...]
    ppermute x18, waiting for transfers between devices: 22 us -> 20.1 us  [plane_shift(): return lax.ppermute(array, ('row', 'col'), pairs)]
    ppermute x6 -> x5, waiting for transfers between devices: 2.63 us -> 3.29 us  [swap(): return lax.ppermute(array, 'col', [(0, 1), (1, 0)])]
  transfers between devices with their start and end apart: 33 -> 32, of which waited for: 16 -> 16; matrix products, arithmetic and copies ran while one was open for 0% -> 0% of each run, Pallas kernels for 25% -> 22%
where the time goes in v3:
time: 142 us
  waiting for transfers between devices  63.7 us (45%)
  starting transfers between devices  40.2 us (28%)
  Pallas kernels  35.9 us (25%)
    ppermute x9, waiting for transfers between devices, depth_shift(): return lax.ppermute(array, ('col', 'depth'), pairs)  40.2 us
    ppermute x18, starting transfers between devices, plane_shift(): return lax.ppermute(array, ('row', 'col'), pairs)  28.2 us
    ppermute x18, waiting for transfers between devices, plane_shift(): return lax.ppermute(array, ('row', 'col'), pairs)  20.1 us
    ppermute x9, starting transfers between devices, depth_shift(): return lax.ppermute(array, ('col', 'depth'), pairs)  11.1 us
    pallas_call x1, Pallas kernels, gate_up(): call(gate_up_body, (shape((2, tok // 2, hid), F32), shape((2, tok // 2, h...  5.64 us
    pallas_call x1, Pallas kernels, weight_grads(): call(grads_body, (shape((feats, hid)),) * 2, (VM,) * 12, [pltpu.VMEM((fea...  5.48 us
    pallas_call x2, Pallas kernels, total_of(): call(functools.partial(total_body, count), (shape((rows, cols)),), (pl.AN...  4.85 us
    pallas_call x1, Pallas kernels, slot_weights(): call(weights_body, (shape(wg.shape), shape(wu.shape), shape(wd.shape)), (...  4.77 us
  transfers between devices with their start and end apart: 32, of which 16 were waited for; matrix products, arithmetic and copies ran while one was open for 0% of the time, Pallas kernels for 22%

profile of v3, /device:TPU:0, one launch (start us, length us, event | category | flops | bytes accessed | tf_op | source)
XLA Modules:
  0.0 141.6 jit_solution(2935155594956691315)
XLA Ops:
  0.6 1.0 pad_maximum_fusion.p0
  1.6 1.6 %collective-permute-start = (bf16[2,512,128]{2,1,0:T(8,128)(2,1)S(1)}, bf16[2,512,128]{2,1,0:T(8,128)(2,1)S(1)}, u32[]{:S(2)}, u32[]{:S(2)}) collective-permute-start(bf16[2,512,128]{2,1,0:T(8,128)(2,1)S(1)} %pad_maximum_fusion.p0), channel_id=1, source_target_pairs={{0,8},{4,36},{8,16},{12,44},{16,24},{20,52},{24,0},{28,60},{32,40}... | collective-permute-start | bytes 786440 | tf_op jit(solution)/shard_map/ppermute | solution.py:54
  3.3 1.7 %collective-permute-start.1 = (bf16[2,512,128]{2,1,0:T(8,128)(2,1)S(1)}, bf16[2,512,128]{2,1,0:T(8,128)(2,1)S(1)}, u32[]{:S(2)}, u32[]{:S(2)}) collective-permute-start(bf16[2,512,128]{2,1,0:T(8,128)(2,1)S(1)} %pad_maximum_fusion.p0), channel_id=1, source_target_pairs={{0,24},{4,100},{8,0},{12,108},{16,8},{20,116},{24,16},{28,124},{32... | collective-permute-start | bytes 786440 | tf_op jit(solution)/shard_map/ppermute | solution.py:54
  4.9 1.9 %collective-permute-start.2 = (bf16[2,512,128]{2,1,0:T(8,128)(2,1)S(1)}, bf16[2,512,128]{2,1,0:T(8,128)(2,1)S(1)}, u32[]{:S(2)}, u32[]{:S(2)}) collective-permute-start(bf16[2,512,128]{2,1,0:T(8,128)(2,1)S(1)} %pad_maximum_fusion.p0), channel_id=1, source_target_pairs={{0,16},{4,68},{8,24},{12,76},{16,0},{20,84},{24,8},{28,92},{32,48}... | collective-permute-start | bytes 786440 | tf_op jit(solution)/shard_map/ppermute | solution.py:54
  6.8 2.4 %collective-permute-done.p1 = bf16[2,512,128]{2,1,0:T(8,128)(2,1)S(1)} collective-permute-done((bf16[2,512,128]{2,1,0:T(8,128)(2,1)S(1)}, bf16[2,512,128]{2,1,0:T(8,128)(2,1)S(1)}, u32[]{:S(2)}, u32[]{:S(2)}) %collective-permute-start) | collective-permute-done | bytes 262176 | tf_op jit(solution)/shard_map/ppermute | solution.py:54
  9.6 3.5 %collective-permute-done.2.p3 = bf16[2,512,128]{2,1,0:T(8,128)(2,1)S(1)} collective-permute-done((bf16[2,512,128]{2,1,0:T(8,128)(2,1)S(1)}, bf16[2,512,128]{2,1,0:T(8,128)(2,1)S(1)}, u32[]{:S(2)}, u32[]{:S(2)}) %collective-permute-start.2) | collective-permute-done | bytes 262176 | tf_op jit(solution)/shard_map/ppermute | solution.py:54
  13.3 1.6 %collective-permute-start.3 = (bf16[4,512,128]{2,1,0:T(8,128)(2,1)S(1)}, bf16[4,512,128]{2,1,0:T(8,128)(2,1)S(1)}, u32[]{:S(2)}, u32[]{:S(2)}) collective-permute-start(bf16[4,512,128]{2,1,0:T(8,128)(2,1)S(1)} %get-tuple-element.69.c0.t0), channel_id=1, source_target_pairs={{0,32},{4,12},{8,40},{12,20},{16,48},{20,28},{24,56},{28,4},{32,64... | collective-permute-start | bytes 1572872 | tf_op jit(solution)/shard_map/ppermute | solution.py:54
  14.9 1.7 %collective-permute-start.4 = (bf16[4,512,128]{2,1,0:T(8,128)(2,1)S(1)}, bf16[4,512,128]{2,1,0:T(8,128)(2,1)S(1)}, u32[]{:S(2)}, u32[]{:S(2)}) collective-permute-start(bf16[4,512,128]{2,1,0:T(8,128)(2,1)S(1)} %get-tuple-element.69.c0.t0), channel_id=1, source_target_pairs={{0,96},{4,28},{8,104},{12,4},{16,112},{20,12},{24,120},{28,20},{32... | collective-permute-start | bytes 1572872 | tf_op jit(solution)/shard_map/ppermute | solution.py:54
  16.6 2.0 %collective-permute-start.5 = (bf16[4,512,128]{2,1,0:T(8,128)(2,1)S(1)}, bf16[4,512,128]{2,1,0:T(8,128)(2,1)S(1)}, u32[]{:S(2)}, u32[]{:S(2)}) collective-permute-start(bf16[4,512,128]{2,1,0:T(8,128)(2,1)S(1)} %get-tuple-element.69.c0.t0), channel_id=1, source_target_pairs={{0,64},{4,20},{8,72},{12,28},{16,80},{20,4},{24,88},{28,12},{32,96... | collective-permute-start | bytes 1572872 | tf_op jit(solution)/shard_map/ppermute | solution.py:54
  18.6 5.2 %collective-permute-done.3.c1.t1 = bf16[4,512,128]{2,1,0:T(8,128)(2,1)S(1)} collective-permute-done((bf16[4,512,128]{2,1,0:T(8,128)(2,1)S(1)}, bf16[4,512,128]{2,1,0:T(8,128)(2,1)S(1)}, u32[]{:S(2)}, u32[]{:S(2)}) %collective-permute-start.3) | collective-permute-done | bytes 524320 | tf_op jit(solution)/shard_map/ppermute | solution.py:54
  24.1 6.5 %collective-permute-done.5.c3.t3 = bf16[4,512,128]{2,1,0:T(8,128)(2,1)S(1)} collective-permute-done((bf16[4,512,128]{2,1,0:T(8,128)(2,1)S(1)}, bf16[4,512,128]{2,1,0:T(8,128)(2,1)S(1)}, u32[]{:S(2)}, u32[]{:S(2)}) %collective-permute-start.5) | collective-permute-done | bytes 524320 | tf_op jit(solution)/shard_map/ppermute | solution.py:54
  30.9 2.0 %collective-permute-start.6 = (bf16[4,512,128]{2,1,0:T(8,128)(2,1)S(1)}, bf16[4,512,128]{2,1,0:T(8,128)(2,1)S(1)}, u32[]{:S(2)}, u32[]{:S(2)}) collective-permute-start(bf16[4,512,128]{2,1,0:T(8,128)(2,1)S(1)} %get-tuple-element.74), channel_id=1, source_target_pairs={{0,1},{1,2},{2,3},{3,0},{4,7},{5,4},{6,5},{7,6},{8,9},{9,10},{10,1... | collective-permute-start | bytes 1572872 | tf_op jit(solution)/shard_map/ppermute | solution.py:63
  32.9 2.2 %collective-permute-start.7 = (bf16[4,512,128]{2,1,0:T(8,128)(2,1)S(1)}, bf16[4,512,128]{2,1,0:T(8,128)(2,1)S(1)}, u32[]{:S(2)}, u32[]{:S(2)}) collective-permute-start(bf16[4,512,128]{2,1,0:T(8,128)(2,1)S(1)} %get-tuple-element.75), channel_id=1, source_target_pairs={{0,3},{1,0},{2,1},{3,2},{4,5},{5,6},{6,7},{7,4},{8,11},{9,8},{10,9... | collective-permute-start | bytes 1572872 | tf_op jit(solution)/shard_map/ppermute | solution.py:63
  35.9 2.1 %collective-permute-start.8 = (bf16[4,512,128]{2,1,0:T(8,128)(2,1)S(1)}, bf16[4,512,128]{2,1,0:T(8,128)(2,1)S(1)}, u32[]{:S(2)}, u32[]{:S(2)}) collective-permute-start(bf16[4,512,128]{2,1,0:T(8,128)(2,1)S(1)} %get-tuple-element.86.c0), channel_id=1, source_target_pairs={{0,32},{4,12},{8,40},{12,20},{16,48},{20,28},{24,56},{28,4},{32,64... | collective-permute-start | bytes 1572872 | tf_op jit(solution)/shard_map/ppermute | solution.py:54
  38.0 1.2 collective-permute-start.9
  39.2 4.8 %shard_map.94 = (bf16[2048,896]{1,0:T(8,128)(2,1)S(1)}, bf16[2048,896]{1,0:T(8,128)(2,1)S(1)}, bf16[896,2048]{1,0:T(8,128)(2,1)S(1)}) custom-call(bf16[2048,896]{1,0:T(8,128)(2,1)} %wg.1, bf16[2048,896]{1,0:T(8,128)(2,1)} %wu.1, bf16[896,2048]{1,0:T(8,128)(2,1)} %wd.1), custom_call_target="tpu_custom_call" | custom-call | bytes 440401 | tf_op jit(solution)/shard_map/pallas_call | solution.py:238
  44.0 5.6 %shard_map.95 = (f32[2,256,896]{2,1,0:T(8,128)S(1)}, bf16[2,256,896]{2,1,0:T(8,128)(2,1)S(1)}) custom-call(bf16[4,512,128]{2,1,0:T(8,128)(2,1)S(1)} %get-tuple-element.69.c0.t0, bf16[4,512,128]{2,1,0:T(8,128)(2,1)S(1)} %collective-permute-done.3.c1.t1, bf16[4,512,128]{2,1,0:T(8,128)(2,1)S(1)} %collective-permute-done.4.c2.t2, ...), custom_call_target="tpu_custom_call" | custom-call | flops 75161928 | bytes 146800 | tf_op jit(solution)/shard_map/pallas_call | solution.py:277
  49.7 1.7 %collective-permute-done.8.c1 = bf16[4,512,128]{2,1,0:T(8,128)(2,1)S(1)} collective-permute-done((bf16[4,512,128]{2,1,0:T(8,128)(2,1)S(1)}, bf16[4,512,128]{2,1,0:T(8,128)(2,1)S(1)}, u32[]{:S(2)}, u32[]{:S(2)}) %collective-permute-start.8) | collective-permute-done | bytes 524320 | tf_op jit(solution)/shard_map/ppermute | solution.py:54
  51.4 2.7 %shard_map.96 = (f32[256,896]{1,0:T(8,128)S(1)}, bf16[3,256,896]{2,1,0:T(8,128)(2,1)S(1)}) custom-call(bf16[4,512,128]{2,1,0:T(8,128)(2,1)S(1)} %get-tuple-element.86.c0, bf16[4,512,128]{2,1,0:T(8,128)(2,1)S(1)} %collective-permute-done.8.c1, bf16[4,512,128]{2,1,0:T(8,128)(2,1)S(1)} %collective-permute-done.9.c2, ...), custom_call_target="tpu_custom_call" | custom-call | flops 37580964 | bytes 73400 | tf_op jit(solution)/shard_map/pallas_call | solution.py:315
  54.2 3.1 %collective-permute-done.11.recv = bf16[3,256,896]{2,1,0:T(8,128)(2,1)S(1)} collective-permute-done((bf16[3,256,896]{2,1,0:T(8,128)(2,1)S(1)}, bf16[3,256,896]{2,1,0:T(8,128)(2,1)S(1)}, u32[]{:S(2)}, u32[]{:S(2)}) %collective-permute-start.11) | collective-permute-done | bytes 1376288 | tf_op jit(solution)/shard_map/ppermute | solution.py:67
  57.4 0.8 shard_map.97
  58.4 1.8 %collective-permute-start.13 = (bf16[4,512,128]{2,1,0:T(8,128)(2,1)S(1)}, bf16[4,512,128]{2,1,0:T(8,128)(2,1)S(1)}, u32[]{:S(2)}, u32[]{:S(2)}) collective-permute-start(bf16[4,512,128]{2,1,0:T(8,128)(2,1)S(1)} %get-tuple-element.90), channel_id=1, source_target_pairs={{0,2},{1,3},{2,0},{3,1},{4,6},{5,7},{6,4},{7,5},{8,10},{9,11},{10,... | collective-permute-start | bytes 1572872 | tf_op jit(solution)/shard_map/ppermute | solution.py:63
  60.2 1.0 collective-permute-start.15
  61.4 2.4 %shard_map.98 = (bf16[4,512,128]{2,1,0:T(8,128)(2,1)S(1)}, bf16[4,512,128]{2,1,0:T(8,128)(2,1)S(1)}, bf16[4,512,128]{2,1,0:T(8,128)(2,1)S(1)}, bf16[4,512,128]{2,1,0:T(8,128)(2,1)S(1)}, bf16[2,256,896]{2,1,0:T(8,128)(2,1)S(1)}) custom-call(bf16[3,256,896]{2,1,0:T(8,128)(2,1)S(1)} %get-tuple-element.96.own, ...), custom_call_target="tpu_custom_call" | custom-call | flops 37580964 | bytes 73400 | tf_op jit(solution)/shard_map/pallas_call | solution.py:383
  63.7 1.5 %collective-permute-start.16 = (bf16[4,512,128]{2,1,0:T(8,128)(2,1)S(1)}, bf16[4,512,128]{2,1,0:T(8,128)(2,1)S(1)}, u32[]{:S(2)}, u32[]{:S(2)}) collective-permute-start(bf16[4,512,128]{2,1,0:T(8,128)(2,1)S(1)} %get-tuple-element.101), channel_id=1, source_target_pairs={{0,32},{4,12},{8,40},{12,20},{16,48},{20,28},{24,56},{28,4},{32,64... | collective-permute-start | bytes 1572872 | tf_op jit(solution)/shard_map/ppermute | solution.py:54
  65.2 1.8 %collective-permute-start.17 = (bf16[4,512,128]{2,1,0:T(8,128)(2,1)S(1)}, bf16[4,512,128]{2,1,0:T(8,128)(2,1)S(1)}, u32[]{:S(2)}, u32[]{:S(2)}) collective-permute-start(bf16[4,512,128]{2,1,0:T(8,128)(2,1)S(1)} %get-tuple-element.102), channel_id=1, source_target_pairs={{0,96},{4,28},{8,104},{12,4},{16,112},{20,12},{24,120},{28,20},{32... | collective-permute-start | bytes 1572872 | tf_op jit(solution)/shard_map/ppermute | solution.py:54
  67.0 0.8 collective-permute-start.18
  67.9 6.3 %collective-permute-done.13.t3 = bf16[4,512,128]{2,1,0:T(8,128)(2,1)S(1)} collective-permute-done((bf16[4,512,128]{2,1,0:T(8,128)(2,1)S(1)}, bf16[4,512,128]{2,1,0:T(8,128)(2,1)S(1)}, u32[]{:S(2)}, u32[]{:S(2)}) %collective-permute-start.13) | collective-permute-done | bytes 524320 | tf_op jit(solution)/shard_map/ppermute | solution.py:63
  74.5 3.0 %shard_map.99 = (bf16[224,2048]{1,0:T(8,128)(2,1)S(1)}, bf16[224,2048]{1,0:T(8,128)(2,1)S(1)}, bf16[224,2048]{1,0:T(8,128)(2,1)S(1)}, bf16[224,2048]{1,0:T(8,128)(2,1)S(1)}) custom-call(bf16[3,256,896]{2,1,0:T(8,128)(2,1)S(1)} %get-tuple-element.96.own, bf16[3,256,896]{2,1,0:T(8,128)(2,1)S(1)} %collective-permute-done.12.other, ...), custom_call_target="tpu_custom_call" | custom-call | flops 37580964 | bytes 41943 | tf_op jit(solution)/shard_map/pallas_call | solution.py:449
  77.5 4.5 %shard_map.100 = (bf16[4,512,128]{2,1,0:T(8,128)(2,1)S(1)}, bf16[4,512,128]{2,1,0:T(8,128)(2,1)S(1)}, bf16[4,512,128]{2,1,0:T(8,128)(2,1)S(1)}, bf16[4,512,128]{2,1,0:T(8,128)(2,1)S(1)}) custom-call(bf16[3,256,896]{2,1,0:T(8,128)(2,1)S(1)} %get-tuple-element.96.own, bf16[3,256,896]{2,1,0:T(8,128)(2,1)S(1)} %collective-permute-done.12.other, ...), custom_call_target="tpu_custom_call" | custom-call | flops 75161928 | bytes 146800 | tf_op jit(solution)/shard_map/pallas_call | solution.py:415
  82.0 1.9 %collective-permute-done.15.p2 = bf16[2,256,896]{2,1,0:T(8,128)(2,1)S(1)} collective-permute-done((bf16[2,256,896]{2,1,0:T(8,128)(2,1)S(1)}, bf16[2,256,896]{2,1,0:T(8,128)(2,1)S(1)}, u32[]{:S(2)}, u32[]{:S(2)}) %collective-permute-start.15) | collective-permute-done | bytes 917536 | tf_op jit(solution)/shard_map/ppermute | solution.py:63
  84.3 1.4 %collective-permute-start.23 = (bf16[2,256,896]{2,1,0:T(8,128)(2,1)S(1)}, bf16[2,256,896]{2,1,0:T(8,128)(2,1)S(1)}, u32[]{:S(2)}, u32[]{:S(2)}) collective-permute-start(bf16[2,256,896]{2,1,0:T(8,128)(2,1)S(1)} %collective-permute-done.15.p2), channel_id=1, source_target_pairs={{0,1},{1,2},{2,3},{3,0},{4,7},{5,4},{6,5},{7,6},{8,9},{9,10},{10,1... | collective-permute-start | bytes 2752520 | tf_op jit(solution)/shard_map/ppermute | solution.py:63
  85.7 1.4 collective-permute-start.20
  87.1 1.8 %collective-permute-start.21 = (bf16[4,512,128]{2,1,0:T(8,128)(2,1)S(1)}, bf16[4,512,128]{2,1,0:T(8,128)(2,1)S(1)}, u32[]{:S(2)}, u32[]{:S(2)}) collective-permute-start(bf16[4,512,128]{2,1,0:T(8,128)(2,1)S(1)} %get-tuple-element.112), channel_id=1, source_target_pairs={{0,96},{4,28},{8,104},{12,4},{16,112},{20,12},{24,120},{28,20},{32... | collective-permute-start | bytes 1572872 | tf_op jit(solution)/shard_map/ppermute | solution.py:54
  89.0 4.8 %collective-permute-done.14.p4 = bf16[2,256,896]{2,1,0:T(8,128)(2,1)S(1)} collective-permute-done((bf16[2,256,896]{2,1,0:T(8,128)(2,1)S(1)}, bf16[2,256,896]{2,1,0:T(8,128)(2,1)S(1)}, u32[]{:S(2)}, u32[]{:S(2)}) %collective-permute-start.14) | collective-permute-done | bytes 917536 | tf_op jit(solution)/shard_map/ppermute | solution.py:63
  93.7 2.1 %collective-permute-start.22 = (bf16[4,512,128]{2,1,0:T(8,128)(2,1)S(1)}, bf16[4,512,128]{2,1,0:T(8,128)(2,1)S(1)}, u32[]{:S(2)}, u32[]{:S(2)}) collective-permute-start(bf16[4,512,128]{2,1,0:T(8,128)(2,1)S(1)} %get-tuple-element.113), channel_id=1, source_target_pairs={{0,64},{4,20},{8,72},{12,28},{16,80},{20,4},{24,88},{28,12},{32,96... | collective-permute-start | bytes 1572872 | tf_op jit(solution)/shard_map/ppermute | solution.py:54
  95.8 7.8 %collective-permute-done.19.refs_1_ = bf16[224,2048]{1,0:T(8,128)(2,1)S(1)} collective-permute-done((bf16[224,2048]{1,0:T(8,128)(2,1)S(1)}, bf16[224,2048]{1,0:T(8,128)(2,1)S(1)}, u32[]{:S(2)}, u32[]{:S(2)}) %collective-permute-start.19) | collective-permute-done | bytes 917536 | tf_op jit(solution)/shard_map/ppermute | solution.py:63
  103.6 2.0 %shard_map.101 = bf16[224,2048]{1,0:T(8,128)(2,1)S(1)} custom-call(bf16[224,2048]{1,0:T(8,128)(2,1)S(1)} %get-tuple-element.92.refs_0_, bf16[224,2048]{1,0:T(8,128)(2,1)S(1)} %collective-permute-done.19.refs_1_), custom_call_target="tpu_custom_call" | custom-call | flops 18350 | bytes 55050 | tf_op jit(solution)/shard_map/pallas_call | solution.py:568
  105.6 7.8 %collective-permute-done.23.p6 = bf16[2,256,896]{2,1,0:T(8,128)(2,1)S(1)} collective-permute-done((bf16[2,256,896]{2,1,0:T(8,128)(2,1)S(1)}, bf16[2,256,896]{2,1,0:T(8,128)(2,1)S(1)}, u32[]{:S(2)}, u32[]{:S(2)}) %collective-permute-start.23) | collective-permute-done | bytes 917536 | tf_op jit(solution)/shard_map/ppermute | solution.py:63
  113.9 1.7 %collective-permute-start.30 = (bf16[224,2048]{1,0:T(8,128)(2,1)S(1)}, bf16[224,2048]{1,0:T(8,128)(2,1)S(1)}, u32[]{:S(2)}, u32[]{:S(2)}) collective-permute-start(bf16[224,2048]{1,0:T(8,128)(2,1)S(1)} %get-tuple-element.128), channel_id=1, source_target_pairs={{0,3},{1,0},{2,1},{3,2},{4,5},{5,6},{6,7},{7,4},{8,11},{9,8},{10,9... | collective-permute-start | bytes 2752520 | tf_op jit(solution)/shard_map/ppermute | solution.py:63
  116.5 1.5 %collective-permute-start.27 = (bf16[2,512,128]{2,1,0:T(8,128)(2,1)S(1)}, bf16[2,512,128]{2,1,0:T(8,128)(2,1)S(1)}, u32[]{:S(2)}, u32[]{:S(2)}) collective-permute-start(bf16[2,512,128]{2,1,0:T(8,128)(2,1)S(1)} %get-tuple-element.120), channel_id=1, source_target_pairs={{0,8},{4,36},{8,16},{12,44},{16,24},{20,52},{24,0},{28,60},{32,40}... | collective-permute-start | bytes 786440 | tf_op jit(solution)/shard_map/ppermute | solution.py:54
  118.0 1.8 %collective-permute-start.28 = (bf16[2,512,128]{2,1,0:T(8,128)(2,1)S(1)}, bf16[2,512,128]{2,1,0:T(8,128)(2,1)S(1)}, u32[]{:S(2)}, u32[]{:S(2)}) collective-permute-start(bf16[2,512,128]{2,1,0:T(8,128)(2,1)S(1)} %get-tuple-element.121), channel_id=1, source_target_pairs={{0,24},{4,100},{8,0},{12,108},{16,8},{20,116},{24,16},{28,124},{32... | collective-permute-start | bytes 786440 | tf_op jit(solution)/shard_map/ppermute | solution.py:54
  119.8 0.9 collective-permute-start.29
  120.7 5.5 %shard_map.103 = (bf16[512,896]{1,0:T(8,128)(2,1)}, bf16[512,896]{1,0:T(8,128)(2,1)}) custom-call(bf16[4,512,128]{2,1,0:T(8,128)(2,1)S(1)} %get-tuple-element.68.t0, bf16[4,512,128]{2,1,0:T(8,128)(2,1)S(1)} %collective-permute-done.6.t1, bf16[4,512,128]{2,1,0:T(8,128)(2,1)S(1)} %collective-permute-done.7.t2, ...), custom_call_target="tpu_custom_call" | custom-call | flops 75161928 | bytes 91750 | tf_op jit(solution)/shard_map/pallas_call | solution.py:479
  126.2 10.5 %collective-permute-done.30.refs_1_ = bf16[224,2048]{1,0:T(8,128)(2,1)S(1)} collective-permute-done((bf16[224,2048]{1,0:T(8,128)(2,1)S(1)}, bf16[224,2048]{1,0:T(8,128)(2,1)S(1)}, u32[]{:S(2)}, u32[]{:S(2)}) %collective-permute-start.30) | collective-permute-done | bytes 917536 | tf_op jit(solution)/shard_map/ppermute | solution.py:63
  136.7 1.2 collective-permute-done.31.refs_2_
  137.9 2.9 %shard_map.105 = bf16[224,2048]{1,0:T(8,128)(2,1)} custom-call(bf16[224,2048]{1,0:T(8,128)(2,1)S(1)} %get-tuple-element.126.refs_0_, bf16[224,2048]{1,0:T(8,128)(2,1)S(1)} %collective-permute-done.30.refs_1_, bf16[224,2048]{1,0:T(8,128)(2,1)S(1)} %collective-permute-done.31.refs_2_), custom_call_target="tpu_custom_call" | custom-call | flops 27525 | bytes 73400 | tf_op jit(solution)/shard_map/pallas_call | solution.py:568
  140.8 0.8 shard_map.104
  (31 shorter events, 4.4 us)
Async XLA Ops:
  1.6 7.7 %collective-permute-start = (bf16[2,512,128]{2,1,0:T(8,128)(2,1)S(1)}, bf16[2,512,128]{2,1,0:T(8,128)(2,1)S(1)}, u32[]{:S(2)}, u32[]{:S(2)}) collective-permute-start(bf16[2,512,128]{2,1,0:T(8,128)(2,1)S(1)} %pad_maximum_fusion.p0), channel_id=1, source_target_pairs={{0,8},{4,36},{8,16},{12,44},{16,24},{20,52},{24,0},{28,60},{32,40}... | collective-permute-start | bytes 786440 | tf_op jit(solution)/shard_map/ppermute | solution.py:54
  3.3 6.4 %collective-permute-start.1 = (bf16[2,512,128]{2,1,0:T(8,128)(2,1)S(1)}, bf16[2,512,128]{2,1,0:T(8,128)(2,1)S(1)}, u32[]{:S(2)}, u32[]{:S(2)}) collective-permute-start(bf16[2,512,128]{2,1,0:T(8,128)(2,1)S(1)} %pad_maximum_fusion.p0), channel_id=1, source_target_pairs={{0,24},{4,100},{8,0},{12,108},{16,8},{20,116},{24,16},{28,124},{32... | collective-permute-start | bytes 786440 | tf_op jit(solution)/shard_map/ppermute | solution.py:54
  4.9 8.2 %collective-permute-start.2 = (bf16[2,512,128]{2,1,0:T(8,128)(2,1)S(1)}, bf16[2,512,128]{2,1,0:T(8,128)(2,1)S(1)}, u32[]{:S(2)}, u32[]{:S(2)}) collective-permute-start(bf16[2,512,128]{2,1,0:T(8,128)(2,1)S(1)} %pad_maximum_fusion.p0), channel_id=1, source_target_pairs={{0,16},{4,68},{8,24},{12,76},{16,0},{20,84},{24,8},{28,92},{32,48}... | collective-permute-start | bytes 786440 | tf_op jit(solution)/shard_map/ppermute | solution.py:54
  13.3 10.5 %collective-permute-start.3 = (bf16[4,512,128]{2,1,0:T(8,128)(2,1)S(1)}, bf16[4,512,128]{2,1,0:T(8,128)(2,1)S(1)}, u32[]{:S(2)}, u32[]{:S(2)}) collective-permute-start(bf16[4,512,128]{2,1,0:T(8,128)(2,1)S(1)} %get-tuple-element.69.c0.t0), channel_id=1, source_target_pairs={{0,32},{4,12},{8,40},{12,20},{16,48},{20,28},{24,56},{28,4},{32,64... | collective-permute-start | bytes 1572872 | tf_op jit(solution)/shard_map/ppermute | solution.py:54
  14.9 9.2 %collective-permute-start.4 = (bf16[4,512,128]{2,1,0:T(8,128)(2,1)S(1)}, bf16[4,512,128]{2,1,0:T(8,128)(2,1)S(1)}, u32[]{:S(2)}, u32[]{:S(2)}) collective-permute-start(bf16[4,512,128]{2,1,0:T(8,128)(2,1)S(1)} %get-tuple-element.69.c0.t0), channel_id=1, source_target_pairs={{0,96},{4,28},{8,104},{12,4},{16,112},{20,12},{24,120},{28,20},{32... | collective-permute-start | bytes 1572872 | tf_op jit(solution)/shard_map/ppermute | solution.py:54
  16.6 14.0 %collective-permute-start.5 = (bf16[4,512,128]{2,1,0:T(8,128)(2,1)S(1)}, bf16[4,512,128]{2,1,0:T(8,128)(2,1)S(1)}, u32[]{:S(2)}, u32[]{:S(2)}) collective-permute-start(bf16[4,512,128]{2,1,0:T(8,128)(2,1)S(1)} %get-tuple-element.69.c0.t0), channel_id=1, source_target_pairs={{0,64},{4,20},{8,72},{12,28},{16,80},{20,4},{24,88},{28,12},{32,96... | collective-permute-start | bytes 1572872 | tf_op jit(solution)/shard_map/ppermute | solution.py:54
  30.9 18.7 %collective-permute-start.6 = (bf16[4,512,128]{2,1,0:T(8,128)(2,1)S(1)}, bf16[4,512,128]{2,1,0:T(8,128)(2,1)S(1)}, u32[]{:S(2)}, u32[]{:S(2)}) collective-permute-start(bf16[4,512,128]{2,1,0:T(8,128)(2,1)S(1)} %get-tuple-element.74), channel_id=1, source_target_pairs={{0,1},{1,2},{2,3},{3,0},{4,7},{5,4},{6,5},{7,6},{8,9},{9,10},{10,1... | collective-permute-start | bytes 1572872 | tf_op jit(solution)/shard_map/ppermute | solution.py:63
  32.9 16.7 %collective-permute-start.7 = (bf16[4,512,128]{2,1,0:T(8,128)(2,1)S(1)}, bf16[4,512,128]{2,1,0:T(8,128)(2,1)S(1)}, u32[]{:S(2)}, u32[]{:S(2)}) collective-permute-start(bf16[4,512,128]{2,1,0:T(8,128)(2,1)S(1)} %get-tuple-element.75), channel_id=1, source_target_pairs={{0,3},{1,0},{2,1},{3,2},{4,5},{5,6},{6,7},{7,4},{8,11},{9,8},{10,9... | collective-permute-start | bytes 1572872 | tf_op jit(solution)/shard_map/ppermute | solution.py:63
  35.1 14.5 %collective-permute-start.10 = (bf16[4,512,128]{2,1,0:T(8,128)(2,1)S(1)}, bf16[4,512,128]{2,1,0:T(8,128)(2,1)S(1)}, u32[]{:S(2)}, u32[]{:S(2)}) collective-permute-start(bf16[4,512,128]{2,1,0:T(8,128)(2,1)S(1)} %get-tuple-element.86.c0), channel_id=1, source_target_pairs={{0,64},{4,20},{8,72},{12,28},{16,80},{20,4},{24,88},{28,12},{32,96... | collective-permute-start | bytes 1572872 | tf_op jit(solution)/shard_map/ppermute | solution.py:54
  35.9 15.6 %collective-permute-start.8 = (bf16[4,512,128]{2,1,0:T(8,128)(2,1)S(1)}, bf16[4,512,128]{2,1,0:T(8,128)(2,1)S(1)}, u32[]{:S(2)}, u32[]{:S(2)}) collective-permute-start(bf16[4,512,128]{2,1,0:T(8,128)(2,1)S(1)} %get-tuple-element.86.c0), channel_id=1, source_target_pairs={{0,32},{4,12},{8,40},{12,20},{16,48},{20,28},{24,56},{28,4},{32,64... | collective-permute-start | bytes 1572872 | tf_op jit(solution)/shard_map/ppermute | solution.py:54
  38.0 13.4 %collective-permute-start.9 = (bf16[4,512,128]{2,1,0:T(8,128)(2,1)S(1)}, bf16[4,512,128]{2,1,0:T(8,128)(2,1)S(1)}, u32[]{:S(2)}, u32[]{:S(2)}) collective-permute-start(bf16[4,512,128]{2,1,0:T(8,128)(2,1)S(1)} %get-tuple-element.86.c0), channel_id=1, source_target_pairs={{0,96},{4,28},{8,104},{12,4},{16,112},{20,12},{24,120},{28,20},{32... | collective-permute-start | bytes 1572872 | tf_op jit(solution)/shard_map/ppermute | solution.py:54
  54.2 3.2 %collective-permute-start.11 = (bf16[3,256,896]{2,1,0:T(8,128)(2,1)S(1)}, bf16[3,256,896]{2,1,0:T(8,128)(2,1)S(1)}, u32[]{:S(2)}, u32[]{:S(2)}) collective-permute-start(bf16[3,256,896]{2,1,0:T(8,128)(2,1)S(1)} %get-tuple-element.83), channel_id=1, source_target_pairs={{0,4},{4,0},{1,5},{5,1},{2,6},{6,2},{3,7},{7,3},{8,12},{12,8},{9,1... | collective-permute-start | bytes 4128776 | tf_op jit(solution)/shard_map/ppermute | solution.py:67
  58.1 3.2 %collective-permute-start.12 = (bf16[3,256,896]{2,1,0:T(8,128)(2,1)S(1)}, bf16[3,256,896]{2,1,0:T(8,128)(2,1)S(1)}, u32[]{:S(2)}, u32[]{:S(2)}) collective-permute-start(bf16[3,256,896]{2,1,0:T(8,128)(2,1)S(1)} %get-tuple-element.96.own), channel_id=1, source_target_pairs={{0,4},{4,0},{1,5},{5,1},{2,6},{6,2},{3,7},{7,3},{8,12},{12,8},{9,1... | collective-permute-start | bytes 4128776 | tf_op jit(solution)/shard_map/ppermute | solution.py:67
  58.4 15.8 %collective-permute-start.13 = (bf16[4,512,128]{2,1,0:T(8,128)(2,1)S(1)}, bf16[4,512,128]{2,1,0:T(8,128)(2,1)S(1)}, u32[]{:S(2)}, u32[]{:S(2)}) collective-permute-start(bf16[4,512,128]{2,1,0:T(8,128)(2,1)S(1)} %get-tuple-element.90), channel_id=1, source_target_pairs={{0,2},{1,3},{2,0},{3,1},{4,6},{5,7},{6,4},{7,5},{8,10},{9,11},{10,... | collective-permute-start | bytes 1572872 | tf_op jit(solution)/shard_map/ppermute | solution.py:63
  60.2 23.7 %collective-permute-start.15 = (bf16[2,256,896]{2,1,0:T(8,128)(2,1)S(1)}, bf16[2,256,896]{2,1,0:T(8,128)(2,1)S(1)}, u32[]{:S(2)}, u32[]{:S(2)}) collective-permute-start(bf16[2,256,896]{2,1,0:T(8,128)(2,1)S(1)} %get-tuple-element.94.p0), channel_id=1, source_target_pairs={{0,1},{1,2},{2,3},{3,0},{4,7},{5,4},{6,5},{7,6},{8,9},{9,10},{10,1... | collective-permute-start | bytes 2752520 | tf_op jit(solution)/shard_map/ppermute | solution.py:63
  63.7 20.2 %collective-permute-start.16 = (bf16[4,512,128]{2,1,0:T(8,128)(2,1)S(1)}, bf16[4,512,128]{2,1,0:T(8,128)(2,1)S(1)}, u32[]{:S(2)}, u32[]{:S(2)}) collective-permute-start(bf16[4,512,128]{2,1,0:T(8,128)(2,1)S(1)} %get-tuple-element.101), channel_id=1, source_target_pairs={{0,32},{4,12},{8,40},{12,20},{16,48},{20,28},{24,56},{28,4},{32,64... | collective-permute-start | bytes 1572872 | tf_op jit(solution)/shard_map/ppermute | solution.py:54
  65.2 18.7 %collective-permute-start.17 = (bf16[4,512,128]{2,1,0:T(8,128)(2,1)S(1)}, bf16[4,512,128]{2,1,0:T(8,128)(2,1)S(1)}, u32[]{:S(2)}, u32[]{:S(2)}) collective-permute-start(bf16[4,512,128]{2,1,0:T(8,128)(2,1)S(1)} %get-tuple-element.102), channel_id=1, source_target_pairs={{0,96},{4,28},{8,104},{12,4},{16,112},{20,12},{24,120},{28,20},{32... | collective-permute-start | bytes 1572872 | tf_op jit(solution)/shard_map/ppermute | solution.py:54
  67.0 16.9 %collective-permute-start.18 = (bf16[4,512,128]{2,1,0:T(8,128)(2,1)S(1)}, bf16[4,512,128]{2,1,0:T(8,128)(2,1)S(1)}, u32[]{:S(2)}, u32[]{:S(2)}) collective-permute-start(bf16[4,512,128]{2,1,0:T(8,128)(2,1)S(1)} %get-tuple-element.103), channel_id=1, source_target_pairs={{0,64},{4,20},{8,72},{12,28},{16,80},{20,4},{24,88},{28,12},{32,96... | collective-permute-start | bytes 1572872 | tf_op jit(solution)/shard_map/ppermute | solution.py:54
  74.2 19.6 %collective-permute-start.14 = (bf16[2,256,896]{2,1,0:T(8,128)(2,1)S(1)}, bf16[2,256,896]{2,1,0:T(8,128)(2,1)S(1)}, u32[]{:S(2)}, u32[]{:S(2)}) collective-permute-start(bf16[2,256,896]{2,1,0:T(8,128)(2,1)S(1)} %get-tuple-element.91.p1), channel_id=1, source_target_pairs={{0,1},{1,2},{2,3},{3,0},{4,7},{5,4},{6,5},{7,6},{8,9},{9,10},{10,1... | collective-permute-start | bytes 2752520 | tf_op jit(solution)/shard_map/ppermute | solution.py:63
  83.9 19.6 %collective-permute-start.19 = (bf16[224,2048]{1,0:T(8,128)(2,1)S(1)}, bf16[224,2048]{1,0:T(8,128)(2,1)S(1)}, u32[]{:S(2)}, u32[]{:S(2)}) collective-permute-start(bf16[224,2048]{1,0:T(8,128)(2,1)S(1)} %get-tuple-element.105), channel_id=1, source_target_pairs={{0,1},{1,2},{2,3},{3,0},{4,7},{5,4},{6,5},{7,6},{8,9},{9,10},{10,1... | collective-permute-start | bytes 2752520 | tf_op jit(solution)/shard_map/ppermute | solution.py:63
  84.3 29.1 %collective-permute-start.23 = (bf16[2,256,896]{2,1,0:T(8,128)(2,1)S(1)}, bf16[2,256,896]{2,1,0:T(8,128)(2,1)S(1)}, u32[]{:S(2)}, u32[]{:S(2)}) collective-permute-start(bf16[2,256,896]{2,1,0:T(8,128)(2,1)S(1)} %collective-permute-done.15.p2), channel_id=1, source_target_pairs={{0,1},{1,2},{2,3},{3,0},{4,7},{5,4},{6,5},{7,6},{8,9},{9,10},{10,1... | collective-permute-start | bytes 2752520 | tf_op jit(solution)/shard_map/ppermute | solution.py:63
  85.7 19.8 %collective-permute-start.20 = (bf16[4,512,128]{2,1,0:T(8,128)(2,1)S(1)}, bf16[4,512,128]{2,1,0:T(8,128)(2,1)S(1)}, u32[]{:S(2)}, u32[]{:S(2)}) collective-permute-start(bf16[4,512,128]{2,1,0:T(8,128)(2,1)S(1)} %get-tuple-element.111), channel_id=1, source_target_pairs={{0,32},{4,12},{8,40},{12,20},{16,48},{20,28},{24,56},{28,4},{32,64... | collective-permute-start | bytes 1572872 | tf_op jit(solution)/shard_map/ppermute | solution.py:54
  87.1 18.4 %collective-permute-start.21 = (bf16[4,512,128]{2,1,0:T(8,128)(2,1)S(1)}, bf16[4,512,128]{2,1,0:T(8,128)(2,1)S(1)}, u32[]{:S(2)}, u32[]{:S(2)}) collective-permute-start(bf16[4,512,128]{2,1,0:T(8,128)(2,1)S(1)} %get-tuple-element.112), channel_id=1, source_target_pairs={{0,96},{4,28},{8,104},{12,4},{16,112},{20,12},{24,120},{28,20},{32... | collective-permute-start | bytes 1572872 | tf_op jit(solution)/shard_map/ppermute | solution.py:54
  93.7 11.8 %collective-permute-start.22 = (bf16[4,512,128]{2,1,0:T(8,128)(2,1)S(1)}, bf16[4,512,128]{2,1,0:T(8,128)(2,1)S(1)}, u32[]{:S(2)}, u32[]{:S(2)}) collective-permute-start(bf16[4,512,128]{2,1,0:T(8,128)(2,1)S(1)} %get-tuple-element.113), channel_id=1, source_target_pairs={{0,64},{4,20},{8,72},{12,28},{16,80},{20,4},{24,88},{28,12},{32,96... | collective-permute-start | bytes 1572872 | tf_op jit(solution)/shard_map/ppermute | solution.py:54
  113.4 3.1 %collective-permute-start.26 = (bf16[2,256,896]{2,1,0:T(8,128)(2,1)S(1)}, bf16[2,256,896]{2,1,0:T(8,128)(2,1)S(1)}, u32[]{:S(2)}, u32[]{:S(2)}) collective-permute-start(bf16[2,256,896]{2,1,0:T(8,128)(2,1)S(1)} %collective-permute-done.23.p6), channel_id=1, source_target_pairs={{0,4},{4,0},{1,5},{5,1},{2,6},{6,2},{3,7},{7,3},{8,12},{12,8},{9,1... | collective-permute-start | bytes 2752520 | tf_op jit(solution)/shard_map/ppermute | solution.py:67
  113.4 4.6 %collective-permute-start.25 = (bf16[2,256,896]{2,1,0:T(8,128)(2,1)S(1)}, bf16[2,256,896]{2,1,0:T(8,128)(2,1)S(1)}, u32[]{:S(2)}, u32[]{:S(2)}) collective-permute-start(bf16[2,256,896]{2,1,0:T(8,128)(2,1)S(1)} %collective-permute-done.14.p4), channel_id=1, source_target_pairs={{0,4},{4,0},{1,5},{5,1},{2,6},{6,2},{3,7},{7,3},{8,12},{12,8},{9,1... | collective-permute-start | bytes 2752520 | tf_op jit(solution)/shard_map/ppermute | solution.py:67
  113.9 5.9 %collective-permute-start.24 = (bf16[2,256,896]{2,1,0:T(8,128)(2,1)S(1)}, bf16[2,256,896]{2,1,0:T(8,128)(2,1)S(1)}, u32[]{:S(2)}, u32[]{:S(2)}) collective-permute-start(bf16[2,256,896]{2,1,0:T(8,128)(2,1)S(1)} %collective-permute-done.15.p2), channel_id=1, source_target_pairs={{0,4},{4,0},{1,5},{5,1},{2,6},{6,2},{3,7},{7,3},{8,12},{12,8},{9,1... | collective-permute-start | bytes 2752520 | tf_op jit(solution)/shard_map/ppermute | solution.py:67
  113.9 22.8 %collective-permute-start.30 = (bf16[224,2048]{1,0:T(8,128)(2,1)S(1)}, bf16[224,2048]{1,0:T(8,128)(2,1)S(1)}, u32[]{:S(2)}, u32[]{:S(2)}) collective-permute-start(bf16[224,2048]{1,0:T(8,128)(2,1)S(1)} %get-tuple-element.128), channel_id=1, source_target_pairs={{0,3},{1,0},{2,1},{3,2},{4,5},{5,6},{6,7},{7,4},{8,11},{9,8},{10,9... | collective-permute-start | bytes 2752520 | tf_op jit(solution)/shard_map/ppermute | solution.py:63
  115.6 22.2 %collective-permute-start.31 = (bf16[224,2048]{1,0:T(8,128)(2,1)S(1)}, bf16[224,2048]{1,0:T(8,128)(2,1)S(1)}, u32[]{:S(2)}, u32[]{:S(2)}) collective-permute-start(bf16[224,2048]{1,0:T(8,128)(2,1)S(1)} %shard_map.101), channel_id=1, source_target_pairs={{0,1},{1,2},{2,3},{3,0},{4,7},{5,4},{6,5},{7,6},{8,9},{9,10},{10,1... | collective-permute-start | bytes 2752520 | tf_op jit(solution)/shard_map/ppermute | solution.py:63
  116.5 24.3 %collective-permute-start.27 = (bf16[2,512,128]{2,1,0:T(8,128)(2,1)S(1)}, bf16[2,512,128]{2,1,0:T(8,128)(2,1)S(1)}, u32[]{:S(2)}, u32[]{:S(2)}) collective-permute-start(bf16[2,512,128]{2,1,0:T(8,128)(2,1)S(1)} %get-tuple-element.120), channel_id=1, source_target_pairs={{0,8},{4,36},{8,16},{12,44},{16,24},{20,52},{24,0},{28,60},{32,40}... | collective-permute-start | bytes 786440 | tf_op jit(solution)/shard_map/ppermute | solution.py:54
  118.0 22.8 %collective-permute-start.28 = (bf16[2,512,128]{2,1,0:T(8,128)(2,1)S(1)}, bf16[2,512,128]{2,1,0:T(8,128)(2,1)S(1)}, u32[]{:S(2)}, u32[]{:S(2)}) collective-permute-start(bf16[2,512,128]{2,1,0:T(8,128)(2,1)S(1)} %get-tuple-element.121), channel_id=1, source_target_pairs={{0,24},{4,100},{8,0},{12,108},{16,8},{20,116},{24,16},{28,124},{32... | collective-permute-start | bytes 786440 | tf_op jit(solution)/shard_map/ppermute | solution.py:54
  119.8 21.0 %collective-permute-start.29 = (bf16[2,512,128]{2,1,0:T(8,128)(2,1)S(1)}, bf16[2,512,128]{2,1,0:T(8,128)(2,1)S(1)}, u32[]{:S(2)}, u32[]{:S(2)}) collective-permute-start(bf16[2,512,128]{2,1,0:T(8,128)(2,1)S(1)} %get-tuple-element.122), channel_id=1, source_target_pairs={{0,16},{4,68},{8,24},{12,76},{16,0},{20,84},{24,8},{28,92},{32,48}... | collective-permute-start | bytes 786440 | tf_op jit(solution)/shard_map/ppermute | solution.py:54

commit v4 on v3

--- a/solution.py
+++ b/solution.py
@@ -529,53 +529,30 @@
     )(*parts)
 
 
-PARTS = 2
-
-
-def total_body(count, *refs):
-    ins, out, slots, res, sems = refs[:count], refs[count], *refs[count + 1 :]
-    tile = out.shape[0] // PARTS
-    loads, stores = [], []
-    for t in range(PARTS):
-        at = pl.ds(t * tile, tile)
-        loads.append(
-            [
-                pltpu.make_async_copy(ref.at[at], slots.at[n, at], sems.at[t, n])
-                for n, ref in enumerate(ins)
-            ]
-        )
-        stores.append(pltpu.make_async_copy(res.at[at], out.at[at], sems.at[t, count]))
-    for item in loads:
-        start_all(item)
-    for t in range(PARTS):
-        wait_all(loads[t])
-
-        @pl.loop(0, tile // 16)
-        def _(i):
-            rows = pl.ds(pl.multiple_of(t * tile + i * 16, 16), 16)
-            total = slots[0, rows, :].astype(F32)
-            for n in range(1, count):
-                total = total + slots[n, rows, :].astype(F32)
-            res[rows, :] = total.astype(BF)
-
-        stores[t].start()
-    wait_all(stores)
+def total_body(*refs):
+    out = refs[-1]
+    rows = 16
+
+    @pl.loop(0, out.shape[0] // rows)
+    def _(i):
+        at = pl.ds(pl.multiple_of(i * rows, rows), rows)
+        total = refs[0][at, :].astype(F32)
+        for ref in refs[1:-1]:
+            total = total + ref[at, :].astype(F32)
+        out[at, :] = total.astype(BF)
 
 
 def total_of(parts):
     rows, cols = parts[0].shape
-    count = len(parts)
-    return call(
-        functools.partial(total_body, count),
+    return call(
+        total_body,
         (shape((rows, cols)),),
-        (pl.ANY,) * count,
-        [
-            pltpu.VMEM((count, rows, cols), BF),
-            pltpu.VMEM((rows, cols), BF),
-            pltpu.SemaphoreType.DMA((PARTS, count + 1)),
-        ],
-        count * rows * cols,
-        2 * (count + 1) * rows * cols,
+        (VM,) * len(parts),
+        [],
+        len(parts) * rows * cols,
+        2 * (len(parts) + 1) * rows * cols,
+        (VM,),
+        limit=16,
     )(*parts)[0]
 
 
@@ -591,20 +568,20 @@
         plane_shift(k, after(chunk_c, tok_chunks[k]), 1) for k in (1, 2, 3)
     ]
     w_gate, w_up, w_down = slot_weights(w_gate, w_up, w_down)
-    picked = pick(tok_chunks)
-    group1, group2 = depth_shift(1, picked[1]), depth_shift(2, picked[2])
+    picked = pick([after(tok_chunks[0], w_gate)] + tok_chunks[1:])
+    group1, group3 = depth_shift(1, picked[1]), depth_shift(3, picked[3])
 
     keep_gu, send_gu = gate_up([after(tok_chunks[0], picked[0])] + tok_chunks[1:], w_gate, w_up)
     keep_d, send = d_act(
-        [after(cot_chunks[0], group1, group2)] + cot_chunks[1:], w_down, send_gu
+        [after(cot_chunks[0], group1, group3)] + cot_chunks[1:], w_down, send_gu
     )
-    group3 = depth_shift(3, after(picked[3], group1, group2))
+    group2 = depth_shift(2, after(picked[2], group1, group3))
     own, grads_own = hidden(keep_gu, keep_d, swap(send))
     other = swap(own)
     near_own = depth_shift(1, grads_own)
 
     *outs, grads_other = out_parts(own, other, w_down)
-    near_other = depth_shift(1, after(grads_other, group3))
+    near_other = depth_shift(1, after(grads_other, group2))
     blocks = down_parts(own, other, [after(cot_chunks[0], outs[0])] + cot_chunks[1:])
     toks = d_tok_parts(after(own, blocks[0]), other, w_gate, w_up)
 

time: 142 us -> 138 us (0.972)
  Pallas kernels: 35.9 us -> 32.7 us
    ppermute x18, waiting for transfers between devices: 20.1 us -> 15 us  [plane_shift(): return lax.ppermute(array, ('row', 'col'), pairs)]
    ppermute x9, waiting for transfers between devices: 40.2 us -> 44.5 us  [depth_shift(): return lax.ppermute(array, ('col', 'depth'), pairs)]
    pallas_call x2, Pallas kernels: 4.85 us -> 1.6 us  [total_of(): call(total_body, (shape((rows, cols)),), (VM,) * len(parts), [], len(part...]
    ppermute x18, starting transfers between devices: 28.2 us -> 26.4 us  [plane_shift(): return lax.ppermute(array, ('row', 'col'), pairs)]
  transfers between devices with their start and end apart: 32 -> 32, of which waited for: 16 -> 17; matrix products, arithmetic and copies ran while one was open for 0% -> 0% of each run, Pallas kernels for 22% -> 20%
where the time goes in v4:
time: 138 us
  waiting for transfers between devices  63.6 us (46%)
  starting transfers between devices  39.5 us (29%)
  Pallas kernels  32.7 us (24%)
    ppermute x9, waiting for transfers between devices, depth_shift(): return lax.ppermute(array, ('col', 'depth'), pairs)  44.5 us
    ppermute x18, starting transfers between devices, plane_shift(): return lax.ppermute(array, ('row', 'col'), pairs)  26.4 us
    ppermute x18, waiting for transfers between devices, plane_shift(): return lax.ppermute(array, ('row', 'col'), pairs)  15 us
    ppermute x9, starting transfers between devices, depth_shift(): return lax.ppermute(array, ('col', 'depth'), pairs)  12.3 us
    pallas_call x1, Pallas kernels, gate_up(): call(gate_up_body, (shape((2, tok // 2, hid), F32), shape((2, tok // 2, h...  5.64 us
    pallas_call x1, Pallas kernels, weight_grads(): call(grads_body, (shape((feats, hid)),) * 2, (VM,) * 12, [pltpu.VMEM((fea...  5.48 us
    pallas_call x1, Pallas kernels, slot_weights(): call(weights_body, (shape(wg.shape), shape(wu.shape), shape(wd.shape)), (...  4.77 us
    pallas_call x1, Pallas kernels, d_tok_parts(): call(d_tok_body, (shape((G, tok, part)),) * G, (VM,) * 4, [pltpu.VMEM((2,...  4.53 us
  transfers between devices with their start and end apart: 32, of which 17 were waited for; matrix products, arithmetic and copies ran while one was open for 0% of the time, Pallas kernels for 20%

profile of v4, /device:TPU:0, one launch (start us, length us, event | category | flops | bytes accessed | tf_op | source)
XLA Modules:
  0.0 137.6 jit_solution(12582337840943072139)
XLA Ops:
  0.6 1.0 pad_maximum_fusion.p0
  1.6 1.6 %collective-permute-start = (bf16[2,512,128]{2,1,0:T(8,128)(2,1)S(1)}, bf16[2,512,128]{2,1,0:T(8,128)(2,1)S(1)}, u32[]{:S(2)}, u32[]{:S(2)}) collective-permute-start(bf16[2,512,128]{2,1,0:T(8,128)(2,1)S(1)} %pad_maximum_fusion.p0), channel_id=1, source_target_pairs={{0,8},{4,36},{8,16},{12,44},{16,24},{20,52},{24,0},{28,60},{32,40}... | collective-permute-start | bytes 786440 | tf_op jit(solution)/shard_map/ppermute | solution.py:54
  3.3 1.7 %collective-permute-start.1 = (bf16[2,512,128]{2,1,0:T(8,128)(2,1)S(1)}, bf16[2,512,128]{2,1,0:T(8,128)(2,1)S(1)}, u32[]{:S(2)}, u32[]{:S(2)}) collective-permute-start(bf16[2,512,128]{2,1,0:T(8,128)(2,1)S(1)} %pad_maximum_fusion.p0), channel_id=1, source_target_pairs={{0,24},{4,100},{8,0},{12,108},{16,8},{20,116},{24,16},{28,124},{32... | collective-permute-start | bytes 786440 | tf_op jit(solution)/shard_map/ppermute | solution.py:54
  4.9 1.9 %collective-permute-start.2 = (bf16[2,512,128]{2,1,0:T(8,128)(2,1)S(1)}, bf16[2,512,128]{2,1,0:T(8,128)(2,1)S(1)}, u32[]{:S(2)}, u32[]{:S(2)}) collective-permute-start(bf16[2,512,128]{2,1,0:T(8,128)(2,1)S(1)} %pad_maximum_fusion.p0), channel_id=1, source_target_pairs={{0,16},{4,68},{8,24},{12,76},{16,0},{20,84},{24,8},{28,92},{32,48}... | collective-permute-start | bytes 786440 | tf_op jit(solution)/shard_map/ppermute | solution.py:54
  6.8 2.4 %collective-permute-done.p1 = bf16[2,512,128]{2,1,0:T(8,128)(2,1)S(1)} collective-permute-done((bf16[2,512,128]{2,1,0:T(8,128)(2,1)S(1)}, bf16[2,512,128]{2,1,0:T(8,128)(2,1)S(1)}, u32[]{:S(2)}, u32[]{:S(2)}) %collective-permute-start) | collective-permute-done | bytes 262176 | tf_op jit(solution)/shard_map/ppermute | solution.py:54
  9.6 3.5 %collective-permute-done.2.p3 = bf16[2,512,128]{2,1,0:T(8,128)(2,1)S(1)} collective-permute-done((bf16[2,512,128]{2,1,0:T(8,128)(2,1)S(1)}, bf16[2,512,128]{2,1,0:T(8,128)(2,1)S(1)}, u32[]{:S(2)}, u32[]{:S(2)}) %collective-permute-start.2) | collective-permute-done | bytes 262176 | tf_op jit(solution)/shard_map/ppermute | solution.py:54
  13.3 1.6 %collective-permute-start.3 = (bf16[4,512,128]{2,1,0:T(8,128)(2,1)S(1)}, bf16[4,512,128]{2,1,0:T(8,128)(2,1)S(1)}, u32[]{:S(2)}, u32[]{:S(2)}) collective-permute-start(bf16[4,512,128]{2,1,0:T(8,128)(2,1)S(1)} %get-tuple-element.72.c0.t0), channel_id=1, source_target_pairs={{0,32},{4,12},{8,40},{12,20},{16,48},{20,28},{24,56},{28,4},{32,64... | collective-permute-start | bytes 1572872 | tf_op jit(solution)/shard_map/ppermute | solution.py:54
  14.9 1.7 %collective-permute-start.4 = (bf16[4,512,128]{2,1,0:T(8,128)(2,1)S(1)}, bf16[4,512,128]{2,1,0:T(8,128)(2,1)S(1)}, u32[]{:S(2)}, u32[]{:S(2)}) collective-permute-start(bf16[4,512,128]{2,1,0:T(8,128)(2,1)S(1)} %get-tuple-element.72.c0.t0), channel_id=1, source_target_pairs={{0,96},{4,28},{8,104},{12,4},{16,112},{20,12},{24,120},{28,20},{32... | collective-permute-start | bytes 1572872 | tf_op jit(solution)/shard_map/ppermute | solution.py:54
  16.6 2.0 %collective-permute-start.5 = (bf16[4,512,128]{2,1,0:T(8,128)(2,1)S(1)}, bf16[4,512,128]{2,1,0:T(8,128)(2,1)S(1)}, u32[]{:S(2)}, u32[]{:S(2)}) collective-permute-start(bf16[4,512,128]{2,1,0:T(8,128)(2,1)S(1)} %get-tuple-element.72.c0.t0), channel_id=1, source_target_pairs={{0,64},{4,20},{8,72},{12,28},{16,80},{20,4},{24,88},{28,12},{32,96... | collective-permute-start | bytes 1572872 | tf_op jit(solution)/shard_map/ppermute | solution.py:54
  18.6 4.8 %shard_map.93 = (bf16[2048,896]{1,0:T(8,128)(2,1)S(1)}, bf16[2048,896]{1,0:T(8,128)(2,1)S(1)}, bf16[896,2048]{1,0:T(8,128)(2,1)S(1)}) custom-call(bf16[2048,896]{1,0:T(8,128)(2,1)} %wg.1, bf16[2048,896]{1,0:T(8,128)(2,1)} %wu.1, bf16[896,2048]{1,0:T(8,128)(2,1)} %wd.1), custom_call_target="tpu_custom_call" | custom-call | bytes 440401 | tf_op jit(solution)/shard_map/pallas_call | solution.py:238
  24.1 6.5 %collective-permute-done.5.c3.t3 = bf16[4,512,128]{2,1,0:T(8,128)(2,1)S(1)} collective-permute-done((bf16[4,512,128]{2,1,0:T(8,128)(2,1)S(1)}, bf16[4,512,128]{2,1,0:T(8,128)(2,1)S(1)}, u32[]{:S(2)}, u32[]{:S(2)}) %collective-permute-start.5) | collective-permute-done | bytes 524320 | tf_op jit(solution)/shard_map/ppermute | solution.py:54
  30.9 2.0 %collective-permute-start.6 = (bf16[4,512,128]{2,1,0:T(8,128)(2,1)S(1)}, bf16[4,512,128]{2,1,0:T(8,128)(2,1)S(1)}, u32[]{:S(2)}, u32[]{:S(2)}) collective-permute-start(bf16[4,512,128]{2,1,0:T(8,128)(2,1)S(1)} %get-tuple-element.76), channel_id=1, source_target_pairs={{0,1},{1,2},{2,3},{3,0},{4,7},{5,4},{6,5},{7,6},{8,9},{9,10},{10,1... | collective-permute-start | bytes 1572872 | tf_op jit(solution)/shard_map/ppermute | solution.py:63
  32.9 3.6 %collective-permute-start.7 = (bf16[4,512,128]{2,1,0:T(8,128)(2,1)S(1)}, bf16[4,512,128]{2,1,0:T(8,128)(2,1)S(1)}, u32[]{:S(2)}, u32[]{:S(2)}) collective-permute-start(bf16[4,512,128]{2,1,0:T(8,128)(2,1)S(1)} %get-tuple-element.77), channel_id=1, source_target_pairs={{0,2},{1,3},{2,0},{3,1},{4,6},{5,7},{6,4},{7,5},{8,10},{9,11},{10,... | collective-permute-start | bytes 1572872 | tf_op jit(solution)/shard_map/ppermute | solution.py:63
  36.5 0.7 collective-permute-start.10
  37.2 2.1 %collective-permute-start.8 = (bf16[4,512,128]{2,1,0:T(8,128)(2,1)S(1)}, bf16[4,512,128]{2,1,0:T(8,128)(2,1)S(1)}, u32[]{:S(2)}, u32[]{:S(2)}) collective-permute-start(bf16[4,512,128]{2,1,0:T(8,128)(2,1)S(1)} %get-tuple-element.88.c0), channel_id=1, source_target_pairs={{0,32},{4,12},{8,40},{12,20},{16,48},{20,28},{24,56},{28,4},{32,64... | collective-permute-start | bytes 1572872 | tf_op jit(solution)/shard_map/ppermute | solution.py:54
  39.4 1.2 collective-permute-start.9
  40.6 5.6 %shard_map.95 = (f32[2,256,896]{2,1,0:T(8,128)S(1)}, bf16[2,256,896]{2,1,0:T(8,128)(2,1)S(1)}) custom-call(bf16[4,512,128]{2,1,0:T(8,128)(2,1)S(1)} %get-tuple-element.72.c0.t0, bf16[4,512,128]{2,1,0:T(8,128)(2,1)S(1)} %collective-permute-done.3.c1.t1, bf16[4,512,128]{2,1,0:T(8,128)(2,1)S(1)} %collective-permute-done.4.c2.t2, ...), custom_call_target="tpu_custom_call" | custom-call | flops 75161928 | bytes 146800 | tf_op jit(solution)/shard_map/pallas_call | solution.py:277
  46.3 8.6 %collective-permute-done.7.t3 = bf16[4,512,128]{2,1,0:T(8,128)(2,1)S(1)} collective-permute-done((bf16[4,512,128]{2,1,0:T(8,128)(2,1)S(1)}, bf16[4,512,128]{2,1,0:T(8,128)(2,1)S(1)}, u32[]{:S(2)}, u32[]{:S(2)}) %collective-permute-start.7) | collective-permute-done | bytes 524320 | tf_op jit(solution)/shard_map/ppermute | solution.py:63
  54.9 2.7 %shard_map.96 = (f32[256,896]{1,0:T(8,128)S(1)}, bf16[3,256,896]{2,1,0:T(8,128)(2,1)S(1)}) custom-call(bf16[4,512,128]{2,1,0:T(8,128)(2,1)S(1)} %get-tuple-element.88.c0, bf16[4,512,128]{2,1,0:T(8,128)(2,1)S(1)} %collective-permute-done.8.c1, bf16[4,512,128]{2,1,0:T(8,128)(2,1)S(1)} %collective-permute-done.9.c2, ...), custom_call_target="tpu_custom_call" | custom-call | flops 37580964 | bytes 73400 | tf_op jit(solution)/shard_map/pallas_call | solution.py:315
  57.7 3.1 %collective-permute-done.11.recv = bf16[3,256,896]{2,1,0:T(8,128)(2,1)S(1)} collective-permute-done((bf16[3,256,896]{2,1,0:T(8,128)(2,1)S(1)}, bf16[3,256,896]{2,1,0:T(8,128)(2,1)S(1)}, u32[]{:S(2)}, u32[]{:S(2)}) %collective-permute-start.11) | collective-permute-done | bytes 1376288 | tf_op jit(solution)/shard_map/ppermute | solution.py:67
  60.8 0.8 shard_map.97
  61.8 1.2 collective-permute-start.13
  63.0 0.9 collective-permute-start.15
  63.9 0.9 collective-permute-done.12.other
  64.8 2.4 %shard_map.98 = (bf16[4,512,128]{2,1,0:T(8,128)(2,1)S(1)}, bf16[4,512,128]{2,1,0:T(8,128)(2,1)S(1)}, bf16[4,512,128]{2,1,0:T(8,128)(2,1)S(1)}, bf16[4,512,128]{2,1,0:T(8,128)(2,1)S(1)}, bf16[2,256,896]{2,1,0:T(8,128)(2,1)S(1)}) custom-call(bf16[3,256,896]{2,1,0:T(8,128)(2,1)S(1)} %get-tuple-element.98.own, ...), custom_call_target="tpu_custom_call" | custom-call | flops 37580964 | bytes 73400 | tf_op jit(solution)/shard_map/pallas_call | solution.py:383
  67.2 1.5 %collective-permute-start.16 = (bf16[4,512,128]{2,1,0:T(8,128)(2,1)S(1)}, bf16[4,512,128]{2,1,0:T(8,128)(2,1)S(1)}, u32[]{:S(2)}, u32[]{:S(2)}) collective-permute-start(bf16[4,512,128]{2,1,0:T(8,128)(2,1)S(1)} %get-tuple-element.103), channel_id=1, source_target_pairs={{0,32},{4,12},{8,40},{12,20},{16,48},{20,28},{24,56},{28,4},{32,64... | collective-permute-start | bytes 1572872 | tf_op jit(solution)/shard_map/ppermute | solution.py:54
  68.7 1.8 %collective-permute-start.17 = (bf16[4,512,128]{2,1,0:T(8,128)(2,1)S(1)}, bf16[4,512,128]{2,1,0:T(8,128)(2,1)S(1)}, u32[]{:S(2)}, u32[]{:S(2)}) collective-permute-start(bf16[4,512,128]{2,1,0:T(8,128)(2,1)S(1)} %get-tuple-element.104), channel_id=1, source_target_pairs={{0,96},{4,28},{8,104},{12,4},{16,112},{20,12},{24,120},{28,20},{32... | collective-permute-start | bytes 1572872 | tf_op jit(solution)/shard_map/ppermute | solution.py:54
  70.8 5.7 %collective-permute-done.13.t2 = bf16[4,512,128]{2,1,0:T(8,128)(2,1)S(1)} collective-permute-done((bf16[4,512,128]{2,1,0:T(8,128)(2,1)S(1)}, bf16[4,512,128]{2,1,0:T(8,128)(2,1)S(1)}, u32[]{:S(2)}, u32[]{:S(2)}) %collective-permute-start.13) | collective-permute-done | bytes 524320 | tf_op jit(solution)/shard_map/ppermute | solution.py:63
  76.6 3.0 %shard_map.99 = (bf16[224,2048]{1,0:T(8,128)(2,1)S(1)}, bf16[224,2048]{1,0:T(8,128)(2,1)S(1)}, bf16[224,2048]{1,0:T(8,128)(2,1)S(1)}, bf16[224,2048]{1,0:T(8,128)(2,1)S(1)}) custom-call(bf16[3,256,896]{2,1,0:T(8,128)(2,1)S(1)} %get-tuple-element.98.own, bf16[3,256,896]{2,1,0:T(8,128)(2,1)S(1)} %collective-permute-done.12.other, ...), custom_call_target="tpu_custom_call" | custom-call | flops 37580964 | bytes 41943 | tf_op jit(solution)/shard_map/pallas_call | solution.py:449
  79.6 4.5 %shard_map.100 = (bf16[4,512,128]{2,1,0:T(8,128)(2,1)S(1)}, bf16[4,512,128]{2,1,0:T(8,128)(2,1)S(1)}, bf16[4,512,128]{2,1,0:T(8,128)(2,1)S(1)}, bf16[4,512,128]{2,1,0:T(8,128)(2,1)S(1)}) custom-call(bf16[3,256,896]{2,1,0:T(8,128)(2,1)S(1)} %get-tuple-element.98.own, bf16[3,256,896]{2,1,0:T(8,128)(2,1)S(1)} %collective-permute-done.12.other, ...), custom_call_target="tpu_custom_call" | custom-call | flops 75161928 | bytes 146800 | tf_op jit(solution)/shard_map/pallas_call | solution.py:415
  84.3 2.6 %collective-permute-start.23 = (bf16[2,256,896]{2,1,0:T(8,128)(2,1)S(1)}, bf16[2,256,896]{2,1,0:T(8,128)(2,1)S(1)}, u32[]{:S(2)}, u32[]{:S(2)}) collective-permute-start(bf16[2,256,896]{2,1,0:T(8,128)(2,1)S(1)} %collective-permute-done.15.p2), channel_id=1, source_target_pairs={{0,1},{1,2},{2,3},{3,0},{4,7},{5,4},{6,5},{7,6},{8,9},{9,10},{10,1... | collective-permute-start | bytes 2752520 | tf_op jit(solution)/shard_map/ppermute | solution.py:63
  87.1 3.0 %collective-permute-start.21 = (bf16[4,512,128]{2,1,0:T(8,128)(2,1)S(1)}, bf16[4,512,128]{2,1,0:T(8,128)(2,1)S(1)}, u32[]{:S(2)}, u32[]{:S(2)}) collective-permute-start(bf16[4,512,128]{2,1,0:T(8,128)(2,1)S(1)} %get-tuple-element.114), channel_id=1, source_target_pairs={{0,96},{4,28},{8,104},{12,4},{16,112},{20,12},{24,120},{28,20},{32... | collective-permute-start | bytes 1572872 | tf_op jit(solution)/shard_map/ppermute | solution.py:54
  90.1 1.2 collective-permute-done.14.p4
  91.3 0.7 collective-permute-start.22
  92.0 9.1 %collective-permute-done.19.refs_1_ = bf16[224,2048]{1,0:T(8,128)(2,1)S(1)} collective-permute-done((bf16[224,2048]{1,0:T(8,128)(2,1)S(1)}, bf16[224,2048]{1,0:T(8,128)(2,1)S(1)}, u32[]{:S(2)}, u32[]{:S(2)}) %collective-permute-start.19) | collective-permute-done | bytes 917536 | tf_op jit(solution)/shard_map/ppermute | solution.py:63
  101.4 1.0 collective-permute-done.21.b2
  102.9 8.1 %collective-permute-done.23.p6 = bf16[2,256,896]{2,1,0:T(8,128)(2,1)S(1)} collective-permute-done((bf16[2,256,896]{2,1,0:T(8,128)(2,1)S(1)}, bf16[2,256,896]{2,1,0:T(8,128)(2,1)S(1)}, u32[]{:S(2)}, u32[]{:S(2)}) %collective-permute-start.23) | collective-permute-done | bytes 917536 | tf_op jit(solution)/shard_map/ppermute | solution.py:63
  111.0 0.5 collective-permute-start.25
  111.5 1.6 %collective-permute-start.30 = (bf16[224,2048]{1,0:T(8,128)(2,1)S(1)}, bf16[224,2048]{1,0:T(8,128)(2,1)S(1)}, u32[]{:S(2)}, u32[]{:S(2)}) collective-permute-start(bf16[224,2048]{1,0:T(8,128)(2,1)S(1)} %get-tuple-element.130), channel_id=1, source_target_pairs={{0,3},{1,0},{2,1},{3,2},{4,5},{5,6},{6,7},{7,4},{8,11},{9,8},{10,9... | collective-permute-start | bytes 2752520 | tf_op jit(solution)/shard_map/ppermute | solution.py:63
  113.5 0.5 shard_map.102
  114.0 1.7 %collective-permute-start.27 = (bf16[2,512,128]{2,1,0:T(8,128)(2,1)S(1)}, bf16[2,512,128]{2,1,0:T(8,128)(2,1)S(1)}, u32[]{:S(2)}, u32[]{:S(2)}) collective-permute-start(bf16[2,512,128]{2,1,0:T(8,128)(2,1)S(1)} %get-tuple-element.122), channel_id=1, source_target_pairs={{0,8},{4,36},{8,16},{12,44},{16,24},{20,52},{24,0},{28,60},{32,40}... | collective-permute-start | bytes 786440 | tf_op jit(solution)/shard_map/ppermute | solution.py:54
  115.7 1.8 %collective-permute-start.28 = (bf16[2,512,128]{2,1,0:T(8,128)(2,1)S(1)}, bf16[2,512,128]{2,1,0:T(8,128)(2,1)S(1)}, u32[]{:S(2)}, u32[]{:S(2)}) collective-permute-start(bf16[2,512,128]{2,1,0:T(8,128)(2,1)S(1)} %get-tuple-element.123), channel_id=1, source_target_pairs={{0,24},{4,100},{8,0},{12,108},{16,8},{20,116},{24,16},{28,124},{32... | collective-permute-start | bytes 786440 | tf_op jit(solution)/shard_map/ppermute | solution.py:54
  117.6 0.7 collective-permute-start.29
  118.2 5.5 %shard_map.103 = (bf16[512,896]{1,0:T(8,128)(2,1)}, bf16[512,896]{1,0:T(8,128)(2,1)}) custom-call(bf16[4,512,128]{2,1,0:T(8,128)(2,1)S(1)} %get-tuple-element.71.t0, bf16[4,512,128]{2,1,0:T(8,128)(2,1)S(1)} %collective-permute-done.6.t1, bf16[4,512,128]{2,1,0:T(8,128)(2,1)S(1)} %collective-permute-done.13.t2, ...), custom_call_target="tpu_custom_call" | custom-call | flops 75161928 | bytes 91750 | tf_op jit(solution)/shard_map/pallas_call | solution.py:479
  123.7 10.5 %collective-permute-done.30.refs_1_ = bf16[224,2048]{1,0:T(8,128)(2,1)S(1)} collective-permute-done((bf16[224,2048]{1,0:T(8,128)(2,1)S(1)}, bf16[224,2048]{1,0:T(8,128)(2,1)S(1)}, u32[]{:S(2)}, u32[]{:S(2)}) %collective-permute-start.30) | collective-permute-done | bytes 917536 | tf_op jit(solution)/shard_map/ppermute | solution.py:63
  134.2 1.2 collective-permute-done.31.refs_2_
  135.4 1.3 shard_map.105
  136.8 0.8 shard_map.104
  (31 shorter events, 3.8 us)
Async XLA Ops:
  1.6 7.7 %collective-permute-start = (bf16[2,512,128]{2,1,0:T(8,128)(2,1)S(1)}, bf16[2,512,128]{2,1,0:T(8,128)(2,1)S(1)}, u32[]{:S(2)}, u32[]{:S(2)}) collective-permute-start(bf16[2,512,128]{2,1,0:T(8,128)(2,1)S(1)} %pad_maximum_fusion.p0), channel_id=1, source_target_pairs={{0,8},{4,36},{8,16},{12,44},{16,24},{20,52},{24,0},{28,60},{32,40}... | collective-permute-start | bytes 786440 | tf_op jit(solution)/shard_map/ppermute | solution.py:54
  3.3 6.4 %collective-permute-start.1 = (bf16[2,512,128]{2,1,0:T(8,128)(2,1)S(1)}, bf16[2,512,128]{2,1,0:T(8,128)(2,1)S(1)}, u32[]{:S(2)}, u32[]{:S(2)}) collective-permute-start(bf16[2,512,128]{2,1,0:T(8,128)(2,1)S(1)} %pad_maximum_fusion.p0), channel_id=1, source_target_pairs={{0,24},{4,100},{8,0},{12,108},{16,8},{20,116},{24,16},{28,124},{32... | collective-permute-start | bytes 786440 | tf_op jit(solution)/shard_map/ppermute | solution.py:54
  4.9 8.2 %collective-permute-start.2 = (bf16[2,512,128]{2,1,0:T(8,128)(2,1)S(1)}, bf16[2,512,128]{2,1,0:T(8,128)(2,1)S(1)}, u32[]{:S(2)}, u32[]{:S(2)}) collective-permute-start(bf16[2,512,128]{2,1,0:T(8,128)(2,1)S(1)} %pad_maximum_fusion.p0), channel_id=1, source_target_pairs={{0,16},{4,68},{8,24},{12,76},{16,0},{20,84},{24,8},{28,92},{32,48}... | collective-permute-start | bytes 786440 | tf_op jit(solution)/shard_map/ppermute | solution.py:54
  13.3 10.5 %collective-permute-start.3 = (bf16[4,512,128]{2,1,0:T(8,128)(2,1)S(1)}, bf16[4,512,128]{2,1,0:T(8,128)(2,1)S(1)}, u32[]{:S(2)}, u32[]{:S(2)}) collective-permute-start(bf16[4,512,128]{2,1,0:T(8,128)(2,1)S(1)} %get-tuple-element.72.c0.t0), channel_id=1, source_target_pairs={{0,32},{4,12},{8,40},{12,20},{16,48},{20,28},{24,56},{28,4},{32,64... | collective-permute-start | bytes 1572872 | tf_op jit(solution)/shard_map/ppermute | solution.py:54
  14.9 9.2 %collective-permute-start.4 = (bf16[4,512,128]{2,1,0:T(8,128)(2,1)S(1)}, bf16[4,512,128]{2,1,0:T(8,128)(2,1)S(1)}, u32[]{:S(2)}, u32[]{:S(2)}) collective-permute-start(bf16[4,512,128]{2,1,0:T(8,128)(2,1)S(1)} %get-tuple-element.72.c0.t0), channel_id=1, source_target_pairs={{0,96},{4,28},{8,104},{12,4},{16,112},{20,12},{24,120},{28,20},{32... | collective-permute-start | bytes 1572872 | tf_op jit(solution)/shard_map/ppermute | solution.py:54
  16.6 14.0 %collective-permute-start.5 = (bf16[4,512,128]{2,1,0:T(8,128)(2,1)S(1)}, bf16[4,512,128]{2,1,0:T(8,128)(2,1)S(1)}, u32[]{:S(2)}, u32[]{:S(2)}) collective-permute-start(bf16[4,512,128]{2,1,0:T(8,128)(2,1)S(1)} %get-tuple-element.72.c0.t0), channel_id=1, source_target_pairs={{0,64},{4,20},{8,72},{12,28},{16,80},{20,4},{24,88},{28,12},{32,96... | collective-permute-start | bytes 1572872 | tf_op jit(solution)/shard_map/ppermute | solution.py:54
  30.9 15.3 %collective-permute-start.6 = (bf16[4,512,128]{2,1,0:T(8,128)(2,1)S(1)}, bf16[4,512,128]{2,1,0:T(8,128)(2,1)S(1)}, u32[]{:S(2)}, u32[]{:S(2)}) collective-permute-start(bf16[4,512,128]{2,1,0:T(8,128)(2,1)S(1)} %get-tuple-element.76), channel_id=1, source_target_pairs={{0,1},{1,2},{2,3},{3,0},{4,7},{5,4},{6,5},{7,6},{8,9},{9,10},{10,1... | collective-permute-start | bytes 1572872 | tf_op jit(solution)/shard_map/ppermute | solution.py:63
  32.9 22.0 %collective-permute-start.7 = (bf16[4,512,128]{2,1,0:T(8,128)(2,1)S(1)}, bf16[4,512,128]{2,1,0:T(8,128)(2,1)S(1)}, u32[]{:S(2)}, u32[]{:S(2)}) collective-permute-start(bf16[4,512,128]{2,1,0:T(8,128)(2,1)S(1)} %get-tuple-element.77), channel_id=1, source_target_pairs={{0,2},{1,3},{2,0},{3,1},{4,6},{5,7},{6,4},{7,5},{8,10},{9,11},{10,... | collective-permute-start | bytes 1572872 | tf_op jit(solution)/shard_map/ppermute | solution.py:63
  36.5 18.4 %collective-permute-start.10 = (bf16[4,512,128]{2,1,0:T(8,128)(2,1)S(1)}, bf16[4,512,128]{2,1,0:T(8,128)(2,1)S(1)}, u32[]{:S(2)}, u32[]{:S(2)}) collective-permute-start(bf16[4,512,128]{2,1,0:T(8,128)(2,1)S(1)} %get-tuple-element.88.c0), channel_id=1, source_target_pairs={{0,64},{4,20},{8,72},{12,28},{16,80},{20,4},{24,88},{28,12},{32,96... | collective-permute-start | bytes 1572872 | tf_op jit(solution)/shard_map/ppermute | solution.py:54
  37.2 17.7 %collective-permute-start.8 = (bf16[4,512,128]{2,1,0:T(8,128)(2,1)S(1)}, bf16[4,512,128]{2,1,0:T(8,128)(2,1)S(1)}, u32[]{:S(2)}, u32[]{:S(2)}) collective-permute-start(bf16[4,512,128]{2,1,0:T(8,128)(2,1)S(1)} %get-tuple-element.88.c0), channel_id=1, source_target_pairs={{0,32},{4,12},{8,40},{12,20},{16,48},{20,28},{24,56},{28,4},{32,64... | collective-permute-start | bytes 1572872 | tf_op jit(solution)/shard_map/ppermute | solution.py:54
  39.4 15.5 %collective-permute-start.9 = (bf16[4,512,128]{2,1,0:T(8,128)(2,1)S(1)}, bf16[4,512,128]{2,1,0:T(8,128)(2,1)S(1)}, u32[]{:S(2)}, u32[]{:S(2)}) collective-permute-start(bf16[4,512,128]{2,1,0:T(8,128)(2,1)S(1)} %get-tuple-element.88.c0), channel_id=1, source_target_pairs={{0,96},{4,28},{8,104},{12,4},{16,112},{20,12},{24,120},{28,20},{32... | collective-permute-start | bytes 1572872 | tf_op jit(solution)/shard_map/ppermute | solution.py:54
  57.6 3.2 %collective-permute-start.11 = (bf16[3,256,896]{2,1,0:T(8,128)(2,1)S(1)}, bf16[3,256,896]{2,1,0:T(8,128)(2,1)S(1)}, u32[]{:S(2)}, u32[]{:S(2)}) collective-permute-start(bf16[3,256,896]{2,1,0:T(8,128)(2,1)S(1)} %get-tuple-element.85), channel_id=1, source_target_pairs={{0,4},{4,0},{1,5},{5,1},{2,6},{6,2},{3,7},{7,3},{8,12},{12,8},{9,1... | collective-permute-start | bytes 4128776 | tf_op jit(solution)/shard_map/ppermute | solution.py:67
  61.6 3.2 %collective-permute-start.12 = (bf16[3,256,896]{2,1,0:T(8,128)(2,1)S(1)}, bf16[3,256,896]{2,1,0:T(8,128)(2,1)S(1)}, u32[]{:S(2)}, u32[]{:S(2)}) collective-permute-start(bf16[3,256,896]{2,1,0:T(8,128)(2,1)S(1)} %get-tuple-element.98.own), channel_id=1, source_target_pairs={{0,4},{4,0},{1,5},{5,1},{2,6},{6,2},{3,7},{7,3},{8,12},{12,8},{9,1... | collective-permute-start | bytes 4128776 | tf_op jit(solution)/shard_map/ppermute | solution.py:67
  61.8 14.8 %collective-permute-start.13 = (bf16[4,512,128]{2,1,0:T(8,128)(2,1)S(1)}, bf16[4,512,128]{2,1,0:T(8,128)(2,1)S(1)}, u32[]{:S(2)}, u32[]{:S(2)}) collective-permute-start(bf16[4,512,128]{2,1,0:T(8,128)(2,1)S(1)} %get-tuple-element.92), channel_id=1, source_target_pairs={{0,3},{1,0},{2,1},{3,2},{4,5},{5,6},{6,7},{7,4},{8,11},{9,8},{10,9... | collective-permute-start | bytes 1572872 | tf_op jit(solution)/shard_map/ppermute | solution.py:63
  63.0 21.2 %collective-permute-start.15 = (bf16[2,256,896]{2,1,0:T(8,128)(2,1)S(1)}, bf16[2,256,896]{2,1,0:T(8,128)(2,1)S(1)}, u32[]{:S(2)}, u32[]{:S(2)}) collective-permute-start(bf16[2,256,896]{2,1,0:T(8,128)(2,1)S(1)} %get-tuple-element.96.p0), channel_id=1, source_target_pairs={{0,1},{1,2},{2,3},{3,0},{4,7},{5,4},{6,5},{7,6},{8,9},{9,10},{10,1... | collective-permute-start | bytes 2752520 | tf_op jit(solution)/shard_map/ppermute | solution.py:63
  67.2 17.0 %collective-permute-start.16 = (bf16[4,512,128]{2,1,0:T(8,128)(2,1)S(1)}, bf16[4,512,128]{2,1,0:T(8,128)(2,1)S(1)}, u32[]{:S(2)}, u32[]{:S(2)}) collective-permute-start(bf16[4,512,128]{2,1,0:T(8,128)(2,1)S(1)} %get-tuple-element.103), channel_id=1, source_target_pairs={{0,32},{4,12},{8,40},{12,20},{16,48},{20,28},{24,56},{28,4},{32,64... | collective-permute-start | bytes 1572872 | tf_op jit(solution)/shard_map/ppermute | solution.py:54
  68.7 15.5 %collective-permute-start.17 = (bf16[4,512,128]{2,1,0:T(8,128)(2,1)S(1)}, bf16[4,512,128]{2,1,0:T(8,128)(2,1)S(1)}, u32[]{:S(2)}, u32[]{:S(2)}) collective-permute-start(bf16[4,512,128]{2,1,0:T(8,128)(2,1)S(1)} %get-tuple-element.104), channel_id=1, source_target_pairs={{0,96},{4,28},{8,104},{12,4},{16,112},{20,12},{24,120},{28,20},{32... | collective-permute-start | bytes 1572872 | tf_op jit(solution)/shard_map/ppermute | solution.py:54
  70.5 13.7 %collective-permute-start.18 = (bf16[4,512,128]{2,1,0:T(8,128)(2,1)S(1)}, bf16[4,512,128]{2,1,0:T(8,128)(2,1)S(1)}, u32[]{:S(2)}, u32[]{:S(2)}) collective-permute-start(bf16[4,512,128]{2,1,0:T(8,128)(2,1)S(1)} %get-tuple-element.105), channel_id=1, source_target_pairs={{0,64},{4,20},{8,72},{12,28},{16,80},{20,4},{24,88},{28,12},{32,96... | collective-permute-start | bytes 1572872 | tf_op jit(solution)/shard_map/ppermute | solution.py:54
  76.6 14.7 %collective-permute-start.14 = (bf16[2,256,896]{2,1,0:T(8,128)(2,1)S(1)}, bf16[2,256,896]{2,1,0:T(8,128)(2,1)S(1)}, u32[]{:S(2)}, u32[]{:S(2)}) collective-permute-start(bf16[2,256,896]{2,1,0:T(8,128)(2,1)S(1)} %get-tuple-element.93.p1), channel_id=1, source_target_pairs={{0,1},{1,2},{2,3},{3,0},{4,7},{5,4},{6,5},{7,6},{8,9},{9,10},{10,1... | collective-permute-start | bytes 2752520 | tf_op jit(solution)/shard_map/ppermute | solution.py:63
  84.2 16.9 %collective-permute-start.19 = (bf16[224,2048]{1,0:T(8,128)(2,1)S(1)}, bf16[224,2048]{1,0:T(8,128)(2,1)S(1)}, u32[]{:S(2)}, u32[]{:S(2)}) collective-permute-start(bf16[224,2048]{1,0:T(8,128)(2,1)S(1)} %get-tuple-element.107), channel_id=1, source_target_pairs={{0,1},{1,2},{2,3},{3,0},{4,7},{5,4},{6,5},{7,6},{8,9},{9,10},{10,1... | collective-permute-start | bytes 2752520 | tf_op jit(solution)/shard_map/ppermute | solution.py:63
  84.3 26.7 %collective-permute-start.23 = (bf16[2,256,896]{2,1,0:T(8,128)(2,1)S(1)}, bf16[2,256,896]{2,1,0:T(8,128)(2,1)S(1)}, u32[]{:S(2)}, u32[]{:S(2)}) collective-permute-start(bf16[2,256,896]{2,1,0:T(8,128)(2,1)S(1)} %collective-permute-done.15.p2), channel_id=1, source_target_pairs={{0,1},{1,2},{2,3},{3,0},{4,7},{5,4},{6,5},{7,6},{8,9},{9,10},{10,1... | collective-permute-start | bytes 2752520 | tf_op jit(solution)/shard_map/ppermute | solution.py:63
  86.9 14.6 %collective-permute-start.20 = (bf16[4,512,128]{2,1,0:T(8,128)(2,1)S(1)}, bf16[4,512,128]{2,1,0:T(8,128)(2,1)S(1)}, u32[]{:S(2)}, u32[]{:S(2)}) collective-permute-start(bf16[4,512,128]{2,1,0:T(8,128)(2,1)S(1)} %get-tuple-element.113), channel_id=1, source_target_pairs={{0,32},{4,12},{8,40},{12,20},{16,48},{20,28},{24,56},{28,4},{32,64... | collective-permute-start | bytes 1572872 | tf_op jit(solution)/shard_map/ppermute | solution.py:54
  87.1 15.3 %collective-permute-start.21 = (bf16[4,512,128]{2,1,0:T(8,128)(2,1)S(1)}, bf16[4,512,128]{2,1,0:T(8,128)(2,1)S(1)}, u32[]{:S(2)}, u32[]{:S(2)}) collective-permute-start(bf16[4,512,128]{2,1,0:T(8,128)(2,1)S(1)} %get-tuple-element.114), channel_id=1, source_target_pairs={{0,96},{4,28},{8,104},{12,4},{16,112},{20,12},{24,120},{28,20},{32... | collective-permute-start | bytes 1572872 | tf_op jit(solution)/shard_map/ppermute | solution.py:54
  91.3 11.6 %collective-permute-start.22 = (bf16[4,512,128]{2,1,0:T(8,128)(2,1)S(1)}, bf16[4,512,128]{2,1,0:T(8,128)(2,1)S(1)}, u32[]{:S(2)}, u32[]{:S(2)}) collective-permute-start(bf16[4,512,128]{2,1,0:T(8,128)(2,1)S(1)} %get-tuple-element.115), channel_id=1, source_target_pairs={{0,64},{4,20},{8,72},{12,28},{16,80},{20,4},{24,88},{28,12},{32,96... | collective-permute-start | bytes 1572872 | tf_op jit(solution)/shard_map/ppermute | solution.py:54
  111.0 3.1 %collective-permute-start.26 = (bf16[2,256,896]{2,1,0:T(8,128)(2,1)S(1)}, bf16[2,256,896]{2,1,0:T(8,128)(2,1)S(1)}, u32[]{:S(2)}, u32[]{:S(2)}) collective-permute-start(bf16[2,256,896]{2,1,0:T(8,128)(2,1)S(1)} %collective-permute-done.23.p6), channel_id=1, source_target_pairs={{0,4},{4,0},{1,5},{5,1},{2,6},{6,2},{3,7},{7,3},{8,12},{12,8},{9,1... | collective-permute-start | bytes 2752520 | tf_op jit(solution)/shard_map/ppermute | solution.py:67
  111.0 4.8 %collective-permute-start.25 = (bf16[2,256,896]{2,1,0:T(8,128)(2,1)S(1)}, bf16[2,256,896]{2,1,0:T(8,128)(2,1)S(1)}, u32[]{:S(2)}, u32[]{:S(2)}) collective-permute-start(bf16[2,256,896]{2,1,0:T(8,128)(2,1)S(1)} %collective-permute-done.14.p4), channel_id=1, source_target_pairs={{0,4},{4,0},{1,5},{5,1},{2,6},{6,2},{3,7},{7,3},{8,12},{12,8},{9,1... | collective-permute-start | bytes 2752520 | tf_op jit(solution)/shard_map/ppermute | solution.py:67
  111.5 6.1 %collective-permute-start.24 = (bf16[2,256,896]{2,1,0:T(8,128)(2,1)S(1)}, bf16[2,256,896]{2,1,0:T(8,128)(2,1)S(1)}, u32[]{:S(2)}, u32[]{:S(2)}) collective-permute-start(bf16[2,256,896]{2,1,0:T(8,128)(2,1)S(1)} %collective-permute-done.15.p2), channel_id=1, source_target_pairs={{0,4},{4,0},{1,5},{5,1},{2,6},{6,2},{3,7},{7,3},{8,12},{12,8},{9,1... | collective-permute-start | bytes 2752520 | tf_op jit(solution)/shard_map/ppermute | solution.py:67
  111.5 22.8 %collective-permute-start.30 = (bf16[224,2048]{1,0:T(8,128)(2,1)S(1)}, bf16[224,2048]{1,0:T(8,128)(2,1)S(1)}, u32[]{:S(2)}, u32[]{:S(2)}) collective-permute-start(bf16[224,2048]{1,0:T(8,128)(2,1)S(1)} %get-tuple-element.130), channel_id=1, source_target_pairs={{0,3},{1,0},{2,1},{3,2},{4,5},{5,6},{6,7},{7,4},{8,11},{9,8},{10,9... | collective-permute-start | bytes 2752520 | tf_op jit(solution)/shard_map/ppermute | solution.py:63
  113.0 22.4 %collective-permute-start.31 = (bf16[224,2048]{1,0:T(8,128)(2,1)S(1)}, bf16[224,2048]{1,0:T(8,128)(2,1)S(1)}, u32[]{:S(2)}, u32[]{:S(2)}) collective-permute-start(bf16[224,2048]{1,0:T(8,128)(2,1)S(1)} %shard_map.101), channel_id=1, source_target_pairs={{0,1},{1,2},{2,3},{3,0},{4,7},{5,4},{6,5},{7,6},{8,9},{9,10},{10,1... | collective-permute-start | bytes 2752520 | tf_op jit(solution)/shard_map/ppermute | solution.py:63
  114.0 22.8 %collective-permute-start.27 = (bf16[2,512,128]{2,1,0:T(8,128)(2,1)S(1)}, bf16[2,512,128]{2,1,0:T(8,128)(2,1)S(1)}, u32[]{:S(2)}, u32[]{:S(2)}) collective-permute-start(bf16[2,512,128]{2,1,0:T(8,128)(2,1)S(1)} %get-tuple-element.122), channel_id=1, source_target_pairs={{0,8},{4,36},{8,16},{12,44},{16,24},{20,52},{24,0},{28,60},{32,40}... | collective-permute-start | bytes 786440 | tf_op jit(solution)/shard_map/ppermute | solution.py:54
  115.7 21.0 %collective-permute-start.28 = (bf16[2,512,128]{2,1,0:T(8,128)(2,1)S(1)}, bf16[2,512,128]{2,1,0:T(8,128)(2,1)S(1)}, u32[]{:S(2)}, u32[]{:S(2)}) collective-permute-start(bf16[2,512,128]{2,1,0:T(8,128)(2,1)S(1)} %get-tuple-element.123), channel_id=1, source_target_pairs={{0,24},{4,100},{8,0},{12,108},{16,8},{20,116},{24,16},{28,124},{32... | collective-permute-start | bytes 786440 | tf_op jit(solution)/shard_map/ppermute | solution.py:54
  117.6 19.2 %collective-permute-start.29 = (bf16[2,512,128]{2,1,0:T(8,128)(2,1)S(1)}, bf16[2,512,128]{2,1,0:T(8,128)(2,1)S(1)}, u32[]{:S(2)}, u32[]{:S(2)}) collective-permute-start(bf16[2,512,128]{2,1,0:T(8,128)(2,1)S(1)} %get-tuple-element.124), channel_id=1, source_target_pairs={{0,16},{4,68},{8,24},{12,76},{16,0},{20,84},{24,8},{28,92},{32,48}... | collective-permute-start | bytes 786440 | tf_op jit(solution)/shard_map/ppermute | solution.py:54

commit v5 on v4

--- a/solution.py
+++ b/solution.py
@@ -556,12 +556,33 @@
     )(*parts)[0]
 
 
+def pair_body(first, second, out, sems):
+    copies = [
+        pltpu.make_async_copy(first, out.at[0], sems.at[0]),
+        pltpu.make_async_copy(second, out.at[1], sems.at[1]),
+    ]
+    start_all(copies)
+    wait_all(copies)
+
+
+def pair(first, second):
+    return call(
+        pair_body,
+        (shape((2,) + first.shape),),
+        (HB, HB),
+        [pltpu.SemaphoreType.DMA((2,))],
+        0,
+        8 * first.shape[0] * first.shape[1],
+        limit=16,
+    )(keep_out(first), keep_out(second))[0]
+
+
 def plane_gather(phase, array):
     return [array] + [plane_shift(k, array, phase) for k in (1, 2, 3)]
 
 
 def local(tokens, w_gate, w_up, w_down, d_out):
-    first = plane_gather(0, jnp.stack([tokens, d_out]))
+    first = plane_gather(0, pair(tokens, d_out))
     chunk_t, chunk_c = place(first)
     tok_chunks = plane_gather(1, chunk_t)
     cot_chunks = [chunk_c] + [

time: 138 us -> 138 us (level)
  no operation moved by 1% of the time
where the time goes in v5:
time: 138 us
  waiting for transfers between devices  63.6 us (46%)
  starting transfers between devices  39.5 us (29%)
  Pallas kernels  33.6 us (24%)
    ppermute x9, waiting for transfers between devices, depth_shift(): return lax.ppermute(array, ('col', 'depth'), pairs)  44.5 us
    ppermute x18, starting transfers between devices, plane_shift(): return lax.ppermute(array, ('row', 'col'), pairs)  26.4 us
    ppermute x18, waiting for transfers between devices, plane_shift(): return lax.ppermute(array, ('row', 'col'), pairs)  15.1 us
    ppermute x9, starting transfers between devices, depth_shift(): return lax.ppermute(array, ('col', 'depth'), pairs)  12.3 us
    pallas_call x1, Pallas kernels, gate_up(): call(gate_up_body, (shape((2, tok // 2, hid), F32), shape((2, tok // 2, h...  5.64 us
    pallas_call x1, Pallas kernels, weight_grads(): call(grads_body, (shape((feats, hid)),) * 2, (VM,) * 12, [pltpu.VMEM((fea...  5.48 us
    pallas_call x1, Pallas kernels, slot_weights(): call(weights_body, (shape(wg.shape), shape(wu.shape), shape(wd.shape)), (...  4.77 us
    pallas_call x1, Pallas kernels, d_tok_parts(): call(d_tok_body, (shape((G, tok, part)),) * G, (VM,) * 4, [pltpu.VMEM((2,...  4.53 us
  transfers between devices with their start and end apart: 32, of which 17 were waited for; matrix products, arithmetic and copies ran while one was open for 0% of the time, Pallas kernels for 20%

profile of v5, /device:TPU:0, one launch (start us, length us, event | category | flops | bytes accessed | tf_op | source)
XLA Modules:
  0.0 137.6 jit_solution(12790235666599821727)
XLA Ops:
  0.6 1.0 shard_map.92.p0
  1.6 1.6 %collective-permute-start = (bf16[2,512,128]{2,1,0:T(8,128)(2,1)S(1)}, bf16[2,512,128]{2,1,0:T(8,128)(2,1)S(1)}, u32[]{:S(2)}, u32[]{:S(2)}) collective-permute-start(bf16[2,512,128]{2,1,0:T(8,128)(2,1)S(1)} %shard_map.92.p0), channel_id=1, source_target_pairs={{0,8},{4,36},{8,16},{12,44},{16,24},{20,52},{24,0},{28,60},{32,40}... | collective-permute-start | bytes 786440 | tf_op jit(solution)/shard_map/ppermute | solution.py:54
  3.3 1.7 %collective-permute-start.1 = (bf16[2,512,128]{2,1,0:T(8,128)(2,1)S(1)}, bf16[2,512,128]{2,1,0:T(8,128)(2,1)S(1)}, u32[]{:S(2)}, u32[]{:S(2)}) collective-permute-start(bf16[2,512,128]{2,1,0:T(8,128)(2,1)S(1)} %shard_map.92.p0), channel_id=1, source_target_pairs={{0,24},{4,100},{8,0},{12,108},{16,8},{20,116},{24,16},{28,124},{32... | collective-permute-start | bytes 786440 | tf_op jit(solution)/shard_map/ppermute | solution.py:54
  4.9 1.9 %collective-permute-start.2 = (bf16[2,512,128]{2,1,0:T(8,128)(2,1)S(1)}, bf16[2,512,128]{2,1,0:T(8,128)(2,1)S(1)}, u32[]{:S(2)}, u32[]{:S(2)}) collective-permute-start(bf16[2,512,128]{2,1,0:T(8,128)(2,1)S(1)} %shard_map.92.p0), channel_id=1, source_target_pairs={{0,16},{4,68},{8,24},{12,76},{16,0},{20,84},{24,8},{28,92},{32,48}... | collective-permute-start | bytes 786440 | tf_op jit(solution)/shard_map/ppermute | solution.py:54
  6.8 2.4 %collective-permute-done.p1 = bf16[2,512,128]{2,1,0:T(8,128)(2,1)S(1)} collective-permute-done((bf16[2,512,128]{2,1,0:T(8,128)(2,1)S(1)}, bf16[2,512,128]{2,1,0:T(8,128)(2,1)S(1)}, u32[]{:S(2)}, u32[]{:S(2)}) %collective-permute-start) | collective-permute-done | bytes 262176 | tf_op jit(solution)/shard_map/ppermute | solution.py:54
  9.6 3.5 %collective-permute-done.2.p3 = bf16[2,512,128]{2,1,0:T(8,128)(2,1)S(1)} collective-permute-done((bf16[2,512,128]{2,1,0:T(8,128)(2,1)S(1)}, bf16[2,512,128]{2,1,0:T(8,128)(2,1)S(1)}, u32[]{:S(2)}, u32[]{:S(2)}) %collective-permute-start.2) | collective-permute-done | bytes 262176 | tf_op jit(solution)/shard_map/ppermute | solution.py:54
  13.3 1.6 %collective-permute-start.3 = (bf16[4,512,128]{2,1,0:T(8,128)(2,1)S(1)}, bf16[4,512,128]{2,1,0:T(8,128)(2,1)S(1)}, u32[]{:S(2)}, u32[]{:S(2)}) collective-permute-start(bf16[4,512,128]{2,1,0:T(8,128)(2,1)S(1)} %get-tuple-element.72.c0.t0), channel_id=1, source_target_pairs={{0,32},{4,12},{8,40},{12,20},{16,48},{20,28},{24,56},{28,4},{32,64... | collective-permute-start | bytes 1572872 | tf_op jit(solution)/shard_map/ppermute | solution.py:54
  14.9 1.7 %collective-permute-start.4 = (bf16[4,512,128]{2,1,0:T(8,128)(2,1)S(1)}, bf16[4,512,128]{2,1,0:T(8,128)(2,1)S(1)}, u32[]{:S(2)}, u32[]{:S(2)}) collective-permute-start(bf16[4,512,128]{2,1,0:T(8,128)(2,1)S(1)} %get-tuple-element.72.c0.t0), channel_id=1, source_target_pairs={{0,96},{4,28},{8,104},{12,4},{16,112},{20,12},{24,120},{28,20},{32... | collective-permute-start | bytes 1572872 | tf_op jit(solution)/shard_map/ppermute | solution.py:54
  16.6 2.0 %collective-permute-start.5 = (bf16[4,512,128]{2,1,0:T(8,128)(2,1)S(1)}, bf16[4,512,128]{2,1,0:T(8,128)(2,1)S(1)}, u32[]{:S(2)}, u32[]{:S(2)}) collective-permute-start(bf16[4,512,128]{2,1,0:T(8,128)(2,1)S(1)} %get-tuple-element.72.c0.t0), channel_id=1, source_target_pairs={{0,64},{4,20},{8,72},{12,28},{16,80},{20,4},{24,88},{28,12},{32,96... | collective-permute-start | bytes 1572872 | tf_op jit(solution)/shard_map/ppermute | solution.py:54
  18.6 4.8 %shard_map.94 = (bf16[2048,896]{1,0:T(8,128)(2,1)S(1)}, bf16[2048,896]{1,0:T(8,128)(2,1)S(1)}, bf16[896,2048]{1,0:T(8,128)(2,1)S(1)}) custom-call(bf16[2048,896]{1,0:T(8,128)(2,1)} %wg.1, bf16[2048,896]{1,0:T(8,128)(2,1)} %wu.1, bf16[896,2048]{1,0:T(8,128)(2,1)} %wd.1), custom_call_target="tpu_custom_call" | custom-call | bytes 440401 | tf_op jit(solution)/shard_map/pallas_call | solution.py:238
  24.1 6.5 %collective-permute-done.5.c3.t3 = bf16[4,512,128]{2,1,0:T(8,128)(2,1)S(1)} collective-permute-done((bf16[4,512,128]{2,1,0:T(8,128)(2,1)S(1)}, bf16[4,512,128]{2,1,0:T(8,128)(2,1)S(1)}, u32[]{:S(2)}, u32[]{:S(2)}) %collective-permute-start.5) | collective-permute-done | bytes 524320 | tf_op jit(solution)/shard_map/ppermute | solution.py:54
  30.9 2.0 %collective-permute-start.6 = (bf16[4,512,128]{2,1,0:T(8,128)(2,1)S(1)}, bf16[4,512,128]{2,1,0:T(8,128)(2,1)S(1)}, u32[]{:S(2)}, u32[]{:S(2)}) collective-permute-start(bf16[4,512,128]{2,1,0:T(8,128)(2,1)S(1)} %get-tuple-element.76), channel_id=1, source_target_pairs={{0,1},{1,2},{2,3},{3,0},{4,7},{5,4},{6,5},{7,6},{8,9},{9,10},{10,1... | collective-permute-start | bytes 1572872 | tf_op jit(solution)/shard_map/ppermute | solution.py:63
  32.9 3.6 %collective-permute-start.7 = (bf16[4,512,128]{2,1,0:T(8,128)(2,1)S(1)}, bf16[4,512,128]{2,1,0:T(8,128)(2,1)S(1)}, u32[]{:S(2)}, u32[]{:S(2)}) collective-permute-start(bf16[4,512,128]{2,1,0:T(8,128)(2,1)S(1)} %get-tuple-element.77), channel_id=1, source_target_pairs={{0,2},{1,3},{2,0},{3,1},{4,6},{5,7},{6,4},{7,5},{8,10},{9,11},{10,... | collective-permute-start | bytes 1572872 | tf_op jit(solution)/shard_map/ppermute | solution.py:63
  36.5 0.7 collective-permute-start.10
  37.2 2.1 %collective-permute-start.8 = (bf16[4,512,128]{2,1,0:T(8,128)(2,1)S(1)}, bf16[4,512,128]{2,1,0:T(8,128)(2,1)S(1)}, u32[]{:S(2)}, u32[]{:S(2)}) collective-permute-start(bf16[4,512,128]{2,1,0:T(8,128)(2,1)S(1)} %get-tuple-element.88.c0), channel_id=1, source_target_pairs={{0,32},{4,12},{8,40},{12,20},{16,48},{20,28},{24,56},{28,4},{32,64... | collective-permute-start | bytes 1572872 | tf_op jit(solution)/shard_map/ppermute | solution.py:54
  39.4 1.2 collective-permute-start.9
  40.6 5.6 %shard_map.96 = (f32[2,256,896]{2,1,0:T(8,128)S(1)}, bf16[2,256,896]{2,1,0:T(8,128)(2,1)S(1)}) custom-call(bf16[4,512,128]{2,1,0:T(8,128)(2,1)S(1)} %get-tuple-element.72.c0.t0, bf16[4,512,128]{2,1,0:T(8,128)(2,1)S(1)} %collective-permute-done.3.c1.t1, bf16[4,512,128]{2,1,0:T(8,128)(2,1)S(1)} %collective-permute-done.4.c2.t2, ...), custom_call_target="tpu_custom_call" | custom-call | flops 75161928 | bytes 146800 | tf_op jit(solution)/shard_map/pallas_call | solution.py:277
  46.3 8.6 %collective-permute-done.7.t3 = bf16[4,512,128]{2,1,0:T(8,128)(2,1)S(1)} collective-permute-done((bf16[4,512,128]{2,1,0:T(8,128)(2,1)S(1)}, bf16[4,512,128]{2,1,0:T(8,128)(2,1)S(1)}, u32[]{:S(2)}, u32[]{:S(2)}) %collective-permute-start.7) | collective-permute-done | bytes 524320 | tf_op jit(solution)/shard_map/ppermute | solution.py:63
  54.9 2.7 %shard_map.97 = (f32[256,896]{1,0:T(8,128)S(1)}, bf16[3,256,896]{2,1,0:T(8,128)(2,1)S(1)}) custom-call(bf16[4,512,128]{2,1,0:T(8,128)(2,1)S(1)} %get-tuple-element.88.c0, bf16[4,512,128]{2,1,0:T(8,128)(2,1)S(1)} %collective-permute-done.8.c1, bf16[4,512,128]{2,1,0:T(8,128)(2,1)S(1)} %collective-permute-done.9.c2, ...), custom_call_target="tpu_custom_call" | custom-call | flops 37580964 | bytes 73400 | tf_op jit(solution)/shard_map/pallas_call | solution.py:315
  57.7 3.1 %collective-permute-done.11.recv = bf16[3,256,896]{2,1,0:T(8,128)(2,1)S(1)} collective-permute-done((bf16[3,256,896]{2,1,0:T(8,128)(2,1)S(1)}, bf16[3,256,896]{2,1,0:T(8,128)(2,1)S(1)}, u32[]{:S(2)}, u32[]{:S(2)}) %collective-permute-start.11) | collective-permute-done | bytes 1376288 | tf_op jit(solution)/shard_map/ppermute | solution.py:67
  60.8 0.8 shard_map.98
  61.8 1.2 collective-permute-start.13
  63.0 0.9 collective-permute-start.15
  63.9 0.9 collective-permute-done.12.other
  64.8 2.4 %shard_map.99 = (bf16[4,512,128]{2,1,0:T(8,128)(2,1)S(1)}, bf16[4,512,128]{2,1,0:T(8,128)(2,1)S(1)}, bf16[4,512,128]{2,1,0:T(8,128)(2,1)S(1)}, bf16[4,512,128]{2,1,0:T(8,128)(2,1)S(1)}, bf16[2,256,896]{2,1,0:T(8,128)(2,1)S(1)}) custom-call(bf16[3,256,896]{2,1,0:T(8,128)(2,1)S(1)} %get-tuple-element.98.own, ...), custom_call_target="tpu_custom_call" | custom-call | flops 37580964 | bytes 73400 | tf_op jit(solution)/shard_map/pallas_call | solution.py:383
  67.2 1.5 %collective-permute-start.16 = (bf16[4,512,128]{2,1,0:T(8,128)(2,1)S(1)}, bf16[4,512,128]{2,1,0:T(8,128)(2,1)S(1)}, u32[]{:S(2)}, u32[]{:S(2)}) collective-permute-start(bf16[4,512,128]{2,1,0:T(8,128)(2,1)S(1)} %get-tuple-element.103), channel_id=1, source_target_pairs={{0,32},{4,12},{8,40},{12,20},{16,48},{20,28},{24,56},{28,4},{32,64... | collective-permute-start | bytes 1572872 | tf_op jit(solution)/shard_map/ppermute | solution.py:54
  68.7 1.8 %collective-permute-start.17 = (bf16[4,512,128]{2,1,0:T(8,128)(2,1)S(1)}, bf16[4,512,128]{2,1,0:T(8,128)(2,1)S(1)}, u32[]{:S(2)}, u32[]{:S(2)}) collective-permute-start(bf16[4,512,128]{2,1,0:T(8,128)(2,1)S(1)} %get-tuple-element.104), channel_id=1, source_target_pairs={{0,96},{4,28},{8,104},{12,4},{16,112},{20,12},{24,120},{28,20},{32... | collective-permute-start | bytes 1572872 | tf_op jit(solution)/shard_map/ppermute | solution.py:54
  70.8 5.7 %collective-permute-done.13.t2 = bf16[4,512,128]{2,1,0:T(8,128)(2,1)S(1)} collective-permute-done((bf16[4,512,128]{2,1,0:T(8,128)(2,1)S(1)}, bf16[4,512,128]{2,1,0:T(8,128)(2,1)S(1)}, u32[]{:S(2)}, u32[]{:S(2)}) %collective-permute-start.13) | collective-permute-done | bytes 524320 | tf_op jit(solution)/shard_map/ppermute | solution.py:63
  76.6 3.0 %shard_map.100 = (bf16[224,2048]{1,0:T(8,128)(2,1)S(1)}, bf16[224,2048]{1,0:T(8,128)(2,1)S(1)}, bf16[224,2048]{1,0:T(8,128)(2,1)S(1)}, bf16[224,2048]{1,0:T(8,128)(2,1)S(1)}) custom-call(bf16[3,256,896]{2,1,0:T(8,128)(2,1)S(1)} %get-tuple-element.98.own, bf16[3,256,896]{2,1,0:T(8,128)(2,1)S(1)} %collective-permute-done.12.other, ...), custom_call_target="tpu_custom_call" | custom-call | flops 37580964 | bytes 41943 | tf_op jit(solution)/shard_map/pallas_call | solution.py:449
  79.6 4.5 %shard_map.101 = (bf16[4,512,128]{2,1,0:T(8,128)(2,1)S(1)}, bf16[4,512,128]{2,1,0:T(8,128)(2,1)S(1)}, bf16[4,512,128]{2,1,0:T(8,128)(2,1)S(1)}, bf16[4,512,128]{2,1,0:T(8,128)(2,1)S(1)}) custom-call(bf16[3,256,896]{2,1,0:T(8,128)(2,1)S(1)} %get-tuple-element.98.own, bf16[3,256,896]{2,1,0:T(8,128)(2,1)S(1)} %collective-permute-done.12.other, ...), custom_call_target="tpu_custom_call" | custom-call | flops 75161928 | bytes 146800 | tf_op jit(solution)/shard_map/pallas_call | solution.py:415
  84.3 2.6 %collective-permute-start.23 = (bf16[2,256,896]{2,1,0:T(8,128)(2,1)S(1)}, bf16[2,256,896]{2,1,0:T(8,128)(2,1)S(1)}, u32[]{:S(2)}, u32[]{:S(2)}) collective-permute-start(bf16[2,256,896]{2,1,0:T(8,128)(2,1)S(1)} %collective-permute-done.15.p2), channel_id=1, source_target_pairs={{0,1},{1,2},{2,3},{3,0},{4,7},{5,4},{6,5},{7,6},{8,9},{9,10},{10,1... | collective-permute-start | bytes 2752520 | tf_op jit(solution)/shard_map/ppermute | solution.py:63
  87.1 3.0 %collective-permute-start.21 = (bf16[4,512,128]{2,1,0:T(8,128)(2,1)S(1)}, bf16[4,512,128]{2,1,0:T(8,128)(2,1)S(1)}, u32[]{:S(2)}, u32[]{:S(2)}) collective-permute-start(bf16[4,512,128]{2,1,0:T(8,128)(2,1)S(1)} %get-tuple-element.114), channel_id=1, source_target_pairs={{0,96},{4,28},{8,104},{12,4},{16,112},{20,12},{24,120},{28,20},{32... | collective-permute-start | bytes 1572872 | tf_op jit(solution)/shard_map/ppermute | solution.py:54
  90.1 1.2 collective-permute-done.14.p4
  91.3 0.7 collective-permute-start.22
  92.0 9.1 %collective-permute-done.19.refs_1_ = bf16[224,2048]{1,0:T(8,128)(2,1)S(1)} collective-permute-done((bf16[224,2048]{1,0:T(8,128)(2,1)S(1)}, bf16[224,2048]{1,0:T(8,128)(2,1)S(1)}, u32[]{:S(2)}, u32[]{:S(2)}) %collective-permute-start.19) | collective-permute-done | bytes 917536 | tf_op jit(solution)/shard_map/ppermute | solution.py:63
  101.4 1.0 collective-permute-done.21.b2
  102.9 8.1 %collective-permute-done.23.p6 = bf16[2,256,896]{2,1,0:T(8,128)(2,1)S(1)} collective-permute-done((bf16[2,256,896]{2,1,0:T(8,128)(2,1)S(1)}, bf16[2,256,896]{2,1,0:T(8,128)(2,1)S(1)}, u32[]{:S(2)}, u32[]{:S(2)}) %collective-permute-start.23) | collective-permute-done | bytes 917536 | tf_op jit(solution)/shard_map/ppermute | solution.py:63
  111.0 0.5 collective-permute-start.25
  111.5 1.6 %collective-permute-start.30 = (bf16[224,2048]{1,0:T(8,128)(2,1)S(1)}, bf16[224,2048]{1,0:T(8,128)(2,1)S(1)}, u32[]{:S(2)}, u32[]{:S(2)}) collective-permute-start(bf16[224,2048]{1,0:T(8,128)(2,1)S(1)} %get-tuple-element.130), channel_id=1, source_target_pairs={{0,3},{1,0},{2,1},{3,2},{4,5},{5,6},{6,7},{7,4},{8,11},{9,8},{10,9... | collective-permute-start | bytes 2752520 | tf_op jit(solution)/shard_map/ppermute | solution.py:63
  113.5 0.5 shard_map.103
  114.0 1.7 %collective-permute-start.27 = (bf16[2,512,128]{2,1,0:T(8,128)(2,1)S(1)}, bf16[2,512,128]{2,1,0:T(8,128)(2,1)S(1)}, u32[]{:S(2)}, u32[]{:S(2)}) collective-permute-start(bf16[2,512,128]{2,1,0:T(8,128)(2,1)S(1)} %get-tuple-element.122), channel_id=1, source_target_pairs={{0,8},{4,36},{8,16},{12,44},{16,24},{20,52},{24,0},{28,60},{32,40}... | collective-permute-start | bytes 786440 | tf_op jit(solution)/shard_map/ppermute | solution.py:54
  115.7 1.8 %collective-permute-start.28 = (bf16[2,512,128]{2,1,0:T(8,128)(2,1)S(1)}, bf16[2,512,128]{2,1,0:T(8,128)(2,1)S(1)}, u32[]{:S(2)}, u32[]{:S(2)}) collective-permute-start(bf16[2,512,128]{2,1,0:T(8,128)(2,1)S(1)} %get-tuple-element.123), channel_id=1, source_target_pairs={{0,24},{4,100},{8,0},{12,108},{16,8},{20,116},{24,16},{28,124},{32... | collective-permute-start | bytes 786440 | tf_op jit(solution)/shard_map/ppermute | solution.py:54
  117.5 0.7 collective-permute-start.29
  118.2 5.5 %shard_map.104 = (bf16[512,896]{1,0:T(8,128)(2,1)}, bf16[512,896]{1,0:T(8,128)(2,1)}) custom-call(bf16[4,512,128]{2,1,0:T(8,128)(2,1)S(1)} %get-tuple-element.71.t0, bf16[4,512,128]{2,1,0:T(8,128)(2,1)S(1)} %collective-permute-done.6.t1, bf16[4,512,128]{2,1,0:T(8,128)(2,1)S(1)} %collective-permute-done.13.t2, ...), custom_call_target="tpu_custom_call" | custom-call | flops 75161928 | bytes 91750 | tf_op jit(solution)/shard_map/pallas_call | solution.py:479
  123.7 10.5 %collective-permute-done.30.refs_1_ = bf16[224,2048]{1,0:T(8,128)(2,1)S(1)} collective-permute-done((bf16[224,2048]{1,0:T(8,128)(2,1)S(1)}, bf16[224,2048]{1,0:T(8,128)(2,1)S(1)}, u32[]{:S(2)}, u32[]{:S(2)}) %collective-permute-start.30) | collective-permute-done | bytes 917536 | tf_op jit(solution)/shard_map/ppermute | solution.py:63
  134.2 1.2 collective-permute-done.31.refs_2_
  135.4 1.3 shard_map.106
  136.8 0.8 shard_map.105
  (31 shorter events, 3.7 us)
Async XLA Ops:
  1.6 7.7 %collective-permute-start = (bf16[2,512,128]{2,1,0:T(8,128)(2,1)S(1)}, bf16[2,512,128]{2,1,0:T(8,128)(2,1)S(1)}, u32[]{:S(2)}, u32[]{:S(2)}) collective-permute-start(bf16[2,512,128]{2,1,0:T(8,128)(2,1)S(1)} %shard_map.92.p0), channel_id=1, source_target_pairs={{0,8},{4,36},{8,16},{12,44},{16,24},{20,52},{24,0},{28,60},{32,40}... | collective-permute-start | bytes 786440 | tf_op jit(solution)/shard_map/ppermute | solution.py:54
  3.3 6.4 %collective-permute-start.1 = (bf16[2,512,128]{2,1,0:T(8,128)(2,1)S(1)}, bf16[2,512,128]{2,1,0:T(8,128)(2,1)S(1)}, u32[]{:S(2)}, u32[]{:S(2)}) collective-permute-start(bf16[2,512,128]{2,1,0:T(8,128)(2,1)S(1)} %shard_map.92.p0), channel_id=1, source_target_pairs={{0,24},{4,100},{8,0},{12,108},{16,8},{20,116},{24,16},{28,124},{32... | collective-permute-start | bytes 786440 | tf_op jit(solution)/shard_map/ppermute | solution.py:54
  4.9 8.2 %collective-permute-start.2 = (bf16[2,512,128]{2,1,0:T(8,128)(2,1)S(1)}, bf16[2,512,128]{2,1,0:T(8,128)(2,1)S(1)}, u32[]{:S(2)}, u32[]{:S(2)}) collective-permute-start(bf16[2,512,128]{2,1,0:T(8,128)(2,1)S(1)} %shard_map.92.p0), channel_id=1, source_target_pairs={{0,16},{4,68},{8,24},{12,76},{16,0},{20,84},{24,8},{28,92},{32,48}... | collective-permute-start | bytes 786440 | tf_op jit(solution)/shard_map/ppermute | solution.py:54
  13.3 10.5 %collective-permute-start.3 = (bf16[4,512,128]{2,1,0:T(8,128)(2,1)S(1)}, bf16[4,512,128]{2,1,0:T(8,128)(2,1)S(1)}, u32[]{:S(2)}, u32[]{:S(2)}) collective-permute-start(bf16[4,512,128]{2,1,0:T(8,128)(2,1)S(1)} %get-tuple-element.72.c0.t0), channel_id=1, source_target_pairs={{0,32},{4,12},{8,40},{12,20},{16,48},{20,28},{24,56},{28,4},{32,64... | collective-permute-start | bytes 1572872 | tf_op jit(solution)/shard_map/ppermute | solution.py:54
  14.9 9.2 %collective-permute-start.4 = (bf16[4,512,128]{2,1,0:T(8,128)(2,1)S(1)}, bf16[4,512,128]{2,1,0:T(8,128)(2,1)S(1)}, u32[]{:S(2)}, u32[]{:S(2)}) collective-permute-start(bf16[4,512,128]{2,1,0:T(8,128)(2,1)S(1)} %get-tuple-element.72.c0.t0), channel_id=1, source_target_pairs={{0,96},{4,28},{8,104},{12,4},{16,112},{20,12},{24,120},{28,20},{32... | collective-permute-start | bytes 1572872 | tf_op jit(solution)/shard_map/ppermute | solution.py:54
  16.6 14.0 %collective-permute-start.5 = (bf16[4,512,128]{2,1,0:T(8,128)(2,1)S(1)}, bf16[4,512,128]{2,1,0:T(8,128)(2,1)S(1)}, u32[]{:S(2)}, u32[]{:S(2)}) collective-permute-start(bf16[4,512,128]{2,1,0:T(8,128)(2,1)S(1)} %get-tuple-element.72.c0.t0), channel_id=1, source_target_pairs={{0,64},{4,20},{8,72},{12,28},{16,80},{20,4},{24,88},{28,12},{32,96... | collective-permute-start | bytes 1572872 | tf_op jit(solution)/shard_map/ppermute | solution.py:54
  30.9 15.3 %collective-permute-start.6 = (bf16[4,512,128]{2,1,0:T(8,128)(2,1)S(1)}, bf16[4,512,128]{2,1,0:T(8,128)(2,1)S(1)}, u32[]{:S(2)}, u32[]{:S(2)}) collective-permute-start(bf16[4,512,128]{2,1,0:T(8,128)(2,1)S(1)} %get-tuple-element.76), channel_id=1, source_target_pairs={{0,1},{1,2},{2,3},{3,0},{4,7},{5,4},{6,5},{7,6},{8,9},{9,10},{10,1... | collective-permute-start | bytes 1572872 | tf_op jit(solution)/shard_map/ppermute | solution.py:63
  32.9 22.0 %collective-permute-start.7 = (bf16[4,512,128]{2,1,0:T(8,128)(2,1)S(1)}, bf16[4,512,128]{2,1,0:T(8,128)(2,1)S(1)}, u32[]{:S(2)}, u32[]{:S(2)}) collective-permute-start(bf16[4,512,128]{2,1,0:T(8,128)(2,1)S(1)} %get-tuple-element.77), channel_id=1, source_target_pairs={{0,2},{1,3},{2,0},{3,1},{4,6},{5,7},{6,4},{7,5},{8,10},{9,11},{10,... | collective-permute-start | bytes 1572872 | tf_op jit(solution)/shard_map/ppermute | solution.py:63
  36.5 18.4 %collective-permute-start.10 = (bf16[4,512,128]{2,1,0:T(8,128)(2,1)S(1)}, bf16[4,512,128]{2,1,0:T(8,128)(2,1)S(1)}, u32[]{:S(2)}, u32[]{:S(2)}) collective-permute-start(bf16[4,512,128]{2,1,0:T(8,128)(2,1)S(1)} %get-tuple-element.88.c0), channel_id=1, source_target_pairs={{0,64},{4,20},{8,72},{12,28},{16,80},{20,4},{24,88},{28,12},{32,96... | collective-permute-start | bytes 1572872 | tf_op jit(solution)/shard_map/ppermute | solution.py:54
  37.2 17.7 %collective-permute-start.8 = (bf16[4,512,128]{2,1,0:T(8,128)(2,1)S(1)}, bf16[4,512,128]{2,1,0:T(8,128)(2,1)S(1)}, u32[]{:S(2)}, u32[]{:S(2)}) collective-permute-start(bf16[4,512,128]{2,1,0:T(8,128)(2,1)S(1)} %get-tuple-element.88.c0), channel_id=1, source_target_pairs={{0,32},{4,12},{8,40},{12,20},{16,48},{20,28},{24,56},{28,4},{32,64... | collective-permute-start | bytes 1572872 | tf_op jit(solution)/shard_map/ppermute | solution.py:54
  39.4 15.5 %collective-permute-start.9 = (bf16[4,512,128]{2,1,0:T(8,128)(2,1)S(1)}, bf16[4,512,128]{2,1,0:T(8,128)(2,1)S(1)}, u32[]{:S(2)}, u32[]{:S(2)}) collective-permute-start(bf16[4,512,128]{2,1,0:T(8,128)(2,1)S(1)} %get-tuple-element.88.c0), channel_id=1, source_target_pairs={{0,96},{4,28},{8,104},{12,4},{16,112},{20,12},{24,120},{28,20},{32... | collective-permute-start | bytes 1572872 | tf_op jit(solution)/shard_map/ppermute | solution.py:54
  57.6 3.2 %collective-permute-start.11 = (bf16[3,256,896]{2,1,0:T(8,128)(2,1)S(1)}, bf16[3,256,896]{2,1,0:T(8,128)(2,1)S(1)}, u32[]{:S(2)}, u32[]{:S(2)}) collective-permute-start(bf16[3,256,896]{2,1,0:T(8,128)(2,1)S(1)} %get-tuple-element.85), channel_id=1, source_target_pairs={{0,4},{4,0},{1,5},{5,1},{2,6},{6,2},{3,7},{7,3},{8,12},{12,8},{9,1... | collective-permute-start | bytes 4128776 | tf_op jit(solution)/shard_map/ppermute | solution.py:67
  61.6 3.2 %collective-permute-start.12 = (bf16[3,256,896]{2,1,0:T(8,128)(2,1)S(1)}, bf16[3,256,896]{2,1,0:T(8,128)(2,1)S(1)}, u32[]{:S(2)}, u32[]{:S(2)}) collective-permute-start(bf16[3,256,896]{2,1,0:T(8,128)(2,1)S(1)} %get-tuple-element.98.own), channel_id=1, source_target_pairs={{0,4},{4,0},{1,5},{5,1},{2,6},{6,2},{3,7},{7,3},{8,12},{12,8},{9,1... | collective-permute-start | bytes 4128776 | tf_op jit(solution)/shard_map/ppermute | solution.py:67
  61.8 14.8 %collective-permute-start.13 = (bf16[4,512,128]{2,1,0:T(8,128)(2,1)S(1)}, bf16[4,512,128]{2,1,0:T(8,128)(2,1)S(1)}, u32[]{:S(2)}, u32[]{:S(2)}) collective-permute-start(bf16[4,512,128]{2,1,0:T(8,128)(2,1)S(1)} %get-tuple-element.92), channel_id=1, source_target_pairs={{0,3},{1,0},{2,1},{3,2},{4,5},{5,6},{6,7},{7,4},{8,11},{9,8},{10,9... | collective-permute-start | bytes 1572872 | tf_op jit(solution)/shard_map/ppermute | solution.py:63
  63.0 21.2 %collective-permute-start.15 = (bf16[2,256,896]{2,1,0:T(8,128)(2,1)S(1)}, bf16[2,256,896]{2,1,0:T(8,128)(2,1)S(1)}, u32[]{:S(2)}, u32[]{:S(2)}) collective-permute-start(bf16[2,256,896]{2,1,0:T(8,128)(2,1)S(1)} %get-tuple-element.96.p0), channel_id=1, source_target_pairs={{0,1},{1,2},{2,3},{3,0},{4,7},{5,4},{6,5},{7,6},{8,9},{9,10},{10,1... | collective-permute-start | bytes 2752520 | tf_op jit(solution)/shard_map/ppermute | solution.py:63
  67.2 17.0 %collective-permute-start.16 = (bf16[4,512,128]{2,1,0:T(8,128)(2,1)S(1)}, bf16[4,512,128]{2,1,0:T(8,128)(2,1)S(1)}, u32[]{:S(2)}, u32[]{:S(2)}) collective-permute-start(bf16[4,512,128]{2,1,0:T(8,128)(2,1)S(1)} %get-tuple-element.103), channel_id=1, source_target_pairs={{0,32},{4,12},{8,40},{12,20},{16,48},{20,28},{24,56},{28,4},{32,64... | collective-permute-start | bytes 1572872 | tf_op jit(solution)/shard_map/ppermute | solution.py:54
  68.7 15.5 %collective-permute-start.17 = (bf16[4,512,128]{2,1,0:T(8,128)(2,1)S(1)}, bf16[4,512,128]{2,1,0:T(8,128)(2,1)S(1)}, u32[]{:S(2)}, u32[]{:S(2)}) collective-permute-start(bf16[4,512,128]{2,1,0:T(8,128)(2,1)S(1)} %get-tuple-element.104), channel_id=1, source_target_pairs={{0,96},{4,28},{8,104},{12,4},{16,112},{20,12},{24,120},{28,20},{32... | collective-permute-start | bytes 1572872 | tf_op jit(solution)/shard_map/ppermute | solution.py:54
  70.5 13.7 %collective-permute-start.18 = (bf16[4,512,128]{2,1,0:T(8,128)(2,1)S(1)}, bf16[4,512,128]{2,1,0:T(8,128)(2,1)S(1)}, u32[]{:S(2)}, u32[]{:S(2)}) collective-permute-start(bf16[4,512,128]{2,1,0:T(8,128)(2,1)S(1)} %get-tuple-element.105), channel_id=1, source_target_pairs={{0,64},{4,20},{8,72},{12,28},{16,80},{20,4},{24,88},{28,12},{32,96... | collective-permute-start | bytes 1572872 | tf_op jit(solution)/shard_map/ppermute | solution.py:54
  76.6 14.7 %collective-permute-start.14 = (bf16[2,256,896]{2,1,0:T(8,128)(2,1)S(1)}, bf16[2,256,896]{2,1,0:T(8,128)(2,1)S(1)}, u32[]{:S(2)}, u32[]{:S(2)}) collective-permute-start(bf16[2,256,896]{2,1,0:T(8,128)(2,1)S(1)} %get-tuple-element.93.p1), channel_id=1, source_target_pairs={{0,1},{1,2},{2,3},{3,0},{4,7},{5,4},{6,5},{7,6},{8,9},{9,10},{10,1... | collective-permute-start | bytes 2752520 | tf_op jit(solution)/shard_map/ppermute | solution.py:63
  84.2 16.9 %collective-permute-start.19 = (bf16[224,2048]{1,0:T(8,128)(2,1)S(1)}, bf16[224,2048]{1,0:T(8,128)(2,1)S(1)}, u32[]{:S(2)}, u32[]{:S(2)}) collective-permute-start(bf16[224,2048]{1,0:T(8,128)(2,1)S(1)} %get-tuple-element.107), channel_id=1, source_target_pairs={{0,1},{1,2},{2,3},{3,0},{4,7},{5,4},{6,5},{7,6},{8,9},{9,10},{10,1... | collective-permute-start | bytes 2752520 | tf_op jit(solution)/shard_map/ppermute | solution.py:63
  84.3 26.7 %collective-permute-start.23 = (bf16[2,256,896]{2,1,0:T(8,128)(2,1)S(1)}, bf16[2,256,896]{2,1,0:T(8,128)(2,1)S(1)}, u32[]{:S(2)}, u32[]{:S(2)}) collective-permute-start(bf16[2,256,896]{2,1,0:T(8,128)(2,1)S(1)} %collective-permute-done.15.p2), channel_id=1, source_target_pairs={{0,1},{1,2},{2,3},{3,0},{4,7},{5,4},{6,5},{7,6},{8,9},{9,10},{10,1... | collective-permute-start | bytes 2752520 | tf_op jit(solution)/shard_map/ppermute | solution.py:63
  86.9 14.5 %collective-permute-start.20 = (bf16[4,512,128]{2,1,0:T(8,128)(2,1)S(1)}, bf16[4,512,128]{2,1,0:T(8,128)(2,1)S(1)}, u32[]{:S(2)}, u32[]{:S(2)}) collective-permute-start(bf16[4,512,128]{2,1,0:T(8,128)(2,1)S(1)} %get-tuple-element.113), channel_id=1, source_target_pairs={{0,32},{4,12},{8,40},{12,20},{16,48},{20,28},{24,56},{28,4},{32,64... | collective-permute-start | bytes 1572872 | tf_op jit(solution)/shard_map/ppermute | solution.py:54
  87.1 15.3 %collective-permute-start.21 = (bf16[4,512,128]{2,1,0:T(8,128)(2,1)S(1)}, bf16[4,512,128]{2,1,0:T(8,128)(2,1)S(1)}, u32[]{:S(2)}, u32[]{:S(2)}) collective-permute-start(bf16[4,512,128]{2,1,0:T(8,128)(2,1)S(1)} %get-tuple-element.114), channel_id=1, source_target_pairs={{0,96},{4,28},{8,104},{12,4},{16,112},{20,12},{24,120},{28,20},{32... | collective-permute-start | bytes 1572872 | tf_op jit(solution)/shard_map/ppermute | solution.py:54
  91.3 11.6 %collective-permute-start.22 = (bf16[4,512,128]{2,1,0:T(8,128)(2,1)S(1)}, bf16[4,512,128]{2,1,0:T(8,128)(2,1)S(1)}, u32[]{:S(2)}, u32[]{:S(2)}) collective-permute-start(bf16[4,512,128]{2,1,0:T(8,128)(2,1)S(1)} %get-tuple-element.115), channel_id=1, source_target_pairs={{0,64},{4,20},{8,72},{12,28},{16,80},{20,4},{24,88},{28,12},{32,96... | collective-permute-start | bytes 1572872 | tf_op jit(solution)/shard_map/ppermute | solution.py:54
  111.0 3.1 %collective-permute-start.26 = (bf16[2,256,896]{2,1,0:T(8,128)(2,1)S(1)}, bf16[2,256,896]{2,1,0:T(8,128)(2,1)S(1)}, u32[]{:S(2)}, u32[]{:S(2)}) collective-permute-start(bf16[2,256,896]{2,1,0:T(8,128)(2,1)S(1)} %collective-permute-done.23.p6), channel_id=1, source_target_pairs={{0,4},{4,0},{1,5},{5,1},{2,6},{6,2},{3,7},{7,3},{8,12},{12,8},{9,1... | collective-permute-start | bytes 2752520 | tf_op jit(solution)/shard_map/ppermute | solution.py:67
  111.0 4.8 %collective-permute-start.25 = (bf16[2,256,896]{2,1,0:T(8,128)(2,1)S(1)}, bf16[2,256,896]{2,1,0:T(8,128)(2,1)S(1)}, u32[]{:S(2)}, u32[]{:S(2)}) collective-permute-start(bf16[2,256,896]{2,1,0:T(8,128)(2,1)S(1)} %collective-permute-done.14.p4), channel_id=1, source_target_pairs={{0,4},{4,0},{1,5},{5,1},{2,6},{6,2},{3,7},{7,3},{8,12},{12,8},{9,1... | collective-permute-start | bytes 2752520 | tf_op jit(solution)/shard_map/ppermute | solution.py:67
  111.5 6.1 %collective-permute-start.24 = (bf16[2,256,896]{2,1,0:T(8,128)(2,1)S(1)}, bf16[2,256,896]{2,1,0:T(8,128)(2,1)S(1)}, u32[]{:S(2)}, u32[]{:S(2)}) collective-permute-start(bf16[2,256,896]{2,1,0:T(8,128)(2,1)S(1)} %collective-permute-done.15.p2), channel_id=1, source_target_pairs={{0,4},{4,0},{1,5},{5,1},{2,6},{6,2},{3,7},{7,3},{8,12},{12,8},{9,1... | collective-permute-start | bytes 2752520 | tf_op jit(solution)/shard_map/ppermute | solution.py:67
  111.5 22.8 %collective-permute-start.30 = (bf16[224,2048]{1,0:T(8,128)(2,1)S(1)}, bf16[224,2048]{1,0:T(8,128)(2,1)S(1)}, u32[]{:S(2)}, u32[]{:S(2)}) collective-permute-start(bf16[224,2048]{1,0:T(8,128)(2,1)S(1)} %get-tuple-element.130), channel_id=1, source_target_pairs={{0,3},{1,0},{2,1},{3,2},{4,5},{5,6},{6,7},{7,4},{8,11},{9,8},{10,9... | collective-permute-start | bytes 2752520 | tf_op jit(solution)/shard_map/ppermute | solution.py:63
  113.0 22.4 %collective-permute-start.31 = (bf16[224,2048]{1,0:T(8,128)(2,1)S(1)}, bf16[224,2048]{1,0:T(8,128)(2,1)S(1)}, u32[]{:S(2)}, u32[]{:S(2)}) collective-permute-start(bf16[224,2048]{1,0:T(8,128)(2,1)S(1)} %shard_map.102), channel_id=1, source_target_pairs={{0,1},{1,2},{2,3},{3,0},{4,7},{5,4},{6,5},{7,6},{8,9},{9,10},{10,1... | collective-permute-start | bytes 2752520 | tf_op jit(solution)/shard_map/ppermute | solution.py:63
  114.0 22.8 %collective-permute-start.27 = (bf16[2,512,128]{2,1,0:T(8,128)(2,1)S(1)}, bf16[2,512,128]{2,1,0:T(8,128)(2,1)S(1)}, u32[]{:S(2)}, u32[]{:S(2)}) collective-permute-start(bf16[2,512,128]{2,1,0:T(8,128)(2,1)S(1)} %get-tuple-element.122), channel_id=1, source_target_pairs={{0,8},{4,36},{8,16},{12,44},{16,24},{20,52},{24,0},{28,60},{32,40}... | collective-permute-start | bytes 786440 | tf_op jit(solution)/shard_map/ppermute | solution.py:54
  115.7 21.0 %collective-permute-start.28 = (bf16[2,512,128]{2,1,0:T(8,128)(2,1)S(1)}, bf16[2,512,128]{2,1,0:T(8,128)(2,1)S(1)}, u32[]{:S(2)}, u32[]{:S(2)}) collective-permute-start(bf16[2,512,128]{2,1,0:T(8,128)(2,1)S(1)} %get-tuple-element.123), channel_id=1, source_target_pairs={{0,24},{4,100},{8,0},{12,108},{16,8},{20,116},{24,16},{28,124},{32... | collective-permute-start | bytes 786440 | tf_op jit(solution)/shard_map/ppermute | solution.py:54
  117.5 19.2 %collective-permute-start.29 = (bf16[2,512,128]{2,1,0:T(8,128)(2,1)S(1)}, bf16[2,512,128]{2,1,0:T(8,128)(2,1)S(1)}, u32[]{:S(2)}, u32[]{:S(2)}) collective-permute-start(bf16[2,512,128]{2,1,0:T(8,128)(2,1)S(1)} %get-tuple-element.124), channel_id=1, source_target_pairs={{0,16},{4,68},{8,24},{12,76},{16,0},{20,84},{24,8},{28,92},{32,48}... | collective-permute-start | bytes 786440 | tf_op jit(solution)/shard_map/ppermute | solution.py:54
